TPU v7x, 32 devices: a whole 2x2x4 slice. The times are simulated.
32 devices in a mesh: dp: 4 (over y, core), ctx: 8 (over z, x).
Axes of the slice: x: 2, y: 2, z: 4, core: 2. Of those that a mesh axis runs over, the one named last changes fastest.
Arguments:
- tokens: bfloat16 [4096, 768], P(('dp', 'ctx')), may hold values from -6 to 6
- w_qkv: bfloat16 [768, 2304], P('dp'), may hold values from -0.21875 to 0.21875
- w_attn_out: bfloat16 [768, 768], P('dp'), may hold values from -6 to 6
- w_in: bfloat16 [768, 2304], P('dp'), may hold values from -0.21875 to 0.21875
- w_down: bfloat16 [1152, 768], P('dp'), may hold values from -0.1875 to 0.1875
- gain_attn: bfloat16 [768], P('dp'), may hold values from 0.25 to 1.75
- gain_mlp: bfloat16 [768], P('dp'), may hold values from 0.25 to 1.75
- cotangent: bfloat16 [4096, 768], P(('dp', 'ctx')), may hold values from -6 to 6
Outputs:
- layer_out: bfloat16 [4096, 768], P(('dp', 'ctx'))
- tokens_grad: float32 [4096, 768], P(('dp', 'ctx'))
- w_qkv_grad: float32 [768, 2304], P('dp')
- w_attn_out_grad: float32 [768, 768], P('dp')
- w_in_grad: float32 [768, 2304], P('dp')
- w_down_grad: float32 [1152, 768], P('dp')
- gain_attn_grad: float32 [768], P('dp')
- gain_mlp_grad: float32 [768], P('dp')
All inputs are finite; a program needn't handle non-finite values.
Results may differ from a plain program's by a relative error of at most 0.02.
Values may be sent and summed in bfloat16 or wider, within the bound.
No kernel may reach another device: no remote copies, remote signals or barrier semaphores. Data moves between devices by JAX's collectives and lax.ppermute only.
A program may use at most 192 MiB of HBM per device.

v0:
```python
import math

import jax
import jax.numpy as jnp
from jax import lax
from jax.sharding import PartitionSpec as P

HEADS = 12
HEAD_DIM = 64


theta_base = 160000.0
norm_eps = 1e-05


def layer_norm(values, gain):
    center = values - jnp.mean(values, axis=-1, keepdims=True)
    spread = jnp.mean(center * center, axis=-1, keepdims=True)
    return center * lax.rsqrt(spread + norm_eps) * gain


def rope_tables(positions, head_size):
    half_size = head_size // 2
    frequencies = jnp.exp(
        jnp.arange(half_size, dtype=jnp.float32) * (-2.0 * math.log(theta_base) / head_size)
    )
    angles = positions[:, None] * frequencies[None, :]
    return (jnp.cos(angles), jnp.sin(angles))


def rotate(values, cosine_table, sine_table):
    half_size = values.shape[-1] // 2
    first_half = values[..., :half_size]
    second_half = values[..., half_size:]
    cos_part = cosine_table[:, None, :]
    sin_part = sine_table[:, None, :]
    return jnp.concatenate(
        [
            first_half * cos_part - second_half * sin_part,
            second_half * cos_part + first_half * sin_part,
        ],
        axis=-1,
    )


def geglu(gate_input, gate_half):
    return jax.nn.gelu(gate_input, approximate=False) * gate_half


def online_update(state, query_cols, key_block, value_block, score_scale):
    run_max, run_total, run_acc = state
    scores = (
        jnp.einsum("hdq,hdk->hqk", query_cols, key_block, preferred_element_type=jnp.float32)
        * score_scale
    )
    new_max = jnp.maximum(run_max, jnp.max(scores, axis=-1))
    factor = jnp.exp(run_max - new_max)
    weights = jnp.exp(scores - new_max[:, :, None])
    new_total = run_total * factor + jnp.sum(weights, axis=-1)
    added = jnp.einsum(
        "hqk,hdk->hdq",
        weights.astype(jnp.bfloat16),
        value_block,
        preferred_element_type=jnp.float32,
    )
    new_acc = run_acc * factor[:, None, :] + added
    return (new_max, new_total, new_acc)


def attention_grads(
    query_cols, grad_cols, lse_block, delta_block, key_block, value_block, score_scale
):
    scores = (
        jnp.einsum("hdq,hdk->hqk", query_cols, key_block, preferred_element_type=jnp.float32)
        * score_scale
    )
    probs = jnp.exp(scores - lse_block[:, :, None])
    grad_probs = jnp.einsum(
        "hdq,hdk->hqk", grad_cols, value_block, preferred_element_type=jnp.float32
    )
    grad_scores = (probs * (grad_probs - delta_block[:, :, None])).astype(jnp.bfloat16)
    query_part = (
        jnp.einsum("hqk,hdk->hdq", grad_scores, key_block, preferred_element_type=jnp.float32)
        * score_scale
    )
    key_part = (
        jnp.einsum("hqk,hdq->hdk", grad_scores, query_cols, preferred_element_type=jnp.float32)
        * score_scale
    )
    value_part = jnp.einsum(
        "hqk,hdq->hdk", probs.astype(jnp.bfloat16), grad_cols, preferred_element_type=jnp.float32
    )
    return (query_part, key_part, value_part)


def on_device(tokens, w_qkv, w_attn_out, w_in, w_down, gain_attn, gain_mlp, cotangent):
    full_qkv, full_out, full_in, full_down, full_gain_attn, full_gain_mlp = (
        lax.all_gather(w_qkv, "dp", axis=0, tiled=True),
        lax.all_gather(w_attn_out, "dp", axis=0, tiled=True),
        lax.all_gather(w_in, "dp", axis=0, tiled=True),
        lax.all_gather(w_down, "dp", axis=0, tiled=True),
        lax.all_gather(gain_attn, "dp", axis=0, tiled=True),
        lax.all_gather(gain_mlp, "dp", axis=0, tiled=True),
    )
    tok_rows = tokens.shape[0]
    model_width = full_out.shape[0]
    hidden_units = full_down.shape[0]
    score_scale = HEAD_DIM ** (-0.5)
    positions = (lax.axis_index("ctx") * tok_rows + jnp.arange(tok_rows, dtype=jnp.int32)).astype(
        jnp.float32
    )
    cosine_table, sine_table = rope_tables(positions, HEAD_DIM)
    gain_one = full_gain_attn.astype(jnp.float32)
    gain_two = full_gain_mlp.astype(jnp.float32)
    inputs = tokens.astype(jnp.float32)
    normed = layer_norm(inputs, gain_one).astype(jnp.bfloat16)
    projected = jnp.dot(normed, full_qkv, preferred_element_type=jnp.float32)
    query_raw = projected[:, :model_width].reshape(tok_rows, HEADS, HEAD_DIM)
    key_raw = projected[:, model_width : 2 * model_width].reshape(tok_rows, HEADS, HEAD_DIM)
    value_raw = projected[:, 2 * model_width :]
    query_cols = jnp.transpose(
        rotate(query_raw, cosine_table, sine_table).astype(jnp.bfloat16), (1, 2, 0)
    )
    key_cols = jnp.transpose(
        rotate(key_raw, cosine_table, sine_table).astype(jnp.bfloat16), (1, 2, 0)
    ).reshape(model_width, tok_rows)
    value_cols = jnp.transpose(value_raw.astype(jnp.bfloat16))
    start_state = (
        jnp.full((HEADS, tok_rows), -1e30, jnp.float32),
        jnp.zeros((HEADS, tok_rows), jnp.float32),
        jnp.zeros((HEADS, HEAD_DIM, tok_rows), jnp.float32),
    )
    kept_keys, kept_values = (
        lax.all_gather(key_cols, "ctx", axis=1, tiled=True),
        lax.all_gather(value_cols, "ctx", axis=1, tiled=True),
    )
    piece_cols = kept_keys.shape[1]
    fold_block_cols = math.gcd(piece_cols, 512)

    def update_step(index, state):
        key_block = lax.dynamic_slice_in_dim(
            kept_keys, index * fold_block_cols, fold_block_cols, 1
        ).reshape(HEADS, HEAD_DIM, fold_block_cols)
        value_block = lax.dynamic_slice_in_dim(
            kept_values, index * fold_block_cols, fold_block_cols, 1
        ).reshape(HEADS, HEAD_DIM, fold_block_cols)
        return online_update(state, query_cols, key_block, value_block, score_scale)

    run_max, run_total, run_acc = lax.fori_loop(
        0, piece_cols // fold_block_cols, update_step, start_state
    )
    lse_rows = run_max + jnp.log(run_total)
    attn = run_acc / run_total[:, None, :]
    attn_low = jnp.transpose(attn, (2, 0, 1)).reshape(tok_rows, model_width).astype(jnp.bfloat16)
    branch = jnp.dot(attn_low, full_out, preferred_element_type=jnp.float32)
    middle = inputs + branch
    normed_two = layer_norm(middle, gain_two).astype(jnp.bfloat16)
    up_proj = jnp.dot(normed_two, full_in, preferred_element_type=jnp.float32)
    hidden = geglu(up_proj[:, :hidden_units], up_proj[:, hidden_units:]).astype(jnp.bfloat16)
    layer_out = (middle + jnp.dot(hidden, full_down, preferred_element_type=jnp.float32)).astype(
        jnp.bfloat16
    )
    grad_down = jnp.dot(hidden.T, cotangent, preferred_element_type=jnp.float32)
    grad_hidden = jnp.dot(cotangent, full_down.T, preferred_element_type=jnp.float32)
    unused_out, geglu_back = jax.vjp(geglu, up_proj[:, :hidden_units], up_proj[:, hidden_units:])
    grad_gate_input, grad_gate_half = geglu_back(grad_hidden)
    grad_up = jnp.concatenate([grad_gate_input, grad_gate_half], axis=-1).astype(jnp.bfloat16)
    grad_in = jnp.dot(normed_two.T, grad_up, preferred_element_type=jnp.float32)
    grad_normed_two = jnp.dot(grad_up, full_in.T, preferred_element_type=jnp.float32)
    unused_two, norm_back_two = jax.vjp(layer_norm, middle, gain_two)
    grad_middle_part, grad_gain_two = norm_back_two(grad_normed_two)
    grad_middle = cotangent.astype(jnp.float32) + grad_middle_part
    grad_branch = grad_middle.astype(jnp.bfloat16)
    grad_out = jnp.dot(attn_low.T, grad_branch, preferred_element_type=jnp.float32)
    grad_attn = jnp.dot(grad_branch, full_out.T, preferred_element_type=jnp.float32).astype(
        jnp.bfloat16
    )
    grad_cols = jnp.transpose(grad_attn).reshape(HEADS, HEAD_DIM, tok_rows)
    row_delta = jnp.sum(grad_cols.astype(jnp.float32) * attn, axis=1)
    zero_heads = jnp.zeros((HEADS, HEAD_DIM, tok_rows), jnp.float32)
    all_keys, all_values = (kept_keys, kept_values)
    seq_cols = all_keys.shape[1]
    block_cols = math.gcd(seq_cols, 512)
    zero_seq = jnp.zeros((model_width, seq_cols), jnp.float32)

    def key_step(index, carry):
        query_sum, key_buffer, value_buffer = carry
        begin = index * block_cols
        key_block = lax.dynamic_slice_in_dim(all_keys, begin, block_cols, 1).reshape(
            HEADS, HEAD_DIM, block_cols
        )
        value_block = lax.dynamic_slice_in_dim(all_values, begin, block_cols, 1).reshape(
            HEADS, HEAD_DIM, block_cols
        )
        query_part, key_part, value_part = attention_grads(
            query_cols, grad_cols, lse_rows, row_delta, key_block, value_block, score_scale
        )
        key_buffer = lax.dynamic_update_slice_in_dim(
            key_buffer, key_part.reshape(model_width, block_cols), begin, 1
        )
        value_buffer = lax.dynamic_update_slice_in_dim(
            value_buffer, value_part.reshape(model_width, block_cols), begin, 1
        )
        return (query_sum + query_part, key_buffer, value_buffer)

    grad_queries, key_terms, value_terms = lax.fori_loop(
        0, seq_cols // block_cols, key_step, (zero_heads, zero_seq, zero_seq)
    )
    grad_key_cols, grad_value_cols = (
        lax.psum_scatter(key_terms, "ctx", scatter_dimension=1, tiled=True),
        lax.psum_scatter(value_terms, "ctx", scatter_dimension=1, tiled=True),
    )
    grad_keys = grad_key_cols.reshape(HEADS, HEAD_DIM, tok_rows)
    grad_values = jnp.transpose(grad_value_cols)

    def rotate_local(values):
        return rotate(values, cosine_table, sine_table)

    unused_rot, rope_back = jax.vjp(rotate_local, query_raw)
    grad_query_raw = rope_back(jnp.transpose(grad_queries, (2, 0, 1)))[0].reshape(
        tok_rows, model_width
    )
    grad_key_raw = rope_back(jnp.transpose(grad_keys, (2, 0, 1)))[0].reshape(tok_rows, model_width)
    grad_projected = jnp.concatenate([grad_query_raw, grad_key_raw, grad_values], axis=-1).astype(
        jnp.bfloat16
    )
    grad_qkv = jnp.dot(normed.T, grad_projected, preferred_element_type=jnp.float32)
    grad_normed = jnp.dot(grad_projected, full_qkv.T, preferred_element_type=jnp.float32)
    unused_one, norm_back_one = jax.vjp(layer_norm, inputs, gain_one)
    grad_inputs, grad_gain_one = norm_back_one(grad_normed)
    tokens_grad = grad_middle + grad_inputs
    owned = (
        lax.psum_scatter(
            grad_qkv.astype(jnp.bfloat16), "dp", scatter_dimension=0, tiled=True
        ).astype(jnp.float32),
        lax.psum_scatter(
            grad_out.astype(jnp.bfloat16), "dp", scatter_dimension=0, tiled=True
        ).astype(jnp.float32),
        lax.psum_scatter(
            grad_in.astype(jnp.bfloat16), "dp", scatter_dimension=0, tiled=True
        ).astype(jnp.float32),
        lax.psum_scatter(
            grad_down.astype(jnp.bfloat16), "dp", scatter_dimension=0, tiled=True
        ).astype(jnp.float32),
        lax.psum_scatter(
            grad_gain_one.astype(jnp.bfloat16), "dp", scatter_dimension=0, tiled=True
        ).astype(jnp.float32),
        lax.psum_scatter(
            grad_gain_two.astype(jnp.bfloat16), "dp", scatter_dimension=0, tiled=True
        ).astype(jnp.float32),
    )
    summed = lax.psum((owned[0], owned[1], owned[2], owned[3], owned[4], owned[5]), "ctx")
    return (
        layer_out,
        tokens_grad,
        summed[0],
        summed[1],
        summed[2],
        summed[3],
        summed[4],
        summed[5],
    )


def solution(mesh):
    return jax.shard_map(
        on_device,
        mesh=mesh,
        in_specs=(
            P(("dp", "ctx"), None),
            P("dp", None),
            P("dp", None),
            P("dp", None),
            P("dp", None),
            P("dp"),
            P("dp"),
            P(("dp", "ctx"), None),
        ),
        out_specs=(
            P(("dp", "ctx"), None),
            P(("dp", "ctx"), None),
            P("dp", None),
            P("dp", None),
            P("dp", None),
            P("dp", None),
            P("dp"),
            P("dp"),
        ),
        check_vma=False,
    )
```

profile of v0, /device:TPU:0, one launch (start us, length us, event | category | flops | bytes accessed | tf_op | source)
XLA Modules:
  0.0 758.9 jit_solution(2677851721552142181)
XLA Ops:
  8.0 1.3 fusion.57
  11.6 8.3 %all-reduce.10 = (bf16[768]{0:T(1024)(128)(2,1)S(1)}, bf16[768]{0:T(1024)(128)(2,1)S(1)}) all-reduce(bf16[768]{0:T(1024)(128)(2,1)S(1)} %dynamic-update-slice, bf16[768]{0:T(1024)(128)(2,1)S(1)} %dynamic-update-slice.1), channel_id=1, replica_groups=mesh['dp'=4,'ctx'=8] {'dp'}, use_global_device_ids=true, to_apply=%add.4 | all-reduce | flops 1536 | bytes 6144
  21.1 1.1 fusion.36
  22.2 20.8 %all-gather.7.cloned.1.call-done = bf16[768,2304]{1,0:T(8,128)(2,1)} async-done(((bf16[192,2304]{1,0:T(8,128)(2,1)}), bf16[768,2304]{1,0:T(8,128)(2,1)}) %all-gather.7.cloned.1.call-update) | async-done | bytes 3538960 | tf_op jit(solution)/shard_map/all_gather | solution.py:98
  43.1 2.8 fusion.50
  50.7 40.2 %all-gather.11.cloned.1.call-done = bf16[768,1024]{0,1:T(8,128)(2,1)} async-done(((bf16[768,128]{0,1:T(8,128)(2,1)}), bf16[768,1024]{0,1:T(8,128)(2,1)}) %all-gather.11.cloned.1.call-update) | async-done | bytes 1572880 | tf_op jit(solution)/shard_map/all_gather | solution.py:135
  91.0 2.6 copy.34
  93.5 44.2 %all-gather.9.cloned.1.call-done = bf16[768,1024]{1,0:T(8,128)(2,1)} async-done(((bf16[768,128]{1,0:T(8,128)(2,1)}), bf16[768,1024]{1,0:T(8,128)(2,1)}) %all-gather.9.cloned.1.call-update) | async-done | bytes 1572880 | tf_op jit(solution)/shard_map/all_gather | solution.py:134
  137.7 11.8 %while.36 = (s32[]{:T(128)}, f32[12,128]{1,0:T(8,128)S(1)}, f32[12,128]{1,0:T(8,128)}, f32[12,64,128]{2,1,0:T(8,128)}, bf16[768,1024]{1,0:T(8,128)(2,1)}, /*inde...) while((s32[]{:T(128)}, f32[12,128]{1,0:T(8,128)S(1)}, ...), condition=%wide.region_5.0_spmd.clone, body=%wide.region_2.0_spmd.clone.sunk | while | flops 207920640 | bytes 21578048 | solution.py:149
  137.7 2.4 constant_dynamic-slice_fusion.7
  143.6 2.4 constant_dynamic-slice_fusion.7
  150.6 4.2 all-gather.13.cloned.1.call-done
  154.8 1.7 fusion.58
  156.8 30.2 %all-gather.15.cloned.1.call-done = bf16[768,2304]{1,0:T(8,128)(2,1)} async-done(((bf16[192,2304]{1,0:T(8,128)(2,1)}), bf16[768,2304]{1,0:T(8,128)(2,1)}) %all-gather.15.cloned.1.call-update) | async-done | bytes 3538960 | tf_op jit(solution)/shard_map/all_gather | solution.py:100
  187.0 2.7 fusion.53
  189.7 19.5 %all-gather.17.cloned.1.call-done = bf16[1152,768]{1,0:T(8,128)(2,1)} async-done(((bf16[288,768]{1,0:T(8,128)(2,1)}), bf16[1152,768]{1,0:T(8,128)(2,1)}) %all-gather.17.cloned.1.call-update) | async-done | bytes 1769488 | tf_op jit(solution)/shard_map/all_gather | solution.py:101
  209.3 3.3 add_convert_fusion
  214.2 1.9 multiply_reduce_fusion
  218.8 2.1 broadcast_in_dim.30
  220.9 2.1 broadcast_in_dim.30.clone
  223.0 29.3 %while.37 = (s32[]{:T(128)}, f32[12,64,128]{2,1,0:T(8,128)}, f32[768,1024]{1,0:T(8,128)}, f32[768,1024]{1,0:T(8,128)}, bf16[768,1024]{1,0:T(8,128)(2,1)}, /*inde...) while((s32[]{:T(128)}, f32[12,64,128]{2,1,0:T(8,128)}, ...), condition=%wide.region_12.0_spmd.clone, body=%wide.region_11.0_spmd.clone.sunk | while | flops 510296064 | bytes 90458496 | solution.py:206
  223.0 1.2 constant_dynamic-slice_fusion.8
  224.9 1.2 constant_dynamic-slice_fusion.9
  226.1 2.2 multiply_convert_fusion.7
  228.3 2.8 fusion.126
  233.5 1.1 copy-done.10
  235.0 1.7 copy-done.11
  237.7 1.2 constant_dynamic-slice_fusion.8
  239.5 1.2 constant_dynamic-slice_fusion.9
  240.7 2.2 multiply_convert_fusion.7
  242.9 2.9 fusion.126
  248.1 1.1 copy-done.10
  249.7 1.7 copy-done.11
  253.4 1.5 convolution_convert_fusion.3
  255.0 1.9 convolution_convert_fusion.2
  257.2 3.0 convolution_convert_fusion
  260.3 67.4 %reduce-scatter.7.cloned.1.call-done = f32[768,128]{1,0:T(8,128)} async-done(((f32[768,1024]{1,0:T(8,128)}), f32[768,128]{1,0:T(8,128)}) %reduce-scatter.7.cloned.1.call-update) | async-done | bytes 393232 | tf_op jit(solution)/shard_map/reduce_scatter | solution.py:210
  327.7 1.1 multiply_add_fusion.3
  328.9 76.6 %reduce-scatter.9.cloned.1.call-done = f32[768,128]{1,0:T(8,128)} async-done(((f32[768,1024]{1,0:T(8,128)}), f32[768,128]{1,0:T(8,128)}) %reduce-scatter.9.cloned.1.call-update) | async-done | bytes 393232 | tf_op jit(solution)/shard_map/reduce_scatter | solution.py:211
  406.6 3.1 convolution_convert_fusion.1
  411.2 1.1 fusion.19
  412.3 21.4 %reduce-scatter.13.cloned.1.call-done = bf16[192,768]{1,0:T(8,128)(2,1)} async-done(((bf16[768,768]{1,0:T(8,128)(2,1)}), bf16[192,768]{1,0:T(8,128)(2,1)}) %reduce-scatter.13.cloned.1.call-update) | async-done | bytes 294928 | tf_op jit(solution)/shard_map/reduce_scatter | solution.py:236
  433.7 32.6 %reduce-scatter.17.cloned.1.call-done = bf16[288,768]{1,0:T(8,128)(2,1)} async-done(((bf16[1152,768]{1,0:T(8,128)(2,1)}), bf16[288,768]{1,0:T(8,128)(2,1)}) %reduce-scatter.17.cloned.1.call-update) | async-done | bytes 442384 | tf_op jit(solution)/shard_map/reduce_scatter | solution.py:242
  466.3 3.6 fusion.37
  470.2 5.8 all-reduce.9
  477.1 32.2 %reduce-scatter.15.cloned.1.call-done = bf16[192,2304]{1,0:T(8,128)(2,1)} async-done(((bf16[768,2304]{1,0:T(8,128)(2,1)}), bf16[192,2304]{1,0:T(8,128)(2,1)}) %reduce-scatter.15.cloned.1.call-update) | async-done | bytes 884752 | tf_op jit(solution)/shard_map/reduce_scatter | solution.py:239
  509.3 43.1 %reduce-scatter.11.cloned.1.call-done = bf16[192,2304]{1,0:T(8,128)(2,1)} async-done(((bf16[768,2304]{1,0:T(8,128)(2,1)}), bf16[192,2304]{1,0:T(8,128)(2,1)}) %reduce-scatter.11.cloned.1.call-update) | async-done | bytes 884752 | tf_op jit(solution)/shard_map/reduce_scatter | solution.py:233
  552.4 199.6 %all-reduce.12 = (f32[192,2304]{1,0:T(8,128)}, f32[192,768]{1,0:T(8,128)}, f32[192,2304]{1,0:T(8,128)}, f32[288,768]{1,0:T(8,128)}, f32[192]{0:T(256)}, /*index=5*/f32[192]{0:T(256)}) all-reduce(bf16[192,2304]{1,0:T(8,128)(2,1)} %reduce-scatter.11.cloned.1.call-done, ...), channel_id=1, replica_groups=mesh['dp'=4,'ctx'=8] {'ctx'}, use_global_device_ids=true, to_apply=%region_18.0 | all-reduce | flops 1253760 | bytes 7523328 | tf_op jit(solution)/shard_map/psum | solution.py:252
  (224 shorter events, 33.7 us)
Async XLA Ops:
  7.2 35.9 %all-gather.7.cloned.1.call-start = ((), (), s32[]{:S(2)}) async-start(), calls=%async_computation.6 | async-start | bytes 4423680 | tf_op jit(solution)/shard_map/all_gather | solution.py:98
  7.9 83.1 %all-gather.11.cloned.1.call-start = ((), (), s32[]{:S(2)}) async-start(), calls=%async_computation.8 | async-start | bytes 1769472 | tf_op jit(solution)/shard_map/all_gather | solution.py:135
  20.0 25.9 %copy-start.38 = (f32[768]{0:T(1024)}, f32[768]{0:T(1024)S(1)}, u32[]{:S(2)}) copy-start(f32[768]{0:T(1024)S(1)} %convert_element_type.115) | copy-start | bytes 9220
  21.0 24.8 %copy-start.46 = (f32[128]{0:T(128)}, f32[128]{0:T(128)S(1)}, u32[]{:S(2)}) copy-start(f32[128]{0:T(128)S(1)} %broadcast_multiply_fusion.1) | copy-start | bytes 1540
  22.2 23.7 %copy-start.57 = (f32[128]{0:T(128)}, f32[128]{0:T(128)S(1)}, u32[]{:S(2)}) copy-start(f32[128]{0:T(128)S(1)} %fusion.36) | copy-start | bytes 1540
  22.2 23.7 %copy-start.48 = (f32[128]{0:T(128)}, f32[128]{0:T(128)S(1)}, u32[]{:S(2)}) copy-start(f32[128]{0:T(128)S(1)} %fusion.43) | copy-start | bytes 1540
  46.6 91.1 %all-gather.9.cloned.1.call-start = ((), (), s32[]{:S(2)}) async-start(), calls=%async_computation.7 | async-start | bytes 1769472 | tf_op jit(solution)/shard_map/all_gather | solution.py:134
  48.1 106.7 %all-gather.13.cloned.1.call-start = ((), (), s32[]{:S(2)}) async-start(), calls=%async_computation.9 | async-start | bytes 1474560 | tf_op jit(solution)/shard_map/all_gather | solution.py:99
  48.7 138.4 %all-gather.15.cloned.1.call-start = ((), (), s32[]{:S(2)}) async-start(), calls=%async_computation.10 | async-start | bytes 4423680 | tf_op jit(solution)/shard_map/all_gather | solution.py:100
  49.3 160.0 %all-gather.17.cloned.1.call-start = ((), (), s32[]{:S(2)}) async-start(), calls=%async_computation.11 | async-start | bytes 2211840 | tf_op jit(solution)/shard_map/all_gather | solution.py:101
  49.9 277.8 %reduce-scatter.7.cloned.1.call-start = ((), (), s32[]{:S(2)}) async-start(), calls=%async_computation.12 | async-start | bytes 3538944 | tf_op jit(solution)/shard_map/reduce_scatter | solution.py:210
  137.7 17.1 %copy-start.14 = (bf16[128,768]{1,0:T(8,128)(2,1)S(1)}, bf16[128,768]{1,0:T(8,128)(2,1)}, u32[]{:S(2)}) copy-start(bf16[128,768]{1,0:T(8,128)(2,1)} %param.12) | copy-start | bytes 589828
  149.5 37.5 %copy-start.44 = (f32[768]{0:T(1024)S(1)}, f32[768]{0:T(1024)}, u32[]{:S(2)}) copy-start(f32[768]{0:T(1024)} %convert_element_type.121) | copy-start | bytes 9220
  150.6 39.1 %copy-start.22 = (bf16[12,64,128]{2,1,0:T(8,128)(2,1)}, bf16[12,64,128]{2,1,0:T(8,128)(2,1)S(1)}, u32[]{:S(2)}) copy-start(bf16[12,64,128]{2,1,0:T(8,128)(2,1)S(1)} %fusion.42) | copy-start | bytes 589828
  156.5 59.6 %copy-start.6 = (f32[128,768]{1,0:T(8,128)}, f32[128,768]{1,0:T(8,128)S(1)}, u32[]{:S(2)}) copy-start(f32[128,768]{1,0:T(8,128)S(1)} %get-tuple-element.500) | copy-start | bytes 1179652
  156.6 59.6 %copy-start.50 = (f32[128]{0:T(128)}, f32[128]{0:T(128)S(1)}, u32[]{:S(2)}) copy-start(f32[128]{0:T(128)S(1)} %broadcast_multiply_fusion) | copy-start | bytes 1540
  156.8 59.4 %copy-start.52 = (f32[128]{0:T(128)}, f32[128]{0:T(128)S(1)}, u32[]{:S(2)}) copy-start(f32[128]{0:T(128)S(1)} %fusion.44) | copy-start | bytes 1540
  156.8 52.5 %copy-start.27 = (bf16[128,768]{1,0:T(8,128)(2,1)S(1)}, bf16[128,768]{1,0:T(8,128)(2,1)}, u32[]{:S(2)}) copy-start(bf16[128,768]{1,0:T(8,128)(2,1)} %param.19) | copy-start | bytes 589828
  209.3 4.9 copy-start.8
  214.2 3.8 copy-start.16
  216.1 2.6 copy-start.5
  216.4 4.5 copy-start.55
  231.8 2.8 copy-start.10
  235.0 2.6 copy-start.13
  246.5 2.8 copy-start.10
  249.7 2.6 copy-start.13
  252.4 153.1 %reduce-scatter.9.cloned.1.call-start = ((), (), s32[]{:S(2)}) async-start(), calls=%async_computation.13 | async-start | bytes 3538944 | tf_op jit(solution)/shard_map/reduce_scatter | solution.py:211
  252.4 2.5 copy-start.21
  252.4 2.5 copy-start.28
  253.1 180.5 %reduce-scatter.13.cloned.1.call-start = ((), (), s32[]{:S(2)}) async-start(), calls=%async_computation.15 | async-start | bytes 1474560 | tf_op jit(solution)/shard_map/reduce_scatter | solution.py:236
  254.9 211.4 %reduce-scatter.17.cloned.1.call-start = ((), (), s32[]{:S(2)}) async-start(), calls=%async_computation.17 | async-start | bytes 2211840 | tf_op jit(solution)/shard_map/reduce_scatter | solution.py:242
  256.9 252.4 %reduce-scatter.15.cloned.1.call-start = ((), (), s32[]{:S(2)}) async-start(), calls=%async_computation.16 | async-start | bytes 4423680 | tf_op jit(solution)/shard_map/reduce_scatter | solution.py:239
  260.2 67.5 %copy-start.9 = (f32[12,64,128]{2,1,0:T(8,128)S(1)}, f32[12,64,128]{2,1,0:T(8,128)}, u32[]{:S(2)}) copy-start(f32[12,64,128]{2,1,0:T(8,128)} %get-tuple-element.308) | copy-start | bytes 1179652
  260.2 67.5 %copy-start.41 = (f32[128,32]{0,1:T(8,128)S(1)}, f32[128,32]{0,1:T(8,128)}, u32[]{:S(2)}) copy-start(f32[128,32]{0,1:T(8,128)} %copy-done.40) | copy-start | bytes 49156
  260.2 67.5 %copy-start.43 = (f32[128,32]{0,1:T(8,128)S(1)}, f32[128,32]{0,1:T(8,128)}, u32[]{:S(2)}) copy-start(f32[128,32]{0,1:T(8,128)} %copy-done.42) | copy-start | bytes 49156
  260.2 146.3 %copy-start.15 = (bf16[128,768]{1,0:T(8,128)(2,1)S(1)}, bf16[128,768]{1,0:T(8,128)(2,1)}, u32[]{:S(2)}) copy-start(bf16[128,768]{1,0:T(8,128)(2,1)} %param.12) | copy-start | bytes 589828
  260.2 146.3 %copy-start.39 = (f32[768]{0:T(1024)S(1)}, f32[768]{0:T(1024)}, u32[]{:S(2)}) copy-start(f32[768]{0:T(1024)} %copy-done.38) | copy-start | bytes 9220
  260.2 146.3 %copy-start.47 = (f32[128]{0:T(128)S(1)}, f32[128]{0:T(128)}, u32[]{:S(2)}) copy-start(f32[128]{0:T(128)} %copy-done.46) | copy-start | bytes 1540
  260.3 146.3 %copy-start.49 = (f32[128]{0:T(128)S(1)}, f32[128]{0:T(128)}, u32[]{:S(2)}) copy-start(f32[128]{0:T(128)} %copy-done.48) | copy-start | bytes 1540
  260.3 292.1 %reduce-scatter.11.cloned.1.call-start = ((), (), s32[]{:S(2)}) async-start(), calls=%async_computation.14 | async-start | bytes 4423680 | tf_op jit(solution)/shard_map/reduce_scatter | solution.py:233
  328.9 80.8 %copy-start.31 = (bf16[128,12,64]{0,2,1:T(8,128)(2,1)}, bf16[128,12,64]{0,2,1:T(8,128)(2,1)S(1)}, u32[]{:S(2)}) copy-start(bf16[128,12,64]{0,2,1:T(8,128)(2,1)S(1)} %get-tuple-element.506) | copy-start | bytes 589828
  406.6 3.1 copy-start.32
  412.3 57.6 %copy-start.58 = (f32[128]{0:T(128)S(1)}, f32[128]{0:T(128)}, u32[]{:S(2)}) copy-start(f32[128]{0:T(128)} %copy-done.57) | copy-start | bytes 1540
  412.3 57.9 %copy-start.54 = (bf16[768]{0:T(1024)(128)(2,1)S(1)}, bf16[768]{0:T(1024)(128)(2,1)}, u32[]{:S(2)}) copy-start(bf16[768]{0:T(1024)(128)(2,1)} %get-tuple-element.419) | copy-start | bytes 4612
  412.3 63.8 %copy-start.18 = (f32[128,768]{1,0:T(8,128)S(1)}, f32[128,768]{1,0:T(8,128)}, u32[]{:S(2)}) copy-start(f32[128,768]{1,0:T(8,128)} %copy-done.17) | copy-start | bytes 1179652
  412.3 63.8 %copy-start.56 = (f32[128]{0:T(128)S(1)}, f32[128]{0:T(128)}, u32[]{:S(2)}) copy-start(f32[128]{0:T(128)} %copy-done.55) | copy-start | bytes 1540
  469.9 82.5 %copy-start.36 = (bf16[288,768]{1,0:T(8,128)(2,1)S(1)}, bf16[288,768]{1,0:T(8,128)(2,1)}, u32[]{:S(2)}) copy-start(bf16[288,768]{1,0:T(8,128)(2,1)} %reduce-scatter.17.cloned.1.call-done) | copy-start | bytes 1327108
  469.9 82.5 %copy-start.37 = (bf16[192,768]{1,0:T(8,128)(2,1)S(1)}, bf16[192,768]{1,0:T(8,128)(2,1)}, u32[]{:S(2)}) copy-start(bf16[192,768]{1,0:T(8,128)(2,1)} %reduce-scatter.13.cloned.1.call-done) | copy-start | bytes 884740
  (34 other events, 49.8 us)
Sparse Core Ops, SparseCore 0:
  9.6 33.4 all-gather.6
  46.8 44.1 all-gather.10
  93.6 44.0 all-gather.8
  139.1 15.6 all-gather.12
  156.2 30.7 all-gather.14
  188.5 20.7 all-gather.16
  252.5 75.1 reduce-scatter.6
  331.3 74.2 reduce-scatter.8
  408.7 24.9 reduce-scatter.12
  436.9 29.3 reduce-scatter.16
  468.9 40.3 reduce-scatter.14
  511.9 40.4 reduce-scatter.10
where the time goes:
time: 760 us; the launch traced here: 759 us
  waiting for transfers between devices  436 us (57%)
  blocking collectives  214 us (28%)
  matrix products  44.2 us (6%)
  local copies, waits for them, and re-layouts  36.9 us (5%)
  between operations  16.3 us (2%)
  other arithmetic  11 us (1%)
    psum x1, blocking collectives, on_device(): lax.psum((owned[0], owned[1], owned[2], owned[3], owned[4], owned[5]), 'c...  200 us
    reduce_scatter x1, waiting for transfers between devices, on_device(): lax.psum_scatter(value_terms, 'ctx', scatter_dimension=1, tiled=True)  76.6 us
    reduce_scatter x1, waiting for transfers between devices, on_device(): lax.psum_scatter(key_terms, 'ctx', scatter_dimension=1, tiled=True)  67.4 us
    all_gather x1, waiting for transfers between devices, on_device(): lax.all_gather(key_cols, 'ctx', axis=1, tiled=True)  44.2 us
    reduce_scatter x1, waiting for transfers between devices, on_device(): lax.psum_scatter(grad_qkv.astype(jnp.bfloat16), 'dp', scatter_dimension=0...  43.1 us
    all_gather x1, waiting for transfers between devices, on_device(): lax.all_gather(value_cols, 'ctx', axis=1, tiled=True)  40.2 us
    reduce_scatter x1, waiting for transfers between devices, on_device(): lax.psum_scatter(grad_down.astype(jnp.bfloat16), 'dp', scatter_dimension=...  32.6 us
    reduce_scatter x1, waiting for transfers between devices, on_device(): lax.psum_scatter(grad_in.astype(jnp.bfloat16), 'dp', scatter_dimension=0,...  32.2 us
  transfers between devices with their start and end apart: 12, of which 12 were waited for; matrix products, arithmetic and copies ran while one was open for 6% of the time, Pallas kernels for 0%

commit v1 on v0

v1 whole, which is shorter than its diff:
```python
import functools
import math

import jax
import jax.numpy as jnp
import numpy as np
from jax import lax
from jax.experimental import pallas as pl
from jax.experimental.pallas import tpu as pltpu
from jax.sharding import PartitionSpec as P

HEADS = 12
HEAD_DIM = 64
THETA = 160000.0
EPS = 1e-05
CHUNK_BITS = 3
CHUNKS = 1 << CHUNK_BITS
BF = jnp.bfloat16
F32 = jnp.float32
VMEM_LIMIT = 58 * 1024 * 1024


def whole(shape):
    return pl.BlockSpec(shape, lambda *_: (0,) * len(shape))


def params(limit=VMEM_LIMIT):
    return pltpu.CompilerParams(vmem_limit_bytes=limit)


def cost(flops, moved, trans=0):
    return pl.CostEstimate(flops=int(flops), bytes_accessed=int(moved), transcendentals=int(trans))


def dot(left, right, dims=((1,), (0,))):
    return lax.dot_general(left, right, (dims, ((), ())), preferred_element_type=F32)


NT = ((1,), (1,))
TN = ((0,), (0,))


def normalise(values):
    center = values - jnp.mean(values, axis=-1, keepdims=True)
    spread = jnp.mean(center * center, axis=-1, keepdims=True)
    scale = lax.rsqrt(spread + EPS)
    return center * scale, scale


def norm_back(grad, xhat, scale, gain):
    inner = grad * gain
    return scale * (
        inner
        - jnp.mean(inner, axis=-1, keepdims=True)
        - xhat * jnp.mean(inner * xhat, axis=-1, keepdims=True)
    )


def swap_halves(values):
    lane = lax.broadcasted_iota(jnp.int32, values.shape, 1)
    return jnp.where(lane % 64 < 32, pltpu.roll(values, 96, 1), pltpu.roll(values, 32, 1))


def rotate(values, cos, sin):
    return values * cos + swap_halves(values) * sin


def rotate_back(values, cos, sin):
    return values * cos - swap_halves(values) * sin


def fold(pieces):
    rows = [p[8 * i : 8 * i + 8] for p in pieces for i in range(p.shape[0] // 8)]
    flat = jnp.concatenate(rows, axis=1)
    half = flat.shape[1] // 2
    return jnp.concatenate([flat[:, :half], flat[:, half:]], axis=0)


def unfold(block, shapes):
    flat = jnp.concatenate([block[:8], block[8:]], axis=1)
    out, at = [], 0
    for rows, cols in shapes:
        parts = []
        for _ in range(rows // 8):
            parts.append(flat[:, at : at + cols])
            at += cols
        out.append(jnp.concatenate(parts, axis=0))
    return out


def place(svec, j, chunk):
    keep = j & 1
    upper = j >> 1
    core = (svec[0] & 1) ^ keep
    rel = chunk ^ svec[1 + keep]
    low = CHUNK_BITS - 1
    first = upper * CHUNKS + rel
    second = ((rel >> low) << CHUNK_BITS) | (upper << low) | (rel & ((1 << low) - 1))
    return jnp.where(core == 0, first, second)


def qkv_kernel(svec, x_ref, w0, w1, w2, w3, gain_ref, cos_ref, sin_ref, n_ref, q_ref, k_ref, v_ref, w_ref, *, own):
    rows = w_ref.shape[0] // 4
    width = n_ref.shape[1]

    @pl.when(pl.program_id(0) == 0)
    def _():
        for j, piece in enumerate((w0, w1, w2, w3)):
            at = pl.multiple_of((svec[0] ^ j) * rows, 16)
            w_ref[pl.ds(at, rows), :] = piece[:rows, :]

    xhat, _ = normalise(x_ref[...].astype(F32))
    normed = (xhat * gain_ref[...]).astype(BF)
    n_ref[...] = normed
    cos, sin = cos_ref[...], sin_ref[...]
    keys = dot(normed, w_ref[:, width : 2 * width])
    for g in range(width // 128):
        cut = slice(128 * g, 128 * g + 128)
        k_ref[:, cut] = rotate(keys[:, cut], cos, sin).astype(BF)
    v_ref[...] = dot(normed, w_ref[:, 2 * width :]).astype(BF)

    @pl.when(pl.program_id(0) == 0)
    def _():
        queries = dot(normed[:own], w_ref[:, :width])
        for g in range(width // 128):
            cut = slice(128 * g, 128 * g + 128)
            q_ref[:, cut] = rotate(queries[:, cut], cos[:own], sin[:own]).astype(BF)


def head_mask(shape, head):
    return lax.broadcasted_iota(jnp.int32, shape, 1) // HEAD_DIM == head


def fold_scale(q, head):
    return jnp.where(head_mask(q.shape, head), q, jnp.zeros_like(q)) * jnp.asarray(HEAD_DIM**-0.5, BF)


def attend_kernel(q_ref, k_ref, v_ref, o_ref, lse_ref):
    q, k, v = q_ref[...], k_ref[...], v_ref[...]
    for h in range(2):
        scores = dot(k, fold_scale(q, h), NT)
        top = jnp.max(scores, axis=0, keepdims=True)
        weights = jnp.exp(scores - top)
        total = jnp.sum(weights, axis=0, keepdims=True)
        out = dot(v, weights.astype(BF), TN)
        cut = slice(HEAD_DIM * h, HEAD_DIM * h + HEAD_DIM)
        o_ref[cut, :] = out[cut, :] / total
        lse_ref[0, h : h + 1, :] = top + jnp.log(total)


def middle_kernel(
    svec, x_ref, at_ref, p0, p1, p2, p3, dy_ref, gain_ref,
    lo_ref, dm_ref, da_ref, dat_ref, gk_ref, gs_ref,
    win, wout, wdown, n2t, attnt, hidt,
):
    width = x_ref.shape[1]
    rows = width // 4
    ff = wdown.shape[0]
    frows = ff // 4
    for j, piece in enumerate((p0, p1, p2, p3)):
        at = pl.multiple_of((svec[0] ^ j) * rows, 16)
        for b in range(3):
            win[pl.ds(at, rows), b * width : (b + 1) * width] = piece[b * rows : (b + 1) * rows, :]
        wout[pl.ds(at, rows), :] = piece[3 * rows : 4 * rows, :]
        fat = pl.multiple_of((svec[0] ^ j) * frows, 16)
        wdown[pl.ds(fat, frows), :] = piece[4 * rows : 4 * rows + frows, :]

    gain = gain_ref[...]
    attn_t = at_ref[...]
    attnt[...] = attn_t.astype(BF)
    attn_low = jnp.transpose(attn_t).astype(BF)
    mid = x_ref[...].astype(F32) + dot(attn_low, wout[...])
    xhat, scale = normalise(mid)
    normed = xhat * gain
    n2t[...] = jnp.transpose(normed).astype(BF)
    up = dot(normed.astype(BF), win[...])
    gate, lin = up[:, :ff], up[:, ff:]
    cdf = 0.5 * (1.0 + lax.erf(gate * (2.0**-0.5)))
    act = gate * cdf
    hidden = act * lin
    hidt[...] = jnp.transpose(hidden).astype(BF)
    lo_ref[...] = (mid + dot(hidden.astype(BF), wdown[...])).astype(BF)
    dy = dy_ref[...]
    d_hidden = dot(dy, wdown[...], NT)
    pdf = jnp.exp(-0.5 * gate * gate) * (1.0 / math.sqrt(2.0 * math.pi))
    d_gate = (d_hidden * lin * (cdf + gate * pdf)).astype(BF)
    d_lin = (d_hidden * act).astype(BF)
    d_up = jnp.concatenate([d_gate, d_lin], axis=1)
    d_mid = dy.astype(F32) + norm_back(dot(d_up, win[...], NT), xhat, scale, gain)
    dm_ref[...] = d_mid
    d_branch = d_mid.astype(BF)
    da_ref[...] = dot(d_branch, wout[...], NT).astype(BF)
    dat_ref[...] = dot(wout[...], d_branch, NT).astype(BF)
    for j in (1, 3, 2, 0):
        q = svec[0] ^ j
        at = pl.multiple_of(q * rows, 16)
        fat = pl.multiple_of(q * frows, 16)
        g_in = dot(n2t[pl.ds(at, rows), :], d_up)
        g_out = dot(attnt[pl.ds(at, rows), :], d_branch)
        g_down = dot(hidt[pl.ds(fat, frows), :], dy)
        target = gs_ref if j & 1 else gk_ref
        step = rows // CHUNKS
        fstep = frows // CHUNKS
        for c in range(CHUNKS):
            fs = 2 * fstep * (c // 2) + (fstep - 4) * (c % 2)
            block = fold(
                [g_in[c * step : (c + 1) * step], g_out[c * step : (c + 1) * step], g_down[fs : fs + fstep + 4]]
            )
            target[place(svec, j, c)] = block.astype(BF)


def attend_back_kernel(q_ref, k_ref, v_ref, da_ref, dat_ref, at_ref, lse_ref, cos_ref, sin_ref, dq_ref, dkv_ref):
    q, k, v, da = q_ref[...], k_ref[...], v_ref[...], da_ref[...]
    own = q.shape[0]
    prod = dat_ref[...].astype(F32) * at_ref[...]
    d_key, d_value, d_query = 0.0, 0.0, []
    for h in range(2):
        cut = slice(HEAD_DIM * h, HEAD_DIM * h + HEAD_DIM)
        q_scaled = fold_scale(q, h)
        da_head = jnp.where(head_mask(da.shape, h), da, jnp.zeros_like(da))
        probs = jnp.exp(dot(k, q_scaled, NT) - lse_ref[0, h : h + 1, :])
        delta = jnp.sum(prod[cut, :], axis=0, keepdims=True)
        d_scores = (probs * (dot(v, da_head, NT) - delta)).astype(BF)
        d_value += dot(probs.astype(BF), da_head)
        d_key += dot(d_scores, q_scaled)
        d_query.append(dot(d_scores, k, TN))
    dkv_ref[0] = rotate_back(d_key, cos_ref[...], sin_ref[...]).astype(BF)
    dkv_ref[1] = d_value.astype(BF)
    d_q = jnp.where(head_mask(q.shape, 0), d_query[0], d_query[1]) * (HEAD_DIM**-0.5)
    dq_ref[...] = rotate_back(d_q, cos_ref[:own, :], sin_ref[:own, :]).astype(BF)


def qkv_grad_kernel(svec, n_ref, dkv_ref, dq_ref, gk_ref, gs_ref, acc):
    width = n_ref.shape[1]
    rows = width // 4
    step = rows // CHUNKS
    own = dq_ref.shape[0]
    normed = n_ref[...]
    first = pl.program_id(0) == 0

    @pl.when(first)
    def _():
        acc[:, :width] = dot(normed[:own], dq_ref[...], TN)
        for b in range(2):
            acc[:, (b + 1) * width : (b + 2) * width] = dot(normed, dkv_ref[b], TN)

    @pl.when(jnp.logical_not(first))
    def _():
        for b in range(2):
            acc[:, (b + 1) * width : (b + 2) * width] += dot(normed, dkv_ref[b], TN)

    @pl.when(pl.program_id(0) == pl.num_programs(0) - 1)
    def _():
        for j in (1, 3, 2, 0):
            target = gs_ref if j & 1 else gk_ref
            at = pl.multiple_of((svec[0] ^ j) * rows, 8)
            for c in range(CHUNKS):
                block = acc[pl.ds(pl.multiple_of(at + c * step, 8), step), :]
                target[place(svec, j, c)] = fold([block]).astype(BF)


def tokens_grad_kernel(x_ref, dq_ref, dkv_ref, w_ref, gain_ref, dm_ref, out_ref):
    d_proj = jnp.concatenate([dq_ref[...], dkv_ref[0], dkv_ref[1]], axis=1)
    d_normed = dot(d_proj, w_ref[...], NT)
    xhat, scale = normalise(x_ref[...].astype(F32))
    out_ref[...] = dm_ref[...] + norm_back(d_normed, xhat, scale, gain_ref[...])


def finish_first_kernel(svec, ra, rb, w_ref, in_ref, out_ref, down_ref, gain_ref, *, step, fstep, width):
    shapes = ((step, 3 * width), (step, width), (fstep + 4, width))
    parts_a = unfold(ra[0].astype(F32), shapes)
    parts_b = unfold(rb[0].astype(F32), shapes)
    both = [jnp.concatenate([a, b], axis=0) for a, b in zip(parts_a[:2], parts_b[:2])]
    in_ref[...] = both[0]
    out_ref[...] = both[1]
    down_ref[...] = jnp.concatenate([parts_a[2], parts_b[2][8:]], axis=0)
    total = jnp.sum(w_ref[...].astype(F32) * both[0], axis=1, keepdims=True)
    gain_ref[...] = jnp.broadcast_to(total, gain_ref.shape)


def finish_second_kernel(svec, ra, rb, w_ref, out_ref, gain_ref, *, step, width):
    shapes = ((step, 3 * width),)
    grad = jnp.concatenate([unfold(ra[0].astype(F32), shapes)[0], unfold(rb[0].astype(F32), shapes)[0]], axis=0)
    out_ref[...] = grad
    total = jnp.sum(w_ref[...].astype(F32) * grad, axis=1, keepdims=True)
    gain_ref[...] = jnp.broadcast_to(total, gain_ref.shape)


class Links:
    def __init__(self, n_dp, n_ctx):
        self.n_dp, self.n_ctx = n_dp, n_ctx
        self.bits = n_ctx.bit_length() - 1
        rise = list(range(self.bits))
        self.orders = (rise, rise[1:] + rise[:1])

    def swap(self, value, dims):
        pairs = []
        for d in range(self.n_dp):
            dim = dims[d & 1]
            for c in range(self.n_ctx):
                if dim == "core":
                    to = (d ^ 1, c)
                elif dim == "y":
                    to = (d ^ 2, c)
                else:
                    to = (d, c ^ (1 << dim))
                pairs.append((d * self.n_ctx + c, to[0] * self.n_ctx + to[1]))
        return lax.ppermute(value, ("dp", "ctx"), pairs)

    def both(self, step):
        return (self.orders[0][step], self.orders[1][step])


def add_low(left, right):
    return (left.astype(F32) + right.astype(F32)).astype(BF)


def reduce_chunks(links, keep, send):
    recv = links.swap(send, ("core", "core"))
    walk = [list(o[:CHUNK_BITS]) for o in links.orders]
    walk[0].insert(0, "y")
    walk[1].insert(1, "y")
    for step in range(CHUNK_BITS + 1):
        half = keep.shape[0] // 2
        send = add_low(keep[half:], recv[half:])
        keep = add_low(keep[:half], recv[:half])
        recv = links.swap(send, (walk[0][step], walk[1][step]))
    total = add_low(keep, recv)
    for step in range(CHUNK_BITS, links.bits):
        total = add_low(total, links.swap(total, links.both(step)))
    for step in reversed(range(CHUNK_BITS)):
        total = jnp.concatenate([total, links.swap(total, links.both(step))], axis=0)
    return total


def on_device(tokens, w_qkv, w_attn_out, w_in, w_down, gain_attn, gain_mlp, cotangent, *, n_dp, n_ctx):
    links = Links(n_dp, n_ctx)
    own, width = tokens.shape
    rows = w_qkv.shape[0]
    frows = w_down.shape[0]
    ff = frows * n_dp
    seq = own * n_ctx
    groups = width // 128
    step, fstep = rows // CHUNKS, frows // CHUNKS
    dp_at = lax.axis_index("dp")
    ctx_at = lax.axis_index("ctx")
    core = dp_at & 1
    upper = dp_at >> 1

    marks = []
    for order in links.orders:
        mark = 0
        for i in range(CHUNK_BITS):
            mark = mark | (((ctx_at >> order[i]) & 1) << (CHUNK_BITS - 1 - i))
        marks.append(mark)
    mine = jnp.where(core == 0, marks[0], marks[1])
    other = jnp.where(core == 0, marks[1], marks[0])
    svec = jnp.stack([dp_at, mine, other]).astype(jnp.int32)

    gains_row = jnp.zeros((16, 3 * width), BF)
    gains_row = gains_row.at[0, :rows].set(gain_attn).at[1, :rows].set(gain_mlp)
    pack_qkv = jnp.concatenate([w_qkv, gains_row], axis=0)
    pack_rest = jnp.concatenate(
        [w_in[:, :width], w_in[:, width : 2 * width], w_in[:, 2 * width :], w_attn_out, w_down], axis=0
    )
    qkv_y = links.swap(pack_qkv, ("y", "y"))
    qkv_c = links.swap(pack_qkv, ("core", "core"))

    everyone = tokens
    for i in reversed(range(links.bits)):
        everyone = jnp.concatenate([everyone, links.swap(everyone, links.both(i))], axis=0)

    qkv_cy = links.swap(qkv_y, ("core", "core"))
    pack_late, _ = lax.optimization_barrier((pack_rest, qkv_y))
    rest_y = links.swap(pack_late, ("y", "y"))
    rest_c = links.swap(pack_late, ("core", "core"))
    rest_cy = links.swap(rest_y, ("core", "core"))

    def gain_of(row):
        g = [p[rows + row, :rows].astype(F32) for p in (pack_qkv, qkv_c, qkv_y, qkv_cy)]
        near = jnp.where(core == 0, jnp.concatenate([g[0], g[1]]), jnp.concatenate([g[1], g[0]]))
        far = jnp.where(core == 0, jnp.concatenate([g[2], g[3]]), jnp.concatenate([g[3], g[2]]))
        full = jnp.where(upper == 0, jnp.concatenate([near, far]), jnp.concatenate([far, near]))
        return full.reshape(1, width)

    gain_one, gain_two = gain_of(0), gain_of(1)

    flips = []
    for order in links.orders:
        at = np.arange(n_ctx)
        flips.append(sum(((at >> i) & 1) << order[links.bits - 1 - i] for i in range(links.bits)).astype(np.int32))
    owner = ctx_at ^ jnp.where(core == 0, jnp.asarray(flips[0]), jnp.asarray(flips[1]))
    positions = (owner[:, None] * own + jnp.arange(own, dtype=jnp.int32)[None, :]).reshape(seq).astype(F32)
    half = HEAD_DIM // 2
    frequencies = jnp.exp(jnp.arange(half, dtype=F32) * (-2.0 * math.log(THETA) / HEAD_DIM))
    angles = positions[:, None] * frequencies[None, :]
    cos, sin = jnp.cos(angles), jnp.sin(angles)
    cos = jnp.concatenate([cos] * 4, axis=1)
    sin = jnp.concatenate([-sin, sin, -sin, sin], axis=1)

    block = math.gcd(seq, 256)
    normed, queries, keys, values, full_qkv = pl.pallas_call(
        functools.partial(qkv_kernel, own=own),
        grid_spec=pltpu.PrefetchScalarGridSpec(
            num_scalar_prefetch=1,
            grid=(seq // block,),
            in_specs=[pl.BlockSpec((block, width), lambda i, s: (i, 0))]
            + [whole(pack_qkv.shape)] * 4
            + [whole((1, width))]
            + [pl.BlockSpec((block, 128), lambda i, s: (i, 0))] * 2,
            out_specs=[
                pl.BlockSpec((block, width), lambda i, s: (i, 0)),
                whole((own, width)),
                pl.BlockSpec((block, width), lambda i, s: (i, 0)),
                pl.BlockSpec((block, width), lambda i, s: (i, 0)),
                whole((width, 3 * width)),
            ],
        ),
        out_shape=[
            jax.ShapeDtypeStruct((seq, width), BF),
            jax.ShapeDtypeStruct((own, width), BF),
            jax.ShapeDtypeStruct((seq, width), BF),
            jax.ShapeDtypeStruct((seq, width), BF),
            jax.ShapeDtypeStruct((width, 3 * width), BF),
        ],
        compiler_params=params(),
        cost_estimate=cost(4 * seq * width * width, 14e6),
        name="qkv",
    )(svec, everyone, pack_qkv, qkv_c, qkv_y, qkv_cy, gain_one, cos, sin)

    own_pair = pl.BlockSpec((own, 128), lambda g: (0, g))
    seq_pair = pl.BlockSpec((seq, 128), lambda g: (0, g))
    turned_pair = pl.BlockSpec((128, own), lambda g: (g, 0))
    lse_pair = pl.BlockSpec((1, 8, own), lambda g: (g, 0, 0))
    attn_t, lse = pl.pallas_call(
        attend_kernel,
        grid=(groups,),
        in_specs=[own_pair, seq_pair, seq_pair],
        out_specs=[turned_pair, lse_pair],
        out_shape=[jax.ShapeDtypeStruct((width, own), F32), jax.ShapeDtypeStruct((groups, 8, own), F32)],
        compiler_params=params(),
        cost_estimate=cost(8 * seq * own * width, 4e6, seq * own * HEADS),
        name="attend",
    )(queries, keys, values)

    vm = pl.BlockSpec(memory_space=pltpu.VMEM)
    length = (3 * step * 4 * width // 3 + (fstep + 4) * width) // 16
    layer_out, d_mid, d_attn, d_attn_t, first_keep, first_send = pl.pallas_call(
        middle_kernel,
        in_specs=[pl.BlockSpec(memory_space=pltpu.SMEM)] + [vm] * 8,
        out_specs=[vm] * 6,
        out_shape=[
            jax.ShapeDtypeStruct((own, width), BF),
            jax.ShapeDtypeStruct((own, width), F32),
            jax.ShapeDtypeStruct((own, width), BF),
            jax.ShapeDtypeStruct((width, own), BF),
            jax.ShapeDtypeStruct((2 * CHUNKS, 16, length), BF),
            jax.ShapeDtypeStruct((2 * CHUNKS, 16, length), BF),
        ],
        scratch_shapes=[
            pltpu.VMEM((width, 3 * width), BF),
            pltpu.VMEM((width, width), BF),
            pltpu.VMEM((ff, width), BF),
            pltpu.VMEM((width, own), BF),
            pltpu.VMEM((width, own), BF),
            pltpu.VMEM((ff, own), BF),
        ],
        compiler_params=params(),
        cost_estimate=cost(6 * own * width * (4 * width + ff), 16e6),
        name="middle",
    )(svec, tokens, attn_t, pack_rest, rest_c, rest_y, rest_cy, cotangent, gain_two)

    d_query, d_kv = pl.pallas_call(
        attend_back_kernel,
        grid=(groups,),
        in_specs=[
            own_pair, seq_pair, seq_pair, own_pair, turned_pair, turned_pair, lse_pair,
            whole((seq, 128)), whole((seq, 128)),
        ],
        out_specs=[own_pair, pl.BlockSpec((2, seq, 128), lambda g: (0, 0, g))],
        out_shape=[jax.ShapeDtypeStruct((own, width), BF), jax.ShapeDtypeStruct((2, seq, width), BF)],
        compiler_params=params(),
        cost_estimate=cost(20 * seq * own * width, 8e6, seq * own * HEADS),
        name="attend_back",
    )(queries, keys, values, d_attn, d_attn_t, attn_t, lse, cos, sin)

    deep = math.gcd(seq, 1024)
    second_keep, second_send = pl.pallas_call(
        qkv_grad_kernel,
        grid_spec=pltpu.PrefetchScalarGridSpec(
            num_scalar_prefetch=1,
            grid=(seq // deep,),
            in_specs=[
                pl.BlockSpec((deep, width), lambda i, s: (i, 0)),
                pl.BlockSpec((2, deep, width), lambda i, s: (0, i, 0)),
                whole((own, width)),
            ],
            out_specs=[whole((2 * CHUNKS, 16, step * 3 * width // 16))] * 2,
            scratch_shapes=[pltpu.VMEM((width, 3 * width), F32)],
        ),
        out_shape=[jax.ShapeDtypeStruct((2 * CHUNKS, 16, step * 3 * width // 16), BF)] * 2,
        compiler_params=params(),
        cost_estimate=cost(4 * seq * width * width, 9e6),
        name="qkv_grad",
    )(svec, normed, d_kv, d_query)

    first = reduce_chunks(links, first_keep, first_send)
    second = reduce_chunks(links, second_keep, second_send)

    for i in range(links.bits):
        mid = d_kv.shape[1] // 2
        d_kv = add_low(d_kv[:, :mid], links.swap(d_kv[:, mid:], links.both(i)))

    tokens_grad = pl.pallas_call(
        tokens_grad_kernel,
        in_specs=[vm] * 6,
        out_specs=vm,
        out_shape=jax.ShapeDtypeStruct((own, width), F32),
        compiler_params=params(),
        cost_estimate=cost(6 * own * width * width, 5e6),
        name="tokens_grad",
    )(tokens, d_query, d_kv, full_qkv, gain_one, d_mid)

    def pair_specs(length):
        return [
            pl.BlockSpec((1, 16, length), lambda i, s: ((2 * i) ^ s[1], 0, 0)),
            pl.BlockSpec((1, 16, length), lambda i, s: ((2 * i + 1) ^ s[1], 0, 0)),
        ]

    def row_spec(count, cols):
        return pl.BlockSpec((count, cols), lambda i, s: (i, 0))

    in_grad, out_grad, down_grad, gain_mlp_sum = pl.pallas_call(
        functools.partial(finish_first_kernel, step=step, fstep=fstep, width=width),
        grid_spec=pltpu.PrefetchScalarGridSpec(
            num_scalar_prefetch=1,
            grid=(CHUNKS // 2,),
            in_specs=pair_specs(length) + [row_spec(2 * step, 3 * width)],
            out_specs=[
                row_spec(2 * step, 3 * width),
                row_spec(2 * step, width),
                row_spec(2 * fstep, width),
                row_spec(2 * step, 128),
            ],
        ),
        out_shape=[
            jax.ShapeDtypeStruct((rows, 3 * width), F32),
            jax.ShapeDtypeStruct((rows, width), F32),
            jax.ShapeDtypeStruct((frows, width), F32),
            jax.ShapeDtypeStruct((rows, 128), F32),
        ],
        compiler_params=params(),
        cost_estimate=cost(1e6, 6e6),
        name="finish_first",
    )(svec, first, first, w_in)

    qkv_grad, gain_attn_sum = pl.pallas_call(
        functools.partial(finish_second_kernel, step=step, width=width),
        grid_spec=pltpu.PrefetchScalarGridSpec(
            num_scalar_prefetch=1,
            grid=(CHUNKS // 2,),
            in_specs=pair_specs(step * 3 * width // 16) + [row_spec(2 * step, 3 * width)],
            out_specs=[row_spec(2 * step, 3 * width), row_spec(2 * step, 128)],
        ),
        out_shape=[jax.ShapeDtypeStruct((rows, 3 * width), F32), jax.ShapeDtypeStruct((rows, 128), F32)],
        compiler_params=params(),
        cost_estimate=cost(1e6, 4e6),
        name="finish_second",
    )(svec, second, second, w_qkv)

    return (
        layer_out,
        tokens_grad,
        qkv_grad,
        out_grad,
        in_grad,
        down_grad,
        gain_attn_sum[:, 0] / gain_attn.astype(F32),
        gain_mlp_sum[:, 0] / gain_mlp.astype(F32),
    )


def solution(mesh):
    return jax.shard_map(
        functools.partial(on_device, n_dp=mesh.shape["dp"], n_ctx=mesh.shape["ctx"]),
        mesh=mesh,
        in_specs=(
            P(("dp", "ctx"), None),
            P("dp", None),
            P("dp", None),
            P("dp", None),
            P("dp", None),
            P("dp"),
            P("dp"),
            P(("dp", "ctx"), None),
        ),
        out_specs=(
            P(("dp", "ctx"), None),
            P(("dp", "ctx"), None),
            P("dp", None),
            P("dp", None),
            P("dp", None),
            P("dp", None),
            P("dp"),
            P("dp"),
        ),
        check_vma=False,
    )
```

time: 760 us -> 267 us (0.35)
  waiting for transfers between devices: 436 us -> 128 us
  blocking collectives: 214 us -> 0 us
  Pallas kernels: 0 us -> 62.7 us
  matrix products: 44.2 us -> 0 us
  starting transfers between devices: 0.88 us -> 38.3 us
  local copies, waits for them, and re-layouts: 36.9 us -> 10.2 us
  between operations: 16.3 us -> 0.92 us
  other arithmetic: 11 us -> 21.5 us
    reduce_scatter x6 -> x0, waiting for transfers between devices: 273 us -> none  [the longest x1 76.6 us: on_device(): lax.psum_scatter(value_terms, 'ctx', scatter_dimension=1, tiled=True)]
    psum x1 -> x0, blocking collectives: 200 us -> none  [on_device(): lax.psum((owned[0], owned[1], owned[2], owned[3], owned[4], owned[5]), 'c...]
    all_gather x6 -> x0, waiting for transfers between devices: 159 us -> none  [the longest x1 44.2 us: on_device(): lax.all_gather(key_cols, 'ctx', axis=1, tiled=True)]
    ppermute x0 -> x28, waiting for transfers between devices: none -> 128 us  [swap(): return lax.ppermute(value, ('dp', 'ctx'), pairs)]
    pallas_call x0 -> x8, Pallas kernels: none -> 62.7 us  [the longest x1 12.6 us: on_device(): pl.pallas_call(middle_kernel, in_specs=[pl.BlockSpec(memory_space=pltpu.S...]
    dot_general x26 -> x0, matrix products: 44.2 us -> none  [the longest x2 5.71 us: attention_grads(): jnp.einsum('hqk,hdk->hdq', grad_scores, key_block, preferred_element_type...]
    ppermute x0 -> x28, starting transfers between devices: none -> 38.3 us  [swap(): return lax.ppermute(value, ('dp', 'ctx'), pairs)]
    unnamed x2 -> x0, blocking collectives: 14.1 us -> none
  transfers between devices with their start and end apart: 12 -> 28, of which waited for: 12 -> 14; matrix products, arithmetic and copies ran while one was open for 6% -> 9% of each run, Pallas kernels for 0% -> 17%
where the time goes in v1:
time: 267 us; the launch traced here: 262 us
  waiting for transfers between devices  128 us (48%)
  Pallas kernels  62.7 us (23%)
  starting transfers between devices  38.3 us (14%)
  other arithmetic  21.5 us (8%)
  local copies, waits for them, and re-layouts  10.2 us (4%)
    ppermute x28, waiting for transfers between devices, swap(): return lax.ppermute(value, ('dp', 'ctx'), pairs)  128 us
    ppermute x28, starting transfers between devices, swap(): return lax.ppermute(value, ('dp', 'ctx'), pairs)  38.3 us
    pallas_call x1, Pallas kernels, on_device(): pl.pallas_call(middle_kernel, in_specs=[pl.BlockSpec(memory_space=pltpu.S...  12.6 us
    pallas_call x1, Pallas kernels, on_device(): pl.pallas_call(functools.partial(qkv_kernel, own=own), grid_spec=pltpu.Pr...  10.6 us
    pallas_call x1, Pallas kernels, on_device(): pl.pallas_call(attend_back_kernel, grid=(groups,), in_specs=[own_pair, se...  9.7 us
    pallas_call x1, Pallas kernels, on_device(): pl.pallas_call(attend_kernel, grid=(groups,), in_specs=[own_pair, seq_pai...  8.02 us
    pallas_call x1, Pallas kernels, on_device(): pl.pallas_call(qkv_grad_kernel, grid_spec=pltpu.PrefetchScalarGridSpec(nu...  7.91 us
    convert_element_type x13, other arithmetic, add_low(): return (left.astype(F32) + right.astype(F32)).astype(BF)  5.77 us
  transfers between devices with their start and end apart: 28, of which 14 were waited for; matrix products, arithmetic and copies ran while one was open for 9% of the time, Pallas kernels for 17%

profile of v1, /device:TPU:0, one launch (start us, length us, event | category | flops | bytes accessed | tf_op | source)
XLA Modules:
  0.0 262.1 jit_solution(5903774905492398531)
XLA Ops:
  2.3 1.3 pad_maximum_fusion.2.w0
  3.7 3.0 %collective-permute-start.4 = (bf16[208,2304]{1,0:T(8,128)(2,1)S(1)}, bf16[208,2304]{1,0:T(8,128)(2,1)}, u32[]{:S(2)}, u32[]{:S(2)}) collective-permute-start(bf16[208,2304]{1,0:T(8,128)(2,1)S(1)} %pad_maximum_fusion.2.w0), channel_id=1, source_target_pairs={{0,16},{1,17},{2,18},{3,19},{4,20},{5,21},{6,22},{7,23},{8,24},{9,... | collective-permute-start | bytes 2875400 | tf_op jit(solution)/shard_map/ppermute | solution.py:308
  10.4 17.6 %collective-permute-done.4.w2 = bf16[208,2304]{1,0:T(8,128)(2,1)} collective-permute-done((bf16[208,2304]{1,0:T(8,128)(2,1)S(1)}, bf16[208,2304]{1,0:T(8,128)(2,1)}, u32[]{:S(2)}, u32[]{:S(2)}) %collective-permute-start.4) | collective-permute-done | bytes 958496 | tf_op jit(solution)/shard_map/ppermute | solution.py:308
  28.0 1.7 collective-permute-start.7
  29.8 2.6 collective-permute-start
  32.4 6.1 %collective-permute-done = bf16[128,768]{1,0:T(8,128)(2,1)S(1)} collective-permute-done((bf16[128,768]{1,0:T(8,128)(2,1)S(1)}, bf16[128,768]{1,0:T(8,128)(2,1)S(1)}, u32[]{:S(2)}, u32[]{:S(2)}) %collective-permute-start) | collective-permute-done | bytes 196640 | tf_op jit(solution)/shard_map/ppermute | solution.py:308
  39.3 1.9 fusion
  41.2 8.2 %collective-permute-done.1 = bf16[256,768]{1,0:T(8,128)(2,1)S(1)} collective-permute-done((bf16[256,768]{1,0:T(8,128)(2,1)S(1)}, bf16[256,768]{1,0:T(8,128)(2,1)S(1)}, u32[]{:S(2)}, u32[]{:S(2)}) %collective-permute-start.1) | collective-permute-done | bytes 393248 | tf_op jit(solution)/shard_map/ppermute | solution.py:308
  49.5 1.6 collective-permute-start.2
  51.1 1.8 pad_maximum_fusion.6
  54.1 10.9 %collective-permute-done.7.p2 = bf16[1056,768]{1,0:T(8,128)(2,1)} collective-permute-done((bf16[1056,768]{1,0:T(8,128)(2,1)}, bf16[1056,768]{1,0:T(8,128)(2,1)}, u32[]{:S(2)}, u32[]{:S(2)}) %collective-permute-start.7) | collective-permute-done | bytes 1622048 | tf_op jit(solution)/shard_map/ppermute | solution.py:308
  66.7 2.4 pad_maximum_fusion.1.x_ref
  70.5 10.6 %qkv.1 = (bf16[1024,768]{1,0:T(8,128)(2,1)}, bf16[128,768]{1,0:T(8,128)(2,1)}, bf16[1024,768]{1,0:T(8,128)(2,1)}, bf16[1024,768]{1,0:T(8,128)(2,1)}, bf16[768,2304]{1,0:T(8,128)(2,1)}) custom-call(s32[3]{0:T(128)} %pad_add_fusion.svec, bf16[1024,768]{1,0:T(8,128)(2,1)} %pad_maximum_fusion.1.x_ref, bf16[208,2304]{1,0:T(8,128)(2,1)} %copy-done.4, ...), custom_call_target="tpu_custom_call" | custom-call | flops 2415919104 | bytes 14000000 | tf_op jit(solution)/shard_map/qkv/pallas_call | solution.py:402
  81.1 8.0 %attend.1 = (f32[768,128]{1,0:T(8,128)}, f32[6,8,128]{2,1,0:T(8,128)}) custom-call(bf16[128,768]{1,0:T(8,128)(2,1)} %get-tuple-element.56.q_ref, bf16[1024,768]{1,0:T(8,128)(2,1)} %get-tuple-element.57.k_ref, bf16[1024,768]{1,0:T(8,128)(2,1)} %get-tuple-element.58.v_ref), custom_call_target="tpu_custom_call" | custom-call | flops 805306368 | bytes 4000000 | tf_op jit(solution)/shard_map/attend/pallas_call | solution.py:435
  89.7 1.2 copy-done.11
  90.9 12.6 %middle.1 = (bf16[128,768]{1,0:T(8,128)(2,1)}, f32[128,768]{1,0:T(8,128)}, bf16[128,768]{1,0:T(8,128)(2,1)}, bf16[768,128]{1,0:T(8,128)(2,1)}, bf16[16,16,6528]{...) custom-call(s32[3]{0:T(128)} %pad_add_fusion.svec, bf16[128,768]{1,0:T(8,128)(2,1)} %x_ref.3, ...), custom_call_target="tpu_custom_call" | custom-call | flops 2491416576 | bytes 16000000 | tf_op jit(solution)/shard_map/middle/pallas_call | solution.py:448
  104.0 9.7 %attend_back.1 = (bf16[128,768]{1,0:T(8,128)(2,1)}, bf16[2,1024,768]{2,1,0:T(8,128)(2,1)}) custom-call(bf16[128,768]{1,0:T(8,128)(2,1)} %get-tuple-element.56.q_ref, bf16[1024,768]{1,0:T(8,128)(2,1)} %get-tuple-element.57.k_ref, bf16[1024,768]{1,0:T(8,128)(2,1)} %get-tuple-element.58.v_ref, bf16[128,768]{1,0:T(8,128)(2,1)} %get-tuple-element.62.da_ref, ...), custom_call_target="tpu_custom_call" | custom-call | flops 2013265920 | bytes 8000000 | tf_op jit(solution)/shard_map/attend_back/pallas_call | solution.py:473
  113.7 1.5 slice.200
  115.2 1.5 collective-permute-start.9
  116.7 7.9 %qkv_grad.1 = (bf16[16,16,3456]{2,1,0:T(8,128)(2,1)}, bf16[16,16,3456]{2,1,0:T(8,128)(2,1)}) custom-call(s32[3]{0:T(128)} %pad_add_fusion.svec, bf16[1024,768]{1,0:T(8,128)(2,1)} %get-tuple-element.69.n_ref, bf16[2,1024,768]{2,1,0:T(8,128)(2,1)} %get-tuple-element.66.dkv_ref, bf16[128,768]{1,0:T(8,128)(2,1)} %get-tuple-element.65.dq_ref), custom_call_target="tpu_custom_call" | custom-call | flops 2415919104 | bytes 9000000 | tf_op jit(solution)/shard_map/qkv_grad/pallas_call | solution.py:488
  124.6 11.2 %collective-permute-done.9 = bf16[2,512,768]{2,1,0:T(8,128)(2,1)} collective-permute-done((bf16[2,512,768]{2,1,0:T(8,128)(2,1)S(1)}, bf16[2,512,768]{2,1,0:T(8,128)(2,1)}, u32[]{:S(2)}, u32[]{:S(2)}) %collective-permute-start.9) | collective-permute-done | bytes 1572896 | tf_op jit(solution)/shard_map/ppermute | solution.py:308
  135.8 2.4 add_convert_fusion.2
  138.2 1.5 collective-permute-start.10
  140.2 1.6 collective-permute-start.13
  142.7 1.5 collective-permute-start.21
  144.2 21.3 %collective-permute-done.10 = bf16[2,256,768]{2,1,0:T(8,128)(2,1)S(1)} collective-permute-done((bf16[2,256,768]{2,1,0:T(8,128)(2,1)S(1)}, bf16[2,256,768]{2,1,0:T(8,128)(2,1)S(1)}, u32[]{:S(2)}, u32[]{:S(2)}) %collective-permute-start.10) | collective-permute-done | bytes 786464 | tf_op jit(solution)/shard_map/ppermute | solution.py:308
  165.7 3.2 %collective-permute-start.11 = (bf16[2,128,768]{2,1,0:T(8,128)(2,1)S(1)}, bf16[2,128,768]{2,1,0:T(8,128)(2,1)S(1)}, u32[]{:S(2)}, u32[]{:S(2)}) collective-permute-start(bf16[2,128,768]{2,1,0:T(8,128)(2,1)S(1)} %slice.249), channel_id=1, source_target_pairs={{0,4},{1,5},{2,6},{3,7},{4,0},{5,1},{6,2},{7,3},{8,9},{9,8},{10,11... | collective-permute-start | bytes 1179656 | tf_op jit(solution)/shard_map/ppermute | solution.py:308
  169.1 1.6 collective-permute-start.14
  170.7 7.8 %collective-permute-done.11 = bf16[2,128,768]{2,1,0:T(8,128)(2,1)S(1)} collective-permute-done((bf16[2,128,768]{2,1,0:T(8,128)(2,1)S(1)}, bf16[2,128,768]{2,1,0:T(8,128)(2,1)S(1)}, u32[]{:S(2)}, u32[]{:S(2)}) %collective-permute-start.11) | collective-permute-done | bytes 393248 | tf_op jit(solution)/shard_map/ppermute | solution.py:308
  179.7 1.6 collective-permute-start.22
  181.4 3.0 %collective-permute-start.15 = (bf16[2,16,3456]{2,1,0:T(8,128)(2,1)S(1)}, bf16[2,16,3456]{2,1,0:T(8,128)(2,1)S(1)}, u32[]{:S(2)}, u32[]{:S(2)}) collective-permute-start(bf16[2,16,3456]{2,1,0:T(8,128)(2,1)S(1)} %get-tuple-element.97), channel_id=1, source_target_pairs={{0,2},{1,3},{2,0},{3,1},{4,6},{5,7},{6,4},{7,5},{8,12},{9,13},{10,... | collective-permute-start | bytes 663560 | tf_op jit(solution)/shard_map/ppermute | solution.py:308
  184.4 7.9 %collective-permute-done.22 = bf16[4,16,6528]{2,1,0:T(8,128)(2,1)S(1)} collective-permute-done((bf16[4,16,6528]{2,1,0:T(8,128)(2,1)S(1)}, bf16[4,16,6528]{2,1,0:T(8,128)(2,1)S(1)}, u32[]{:S(2)}, u32[]{:S(2)}) %collective-permute-start.22) | collective-permute-done | bytes 835616 | tf_op jit(solution)/shard_map/ppermute | solution.py:308
  192.5 3.0 %collective-permute-start.23 = (bf16[2,16,6528]{2,1,0:T(8,128)(2,1)S(1)}, bf16[2,16,6528]{2,1,0:T(8,128)(2,1)S(1)}, u32[]{:S(2)}, u32[]{:S(2)}) collective-permute-start(bf16[2,16,6528]{2,1,0:T(8,128)(2,1)S(1)} %get-tuple-element.89), channel_id=1, source_target_pairs={{0,2},{1,3},{2,0},{3,1},{4,6},{5,7},{6,4},{7,5},{8,12},{9,13},{10,... | collective-permute-start | bytes 1253384 | tf_op jit(solution)/shard_map/ppermute | solution.py:308
  195.6 2.6 collective-permute-start.16
  198.1 7.0 %collective-permute-done.23 = bf16[2,16,6528]{2,1,0:T(8,128)(2,1)S(1)} collective-permute-done((bf16[2,16,6528]{2,1,0:T(8,128)(2,1)S(1)}, bf16[2,16,6528]{2,1,0:T(8,128)(2,1)S(1)}, u32[]{:S(2)}, u32[]{:S(2)}) %collective-permute-start.23) | collective-permute-done | bytes 417824 | tf_op jit(solution)/shard_map/ppermute | solution.py:308
  205.2 2.0 collective-permute-start.24
  208.3 12.8 %collective-permute-done.24 = bf16[1,16,6528]{2,1,0:T(8,128)(2,1)S(1)} collective-permute-done((bf16[1,16,6528]{2,1,0:T(8,128)(2,1)S(1)}, bf16[1,16,6528]{2,1,0:T(8,128)(2,1)S(1)}, u32[]{:S(2)}, u32[]{:S(2)}) %collective-permute-start.24) | collective-permute-done | bytes 208928 | tf_op jit(solution)/shard_map/ppermute | solution.py:308
  221.2 2.2 collective-permute-done.17
  223.5 5.4 %collective-permute-done.25 = bf16[1,16,6528]{2,1,0:T(8,128)(2,1)S(1)} collective-permute-done((bf16[1,16,6528]{2,1,0:T(8,128)(2,1)S(1)}, bf16[1,16,6528]{2,1,0:T(8,128)(2,1)S(1)}, u32[]{:S(2)}, u32[]{:S(2)}) %collective-permute-start.25) | collective-permute-done | bytes 208928 | tf_op jit(solution)/shard_map/ppermute | solution.py:308
  229.1 2.1 collective-permute-done.18
  231.3 1.6 collective-permute-start.19
  232.8 7.8 %collective-permute-done.26 = bf16[2,16,6528]{2,1,0:T(8,128)(2,1)S(1)} collective-permute-done((bf16[2,16,6528]{2,1,0:T(8,128)(2,1)S(1)}, bf16[2,16,6528]{2,1,0:T(8,128)(2,1)S(1)}, u32[]{:S(2)}, u32[]{:S(2)}) %collective-permute-start.26) | collective-permute-done | bytes 417824 | tf_op jit(solution)/shard_map/ppermute | solution.py:308
  240.8 1.8 collective-permute-start.27
  242.6 4.5 %tokens_grad.1 = f32[128,768]{1,0:T(8,128)} custom-call(bf16[128,768]{1,0:T(8,128)(2,1)} %x_ref.3, bf16[128,768]{1,0:T(8,128)(2,1)} %get-tuple-element.65.dq_ref, bf16[2,128,768]{2,1,0:T(8,128)(2,1)} %add_convert_fusion.12.dkv_ref, bf16[768,2304]{1,0:T(8,128)(2,1)} %get-tuple-element.67.w_ref, f32[1,768]{1,0:T(1,128)} %broadcast_select_fusion.1.gain_ref, ...), custom_call_target="tpu_custom_call" | custom-call | flops 452984832 | bytes 5000000 | tf_op jit(solution)/shard_map/tokens_grad/pallas_call | solution.py:514
  247.1 1.0 pad_maximum_fusion.3.ra.rb
  248.1 4.6 %finish_second.1 = (f32[192,2304]{1,0:T(8,128)}, f32[192,128]{1,0:T(8,128)}) custom-call(s32[3]{0:T(128)} %pad_add_fusion.svec, bf16[8,16,3456]{2,1,0:T(8,128)(2,1)} %pad_maximum_fusion.3.ra.rb, bf16[8,16,3456]{2,1,0:T(8,128)(2,1)} %pad_maximum_fusion.3.ra.rb, bf16[192,2304]{1,0:T(8,128)(2,1)} %w_ref.2), custom_call_target="tpu_custom_call" | custom-call | flops 1000000 | bytes 4000000 | tf_op jit(solution)/shard_map/finish_second/pallas_call | solution.py:557
  254.3 1.4 pad_maximum_fusion.ra.rb
  255.7 4.8 %finish_first.1 = (f32[192,2304]{1,0:T(8,128)}, f32[192,768]{1,0:T(8,128)}, f32[288,768]{1,0:T(8,128)}, f32[192,128]{1,0:T(8,128)}) custom-call(s32[3]{0:T(128)} %pad_add_fusion.svec, bf16[8,16,6528]{2,1,0:T(8,128)(2,1)} %pad_maximum_fusion.ra.rb, bf16[8,16,6528]{2,1,0:T(8,128)(2,1)} %pad_maximum_fusion.ra.rb, bf16[192,2304]{1,0:T(8,128)(2,1)} %w_ref.3), custom_call_target="tpu_custom_call" | custom-call | flops 1000000 | bytes 6000000 | tf_op jit(solution)/shard_map/finish_first/pallas_call | solution.py:533
  (99 shorter events, 19.8 us)
Async XLA Ops:
  0.6 6.1 %copy-start = (bf16[192,2304]{1,0:T(8,128)(2,1)S(1)}, bf16[192,2304]{1,0:T(8,128)(2,1)}, u32[]{:S(2)}) copy-start(bf16[192,2304]{1,0:T(8,128)(2,1)} %w_ref.3) | copy-start | bytes 2654212
  2.3 6.6 %copy-start.6 = (bf16[192,768]{1,0:T(8,128)(2,1)S(1)}, bf16[192,768]{1,0:T(8,128)(2,1)}, u32[]{:S(2)}) copy-start(bf16[192,768]{1,0:T(8,128)(2,1)} %param.16) | copy-start | bytes 884740
  2.3 7.3 %copy-start.5 = (bf16[288,768]{1,0:T(8,128)(2,1)S(1)}, bf16[288,768]{1,0:T(8,128)(2,1)}, u32[]{:S(2)}) copy-start(bf16[288,768]{1,0:T(8,128)(2,1)} %param.18) | copy-start | bytes 1327108
  3.6 34.9 %copy-start.4 = (bf16[208,2304]{1,0:T(8,128)(2,1)}, bf16[208,2304]{1,0:T(8,128)(2,1)S(1)}, u32[]{:S(2)}) copy-start(bf16[208,2304]{1,0:T(8,128)(2,1)S(1)} %pad_maximum_fusion.2.w0) | copy-start | bytes 2875396
  3.6 26.1 %copy-start.2 = (bf16[128,768]{1,0:T(8,128)(2,1)S(1)}, bf16[128,768]{1,0:T(8,128)(2,1)}, u32[]{:S(2)}) copy-start(bf16[128,768]{1,0:T(8,128)(2,1)} %x_ref.3) | copy-start | bytes 589828
  3.7 28.7 %copy-start.9 = (s32[8]{0:T(128)S(1)}, s32[8]{0:T(128)}, u32[]{:S(2)}) copy-start(s32[8]{0:T(128)} %constant.77.clone) | copy-start | bytes 100
  3.7 28.7 %copy-start.10 = (s32[8]{0:T(128)S(1)}, s32[8]{0:T(128)}, u32[]{:S(2)}) copy-start(s32[8]{0:T(128)} %constant.76.clone) | copy-start | bytes 100
  3.7 24.4 %collective-permute-start.4 = (bf16[208,2304]{1,0:T(8,128)(2,1)S(1)}, bf16[208,2304]{1,0:T(8,128)(2,1)}, u32[]{:S(2)}, u32[]{:S(2)}) collective-permute-start(bf16[208,2304]{1,0:T(8,128)(2,1)S(1)} %pad_maximum_fusion.2.w0), channel_id=1, source_target_pairs={{0,16},{1,17},{2,18},{3,19},{4,20},{5,21},{6,22},{7,23},{8,24},{9,... | collective-permute-start | bytes 2875400 | tf_op jit(solution)/shard_map/ppermute | solution.py:308
  28.0 37.0 %collective-permute-start.7 = (bf16[1056,768]{1,0:T(8,128)(2,1)}, bf16[1056,768]{1,0:T(8,128)(2,1)}, u32[]{:S(2)}, u32[]{:S(2)}) collective-permute-start(bf16[1056,768]{1,0:T(8,128)(2,1)} %constant_dynamic-update-slice_fusion.p0), channel_id=1, source_target_pairs={{0,16},{1,17},{2,18},{3,19},{4,20},{5,21},{6,22},{7,23},{8,24},{9,... | collective-permute-start | bytes 4866056 | tf_op jit(solution)/shard_map/ppermute | solution.py:308
  29.8 35.2 %collective-permute-start.3 = (bf16[208,2304]{1,0:T(8,128)(2,1)S(1)}, bf16[208,2304]{1,0:T(8,128)(2,1)}, u32[]{:S(2)}, u32[]{:S(2)}) collective-permute-start(bf16[208,2304]{1,0:T(8,128)(2,1)S(1)} %pad_maximum_fusion.2.w0), channel_id=1, source_target_pairs={{0,8},{1,9},{2,10},{3,11},{4,12},{5,13},{6,14},{7,15},{8,0},{9,1},... | collective-permute-start | bytes 2875400 | tf_op jit(solution)/shard_map/ppermute | solution.py:308
  29.8 8.7 %collective-permute-start = (bf16[128,768]{1,0:T(8,128)(2,1)S(1)}, bf16[128,768]{1,0:T(8,128)(2,1)S(1)}, u32[]{:S(2)}, u32[]{:S(2)}) collective-permute-start(bf16[128,768]{1,0:T(8,128)(2,1)S(1)} %copy-done.2), channel_id=1, source_target_pairs={{0,4},{1,5},{2,6},{3,7},{4,0},{5,1},{6,2},{7,3},{8,9},{9,8},{10,11... | collective-permute-start | bytes 589832 | tf_op jit(solution)/shard_map/ppermute | solution.py:308
  38.5 10.9 %collective-permute-start.1 = (bf16[256,768]{1,0:T(8,128)(2,1)S(1)}, bf16[256,768]{1,0:T(8,128)(2,1)S(1)}, u32[]{:S(2)}, u32[]{:S(2)}) collective-permute-start(bf16[256,768]{1,0:T(8,128)(2,1)S(1)} %pad_maximum_fusion.10), channel_id=1, source_target_pairs={{0,2},{1,3},{2,0},{3,1},{4,6},{5,7},{6,4},{7,5},{8,12},{9,13},{10,... | collective-permute-start | bytes 1179656 | tf_op jit(solution)/shard_map/ppermute | solution.py:308
  49.5 3.4 %copy-start.8 = (bf16[192]{0:T(256)(128)(2,1)S(1)}, bf16[192]{0:T(256)(128)(2,1)}, u32[]{:S(2)}) copy-start(bf16[192]{0:T(256)(128)(2,1)} %param.20) | copy-start | bytes 1156
  49.5 17.2 %collective-permute-start.2 = (bf16[512,768]{1,0:T(8,128)(2,1)S(1)}, bf16[512,768]{1,0:T(8,128)(2,1)}, u32[]{:S(2)}, u32[]{:S(2)}) collective-permute-start(bf16[512,768]{1,0:T(8,128)(2,1)S(1)} %pad_maximum_fusion.5), channel_id=1, source_target_pairs={{0,1},{1,0},{2,3},{3,2},{4,5},{5,4},{6,7},{7,6},{8,10},{9,11},{10,... | collective-permute-start | bytes 2359304 | tf_op jit(solution)/shard_map/ppermute | solution.py:308
  51.1 18.0 %collective-permute-start.5 = (bf16[208,2304]{1,0:T(8,128)(2,1)}, bf16[208,2304]{1,0:T(8,128)(2,1)}, u32[]{:S(2)}, u32[]{:S(2)}) collective-permute-start(bf16[208,2304]{1,0:T(8,128)(2,1)} %collective-permute-done.4.w2), channel_id=1, source_target_pairs={{0,8},{1,9},{2,10},{3,11},{4,12},{5,13},{6,14},{7,15},{8,0},{9,1},... | collective-permute-start | bytes 2875400 | tf_op jit(solution)/shard_map/ppermute | solution.py:308
  53.6 36.1 %collective-permute-start.6 = (bf16[1056,768]{1,0:T(8,128)(2,1)}, bf16[1056,768]{1,0:T(8,128)(2,1)S(1)}, u32[]{:S(2)}, u32[]{:S(2)}) collective-permute-start(bf16[1056,768]{1,0:T(8,128)(2,1)} %constant_dynamic-update-slice_fusion.p0), channel_id=1, source_target_pairs={{0,8},{1,9},{2,10},{3,11},{4,12},{5,13},{6,14},{7,15},{8,0},{9,1},... | collective-permute-start | bytes 4866056 | tf_op jit(solution)/shard_map/ppermute | solution.py:308
  65.0 24.7 %collective-permute-start.8 = (bf16[1056,768]{1,0:T(8,128)(2,1)}, bf16[1056,768]{1,0:T(8,128)(2,1)}, u32[]{:S(2)}, u32[]{:S(2)}) collective-permute-start(bf16[1056,768]{1,0:T(8,128)(2,1)} %collective-permute-done.7.p2), channel_id=1, source_target_pairs={{0,8},{1,9},{2,10},{3,11},{4,12},{5,13},{6,14},{7,15},{8,0},{9,1},... | collective-permute-start | bytes 4866056 | tf_op jit(solution)/shard_map/ppermute | solution.py:308
  89.7 1.2 copy-start.11
  103.5 38.3 %collective-permute-start.20 = (bf16[16,16,6528]{2,1,0:T(8,128)(2,1)}, bf16[16,16,6528]{2,1,0:T(8,128)(2,1)S(1)}, u32[]{:S(2)}, u32[]{:S(2)}) collective-permute-start(bf16[16,16,6528]{2,1,0:T(8,128)(2,1)} %get-tuple-element.74), channel_id=1, source_target_pairs={{0,8},{1,9},{2,10},{3,11},{4,12},{5,13},{6,14},{7,15},{8,0},{9,1},... | collective-permute-start | bytes 10027016 | tf_op jit(solution)/shard_map/ppermute | solution.py:308
  115.2 20.6 %collective-permute-start.9 = (bf16[2,512,768]{2,1,0:T(8,128)(2,1)S(1)}, bf16[2,512,768]{2,1,0:T(8,128)(2,1)}, u32[]{:S(2)}, u32[]{:S(2)}) collective-permute-start(bf16[2,512,768]{2,1,0:T(8,128)(2,1)S(1)} %slice.200), channel_id=1, source_target_pairs={{0,1},{1,0},{2,3},{3,2},{4,5},{5,4},{6,7},{7,6},{8,10},{9,11},{10,... | collective-permute-start | bytes 4718600 | tf_op jit(solution)/shard_map/ppermute | solution.py:308
  124.6 15.2 %collective-permute-start.12 = (bf16[16,16,3456]{2,1,0:T(8,128)(2,1)}, bf16[16,16,3456]{2,1,0:T(8,128)(2,1)S(1)}, u32[]{:S(2)}, u32[]{:S(2)}) collective-permute-start(bf16[16,16,3456]{2,1,0:T(8,128)(2,1)} %get-tuple-element.71), channel_id=1, source_target_pairs={{0,8},{1,9},{2,10},{3,11},{4,12},{5,13},{6,14},{7,15},{8,0},{9,1},... | collective-permute-start | bytes 5308424 | tf_op jit(solution)/shard_map/ppermute | solution.py:308
  135.8 4.0 %copy-start.3 = (bf16[16,16,3456]{2,1,0:T(8,128)(2,1)S(1)}, bf16[16,16,3456]{2,1,0:T(8,128)(2,1)}, u32[]{:S(2)}) copy-start(bf16[16,16,3456]{2,1,0:T(8,128)(2,1)} %get-tuple-element.70) | copy-start | bytes 5308420
  138.2 27.2 %collective-permute-start.10 = (bf16[2,256,768]{2,1,0:T(8,128)(2,1)S(1)}, bf16[2,256,768]{2,1,0:T(8,128)(2,1)S(1)}, u32[]{:S(2)}, u32[]{:S(2)}) collective-permute-start(bf16[2,256,768]{2,1,0:T(8,128)(2,1)S(1)} %slice.247), channel_id=1, source_target_pairs={{0,2},{1,3},{2,0},{3,1},{4,6},{5,7},{6,4},{7,5},{8,12},{9,13},{10,... | collective-permute-start | bytes 2359304 | tf_op jit(solution)/shard_map/ppermute | solution.py:308
  139.8 2.0 copy-start.1
  140.2 28.7 %collective-permute-start.13 = (bf16[8,16,3456]{2,1,0:T(8,128)(2,1)S(1)}, bf16[8,16,3456]{2,1,0:T(8,128)(2,1)S(1)}, u32[]{:S(2)}, u32[]{:S(2)}) collective-permute-start(bf16[8,16,3456]{2,1,0:T(8,128)(2,1)S(1)} %get-tuple-element.83), channel_id=1, source_target_pairs={{0,16},{1,17},{2,18},{3,19},{4,20},{5,21},{6,22},{7,23},{8,10},{9,... | collective-permute-start | bytes 2654216 | tf_op jit(solution)/shard_map/ppermute | solution.py:308
  142.7 36.7 %collective-permute-start.21 = (bf16[8,16,6528]{2,1,0:T(8,128)(2,1)S(1)}, bf16[8,16,6528]{2,1,0:T(8,128)(2,1)S(1)}, u32[]{:S(2)}, u32[]{:S(2)}) collective-permute-start(bf16[8,16,6528]{2,1,0:T(8,128)(2,1)S(1)} %get-tuple-element.81), channel_id=1, source_target_pairs={{0,16},{1,17},{2,18},{3,19},{4,20},{5,21},{6,22},{7,23},{8,10},{9,... | collective-permute-start | bytes 5013512 | tf_op jit(solution)/shard_map/ppermute | solution.py:308
  165.7 12.8 %collective-permute-start.11 = (bf16[2,128,768]{2,1,0:T(8,128)(2,1)S(1)}, bf16[2,128,768]{2,1,0:T(8,128)(2,1)S(1)}, u32[]{:S(2)}, u32[]{:S(2)}) collective-permute-start(bf16[2,128,768]{2,1,0:T(8,128)(2,1)S(1)} %slice.249), channel_id=1, source_target_pairs={{0,4},{1,5},{2,6},{3,7},{4,0},{5,1},{6,2},{7,3},{8,9},{9,8},{10,11... | collective-permute-start | bytes 1179656 | tf_op jit(solution)/shard_map/ppermute | solution.py:308
  169.1 12.2 %collective-permute-start.14 = (bf16[4,16,3456]{2,1,0:T(8,128)(2,1)S(1)}, bf16[4,16,3456]{2,1,0:T(8,128)(2,1)S(1)}, u32[]{:S(2)}, u32[]{:S(2)}) collective-permute-start(bf16[4,16,3456]{2,1,0:T(8,128)(2,1)S(1)} %get-tuple-element.87), channel_id=1, source_target_pairs={{0,1},{1,0},{2,3},{3,2},{4,5},{5,4},{6,7},{7,6},{8,24},{9,25},{10,... | collective-permute-start | bytes 1327112 | tf_op jit(solution)/shard_map/ppermute | solution.py:308
  179.7 12.6 %collective-permute-start.22 = (bf16[4,16,6528]{2,1,0:T(8,128)(2,1)S(1)}, bf16[4,16,6528]{2,1,0:T(8,128)(2,1)S(1)}, u32[]{:S(2)}, u32[]{:S(2)}) collective-permute-start(bf16[4,16,6528]{2,1,0:T(8,128)(2,1)S(1)} %get-tuple-element.85), channel_id=1, source_target_pairs={{0,1},{1,0},{2,3},{3,2},{4,5},{5,4},{6,7},{7,6},{8,24},{9,25},{10,... | collective-permute-start | bytes 2506760 | tf_op jit(solution)/shard_map/ppermute | solution.py:308
  181.4 14.1 %collective-permute-start.15 = (bf16[2,16,3456]{2,1,0:T(8,128)(2,1)S(1)}, bf16[2,16,3456]{2,1,0:T(8,128)(2,1)S(1)}, u32[]{:S(2)}, u32[]{:S(2)}) collective-permute-start(bf16[2,16,3456]{2,1,0:T(8,128)(2,1)S(1)} %get-tuple-element.97), channel_id=1, source_target_pairs={{0,2},{1,3},{2,0},{3,1},{4,6},{5,7},{6,4},{7,5},{8,12},{9,13},{10,... | collective-permute-start | bytes 663560 | tf_op jit(solution)/shard_map/ppermute | solution.py:308
  192.5 12.6 %collective-permute-start.23 = (bf16[2,16,6528]{2,1,0:T(8,128)(2,1)S(1)}, bf16[2,16,6528]{2,1,0:T(8,128)(2,1)S(1)}, u32[]{:S(2)}, u32[]{:S(2)}) collective-permute-start(bf16[2,16,6528]{2,1,0:T(8,128)(2,1)S(1)} %get-tuple-element.89), channel_id=1, source_target_pairs={{0,2},{1,3},{2,0},{3,1},{4,6},{5,7},{6,4},{7,5},{8,12},{9,13},{10,... | collective-permute-start | bytes 1253384 | tf_op jit(solution)/shard_map/ppermute | solution.py:308
  195.6 11.6 %collective-permute-start.16 = (bf16[1,16,3456]{2,1,0:T(8,128)(2,1)S(1)}, bf16[1,16,3456]{2,1,0:T(8,128)(2,1)S(1)}, u32[]{:S(2)}, u32[]{:S(2)}) collective-permute-start(bf16[1,16,3456]{2,1,0:T(8,128)(2,1)S(1)} %add_convert_fusion.19), channel_id=1, source_target_pairs={{0,4},{1,5},{2,6},{3,7},{4,0},{5,1},{6,2},{7,3},{8,9},{9,8},{10,11... | collective-permute-start | bytes 331784 | tf_op jit(solution)/shard_map/ppermute | solution.py:308
  205.2 15.9 %collective-permute-start.24 = (bf16[1,16,6528]{2,1,0:T(8,128)(2,1)S(1)}, bf16[1,16,6528]{2,1,0:T(8,128)(2,1)S(1)}, u32[]{:S(2)}, u32[]{:S(2)}) collective-permute-start(bf16[1,16,6528]{2,1,0:T(8,128)(2,1)S(1)} %add_convert_fusion.16), channel_id=1, source_target_pairs={{0,4},{1,5},{2,6},{3,7},{4,0},{5,1},{6,2},{7,3},{8,9},{9,8},{10,11... | collective-permute-start | bytes 626696 | tf_op jit(solution)/shard_map/ppermute | solution.py:308
  207.2 16.2 %collective-permute-start.17 = (bf16[1,16,3456]{2,1,0:T(8,128)(2,1)S(1)}, bf16[1,16,3456]{2,1,0:T(8,128)(2,1)S(1)}, u32[]{:S(2)}, u32[]{:S(2)}) collective-permute-start(bf16[1,16,3456]{2,1,0:T(8,128)(2,1)S(1)} %add_convert_fusion.18), channel_id=1, source_target_pairs={{0,4},{1,5},{2,6},{3,7},{4,0},{5,1},{6,2},{7,3},{8,9},{9,8},{10,11... | collective-permute-start | bytes 331784 | tf_op jit(solution)/shard_map/ppermute | solution.py:308
  221.1 7.8 %collective-permute-start.25 = (bf16[1,16,6528]{2,1,0:T(8,128)(2,1)S(1)}, bf16[1,16,6528]{2,1,0:T(8,128)(2,1)S(1)}, u32[]{:S(2)}, u32[]{:S(2)}) collective-permute-start(bf16[1,16,6528]{2,1,0:T(8,128)(2,1)S(1)} %add_convert_fusion.15), channel_id=1, source_target_pairs={{0,4},{1,5},{2,6},{3,7},{4,0},{5,1},{6,2},{7,3},{8,9},{9,8},{10,11... | collective-permute-start | bytes 626696 | tf_op jit(solution)/shard_map/ppermute | solution.py:308
  223.5 7.8 %collective-permute-start.18 = (bf16[2,16,3456]{2,1,0:T(8,128)(2,1)S(1)}, bf16[2,16,3456]{2,1,0:T(8,128)(2,1)S(1)}, u32[]{:S(2)}, u32[]{:S(2)}) collective-permute-start(bf16[2,16,3456]{2,1,0:T(8,128)(2,1)S(1)} %pad_maximum_fusion.11), channel_id=1, source_target_pairs={{0,2},{1,3},{2,0},{3,1},{4,6},{5,7},{6,4},{7,5},{8,12},{9,13},{10,... | collective-permute-start | bytes 663560 | tf_op jit(solution)/shard_map/ppermute | solution.py:308
  229.0 11.6 %collective-permute-start.26 = (bf16[2,16,6528]{2,1,0:T(8,128)(2,1)S(1)}, bf16[2,16,6528]{2,1,0:T(8,128)(2,1)S(1)}, u32[]{:S(2)}, u32[]{:S(2)}) collective-permute-start(bf16[2,16,6528]{2,1,0:T(8,128)(2,1)S(1)} %pad_maximum_fusion.9), channel_id=1, source_target_pairs={{0,2},{1,3},{2,0},{3,1},{4,6},{5,7},{6,4},{7,5},{8,12},{9,13},{10,... | collective-permute-start | bytes 1253384 | tf_op jit(solution)/shard_map/ppermute | solution.py:308
  231.3 15.8 %collective-permute-start.19 = (bf16[4,16,3456]{2,1,0:T(8,128)(2,1)S(1)}, bf16[4,16,3456]{2,1,0:T(8,128)(2,1)S(1)}, u32[]{:S(2)}, u32[]{:S(2)}) collective-permute-start(bf16[4,16,3456]{2,1,0:T(8,128)(2,1)S(1)} %pad_maximum_fusion.8), channel_id=1, source_target_pairs={{0,1},{1,0},{2,3},{3,2},{4,5},{5,4},{6,7},{7,6},{8,10},{9,11},{10,... | collective-permute-start | bytes 1327112 | tf_op jit(solution)/shard_map/ppermute | solution.py:308
  240.8 13.5 %collective-permute-start.27 = (bf16[4,16,6528]{2,1,0:T(8,128)(2,1)S(1)}, bf16[4,16,6528]{2,1,0:T(8,128)(2,1)S(1)}, u32[]{:S(2)}, u32[]{:S(2)}) collective-permute-start(bf16[4,16,6528]{2,1,0:T(8,128)(2,1)S(1)} %pad_maximum_fusion.4), channel_id=1, source_target_pairs={{0,1},{1,0},{2,3},{3,2},{4,5},{5,4},{6,7},{7,6},{8,10},{9,11},{10,... | collective-permute-start | bytes 2506760 | tf_op jit(solution)/shard_map/ppermute | solution.py:308
  248.1 5.6 %copy-start.7 = (bf16[192]{0:T(256)(128)(2,1)S(1)}, bf16[192]{0:T(256)(128)(2,1)}, u32[]{:S(2)}) copy-start(bf16[192]{0:T(256)(128)(2,1)} %param.19) | copy-start | bytes 1156

commit v2 on v1

v2 whole, which is shorter than its diff:
```python
import functools
import math

import jax
import jax.numpy as jnp
import numpy as np
from jax import lax
from jax.experimental import pallas as pl
from jax.experimental.pallas import tpu as pltpu
from jax.sharding import PartitionSpec as P

HEADS = 12
HEAD_DIM = 64
THETA = 160000.0
EPS = 1e-05
CHUNK_BITS = 3
CHUNKS = 1 << CHUNK_BITS
BF = jnp.bfloat16
F32 = jnp.float32
COSTS = {
    "pack_up": 0.5,
    "qkv_near": 0.5,
    "qkv_far": 0.5,
    "attend": 0.5,
    "middle": 0.5,
    "middle_grad": 0.5,
    "every_query": 0.5,
    "attend_back": 0.5,
    "qkv_grad": 0.5,
    "attend_keys": 0.5,
    "tokens_grad": 0.5,
    "finish_first": 0.5,
    "finish_second": 0.5,
}
FIRST_WALKS = ((0, 1, 2), (1, 0, 2))
SECOND_WALKS = (("y", 0, 1, 2), (1, "y", 0, 2))
VMEM_LIMIT = 58 * 1024 * 1024


def whole(shape):
    return pl.BlockSpec(shape, lambda *_: (0,) * len(shape))


def params(limit=VMEM_LIMIT):
    return pltpu.CompilerParams(vmem_limit_bytes=limit)


def cost(micros):
    return pl.CostEstimate(flops=int(micros * 1.15e9), bytes_accessed=0, transcendentals=0)


def dot(left, right, dims=((1,), (0,))):
    return lax.dot_general(left, right, (dims, ((), ())), preferred_element_type=F32)


NT = ((1,), (1,))
TN = ((0,), (0,))


def normalise(values):
    center = values - jnp.mean(values, axis=-1, keepdims=True)
    spread = jnp.mean(center * center, axis=-1, keepdims=True)
    scale = lax.rsqrt(spread + EPS)
    return center * scale, scale


def norm_back(grad, xhat, scale, gain):
    inner = grad * gain
    return scale * (
        inner
        - jnp.mean(inner, axis=-1, keepdims=True)
        - xhat * jnp.mean(inner * xhat, axis=-1, keepdims=True)
    )


def swap_halves(values):
    lane = lax.broadcasted_iota(jnp.int32, values.shape, 1)
    return jnp.where(lane % 64 < 32, pltpu.roll(values, 96, 1), pltpu.roll(values, 32, 1))


def rotate(values, cos, sin):
    return values * cos + swap_halves(values) * sin


def rotate_back(values, cos, sin):
    return values * cos - swap_halves(values) * sin


def fold(pieces):
    rows = [p[8 * i : 8 * i + 8] for p in pieces for i in range(p.shape[0] // 8)]
    flat = jnp.concatenate(rows, axis=1)
    half = flat.shape[1] // 2
    return jnp.concatenate([flat[:, :half], flat[:, half:]], axis=0)


def unfold(block, shapes):
    flat = jnp.concatenate([block[:8], block[8:]], axis=1)
    out, at = [], 0
    for rows, cols in shapes:
        parts = []
        for _ in range(rows // 8):
            parts.append(flat[:, at : at + cols])
            at += cols
        out.append(jnp.concatenate(parts, axis=0))
    return out


def chunk_at(svec, keep, spot):
    found = []
    for walk in SECOND_WALKS:
        low = CHUNK_BITS - walk.index("y")
        rel = ((spot >> (low + 1)) << low) | (spot & ((1 << low) - 1))
        found.append(((spot >> low) & 1, rel))
    core = (svec[0] & 1) ^ keep
    upper = jnp.where(core == 0, found[0][0], found[1][0])
    return upper, jnp.where(core == 0, found[0][1], found[1][1]) ^ svec[3 + keep]


def spread(svec, pieces, half, begins, to_ref, to_cols):
    for j, parts in enumerate(pieces):
        halved = len(parts) == 3
        for h in range(2):
            to = (svec[0] ^ j) * (2 * half) + (svec[1] ^ h if halved else h) * half
            at = begins[1] if halved else begins[0] + h * half
            part = parts[h if halved else 0]
            to_ref[pl.ds(pl.multiple_of(to, 16), half), to_cols] = part[at : at + half, parts[-1]]


def pack_up_kernel(svec, in_ref, w_ref, out_ref):
    half, width = w_ref.shape
    for b in range(3):
        out_ref[b * half : (b + 1) * half, :] = in_ref[:, b * width : (b + 1) * width]
    out_ref[3 * half :, :] = w_ref[...]


def project(x_ref, gain, cos_ref, sin_ref, w_ref, n_ref, k_ref, v_ref):
    width = n_ref.shape[1]
    xhat, _ = normalise(x_ref[...].astype(F32))
    normed = (xhat * gain).astype(BF)
    n_ref[...] = normed
    cos, sin = cos_ref[...], sin_ref[...]
    keys = dot(normed, w_ref[:, width : 2 * width])
    for g in range(width // 128):
        cut = slice(128 * g, 128 * g + 128)
        k_ref[:, cut] = rotate(keys[:, cut], cos, sin).astype(BF)
    v_ref[...] = dot(normed, w_ref[:, 2 * width :]).astype(BF)
    return normed, cos, sin


def qkv_near_kernel(
    svec, x_ref, w0, w1, w2, w3, g0_ref, g1_ref, g2_ref, g3_ref, cos_ref, sin_ref,
    n_ref, q_ref, k_ref, v_ref, w_ref, gain_ref, *, own,
):
    rows = w_ref.shape[0] // 4
    width = n_ref.shape[1]
    first = pl.program_id(0) == 0

    @pl.when(first)
    def _():
        for j, piece in enumerate((w0, w1, w2, w3)):
            w_ref[pl.ds(pl.multiple_of((svec[0] ^ j) * rows, 16), rows), :] = piece[...]
        g = [r[:, :rows] for r in (g0_ref, g1_ref, g2_ref, g3_ref)]
        core, upper = svec[0] & 1, svec[0] >> 1
        near = jnp.where(core == 0, jnp.concatenate([g[0], g[1]], axis=1), jnp.concatenate([g[1], g[0]], axis=1))
        far = jnp.where(core == 0, jnp.concatenate([g[2], g[3]], axis=1), jnp.concatenate([g[3], g[2]], axis=1))
        full = jnp.where(upper == 0, jnp.concatenate([near, far], axis=1), jnp.concatenate([far, near], axis=1))
        gain_ref[...] = full

    normed, cos, sin = project(x_ref, gain_ref[0:1, :], cos_ref, sin_ref, w_ref, n_ref, k_ref, v_ref)

    @pl.when(first)
    def _():
        queries = dot(normed[:own], w_ref[:, :width])
        for g in range(width // 128):
            cut = slice(128 * g, 128 * g + 128)
            q_ref[:, cut] = rotate(queries[:, cut], cos[:own], sin[:own]).astype(BF)


def qkv_far_kernel(x_ref, w_ref, gain_ref, cos_ref, sin_ref, n_ref, k_ref, v_ref):
    project(x_ref, gain_ref[0:1, :], cos_ref, sin_ref, w_ref, n_ref, k_ref, v_ref)


def both_halves(near_ref, far_ref):
    return jnp.concatenate([near_ref[...], far_ref[...]], axis=0)


def queries_kernel(near_ref, far_ref, w_ref, cos_ref, sin_ref, q_ref):
    there = pl.program_id(0) >= pl.num_programs(0) // 2
    queries = dot(jnp.where(there, far_ref[...], near_ref[...]), w_ref[...])
    cos, sin = cos_ref[...], sin_ref[...]
    for g in range(queries.shape[1] // 128):
        cut = slice(128 * g, 128 * g + 128)
        q_ref[:, cut] = rotate(queries[:, cut], cos, sin).astype(BF)


def head_mask(shape, head):
    return lax.broadcasted_iota(jnp.int32, shape, 1) // HEAD_DIM == head


def fold_scale(q, head):
    return jnp.where(head_mask(q.shape, head), q, jnp.zeros_like(q)) * jnp.asarray(HEAD_DIM**-0.5, BF)


def attend_kernel(q_ref, kn_ref, kf_ref, vn_ref, vf_ref, o_ref, lse_ref):
    q, k, v = q_ref[...], both_halves(kn_ref, kf_ref), both_halves(vn_ref, vf_ref)
    for h in range(2):
        scores = dot(k, fold_scale(q, h), NT)
        top = jnp.max(scores, axis=0, keepdims=True)
        weights = jnp.exp(scores - top)
        total = jnp.sum(weights, axis=0, keepdims=True)
        out = dot(v, weights.astype(BF), TN)
        cut = slice(HEAD_DIM * h, HEAD_DIM * h + HEAD_DIM)
        o_ref[cut, :] = out[cut, :] / total
        lse_ref[0, h : h + 1, :] = top + jnp.log(total)


def middle_kernel(
    svec, x_ref, at_ref, lse_ref, i0, i1, o0, o1, af, as_, acf, acs, b0, b1, b2, b3, dy_ref, gains_ref,
    lo_ref, dm_ref, pay_ref, dat_ref, mine_ref, core_ref, y_ref,
    win, wout, wdown, n2t, attnt, hidt,
):
    width = x_ref.shape[1]
    own = x_ref.shape[0]
    half = width // 8
    ff = wdown.shape[0]
    frows = ff // 4
    every = slice(None)
    for b in range(3):
        cut = slice(b * width, (b + 1) * width)
        spread(svec, ((i0, cut), (i1, cut), (af, as_, every), (acf, acs, every)), half, (0, b * half), win, cut)
    spread(svec, ((o0, every), (o1, every), (af, as_, every), (acf, acs, every)), half, (0, 3 * half), wout, every)
    for j, piece in enumerate((b0, b1, b2, b3)):
        wdown[pl.ds(pl.multiple_of((svec[0] ^ j) * frows, 16), frows), :] = piece[...]

    gain = gains_ref[1:2, :]
    attn_t = at_ref[...]
    attnt[...] = attn_t.astype(BF)
    attn_low = jnp.transpose(attn_t).astype(BF)
    mid = x_ref[...].astype(F32) + dot(attn_low, wout[...])
    xhat, scale = normalise(mid)
    normed = xhat * gain
    n2t[...] = jnp.transpose(normed).astype(BF)
    up = dot(normed.astype(BF), win[...])
    gate, lin = up[:, :ff], up[:, ff:]
    cdf = 0.5 * (1.0 + lax.erf(gate * (2.0**-0.5)))
    act = gate * cdf
    hidden = act * lin
    hidt[...] = jnp.transpose(hidden).astype(BF)
    lo_ref[...] = (mid + dot(hidden.astype(BF), wdown[...])).astype(BF)
    dy = dy_ref[...]
    d_hidden = dot(dy, wdown[...], NT)
    pdf = jnp.exp(-0.5 * gate * gate) * (1.0 / math.sqrt(2.0 * math.pi))
    d_gate = (d_hidden * lin * (cdf + gate * pdf)).astype(BF)
    d_lin = (d_hidden * act).astype(BF)
    d_up = jnp.concatenate([d_gate, d_lin], axis=1)
    d_mid = dy.astype(F32) + norm_back(dot(d_up, win[...], NT), xhat, scale, gain)
    dm_ref[...] = d_mid
    d_branch = d_mid.astype(BF)
    rows = width // 4
    part = 2 * rows + frows
    for j, (to_ref, begin) in enumerate(((mine_ref, 0), (core_ref, 0), (y_ref, 0), (y_ref, part))):
        q = svec[0] ^ j
        at = pl.multiple_of(q * rows, 16)
        to_ref[begin : begin + rows, :] = n2t[pl.ds(at, rows), :]
        to_ref[begin + rows : begin + 2 * rows, :] = attnt[pl.ds(at, rows), :]
        to_ref[begin + 2 * rows : begin + part, :] = hidt[pl.ds(pl.multiple_of(q * frows, 16), frows), :]
    d_all = jnp.concatenate([d_up, d_branch, dy], axis=1)
    for b in range(5 * width // 128):
        piece = d_all[:, 128 * b : 128 * b + 128]
        for to_ref, begin in ((core_ref, part), (y_ref, 2 * part)):
            to_ref[begin + b * own : begin + (b + 1) * own, :] = piece
    pay_ref[0, :own, :] = dot(d_branch, wout[...], NT).astype(BF)
    d_attn_t = dot(wout[...], d_branch, NT).astype(BF)
    dat_ref[...] = d_attn_t
    prod = d_attn_t.astype(F32) * attn_t
    for g in range(width // 128):
        stats = []
        for h in range(2):
            begin = 128 * g + HEAD_DIM * h
            delta = jnp.sum(prod[begin : begin + HEAD_DIM, :], axis=0, keepdims=True)
            for row in (lse_ref[g, h : h + 1, :], delta):
                high = row.astype(BF).astype(F32)
                stats += [high, row - high]
        stats = jnp.concatenate(stats + [jnp.zeros((8, own), F32)], axis=0)
        pay_ref[0, own:, 128 * g : 128 * g + 128] = stats.astype(BF)


def middle_grad_kernel(
    svec, mine_ref, core_ref, c_ref, y_ref, cy_ref,
    low_ref, high_ref, left, right, g_in, g_out, g_down,
):
    part = mine_ref.shape[0]
    own = mine_ref.shape[1]
    width = right.shape[1] // 5
    rows = width // 4
    frows = part - 2 * rows
    step, fstep = rows // CHUNKS, frows // CHUNKS
    sources = ((mine_ref, 0, core_ref, part), (c_ref, 0, c_ref, part), (y_ref, 0, y_ref, 2 * part), (cy_ref, part, cy_ref, 2 * part))
    for i, (x_ref, x_at, d_ref, d_at) in enumerate(sources):
        left[:, i * own : (i + 1) * own] = x_ref[x_at : x_at + part, :]
        for b in range(5 * width // 128):
            right[i * own : (i + 1) * own, 128 * b : 128 * b + 128] = d_ref[d_at + b * own : d_at + (b + 1) * own, :]
    g_in[...] = dot(left[:rows, :], right[:, : 3 * width])
    g_out[...] = dot(left[rows : 2 * rows, :], right[:, 3 * width : 4 * width])
    g_down[...] = dot(left[2 * rows :, :], right[:, 4 * width :])
    for spot in reversed(range(CHUNKS)):
        c = spot ^ svec[2]
        at = pl.multiple_of(c * step, 8)
        fat = pl.multiple_of(2 * fstep * (c >> 1) + (fstep - 4) * (c & 1), 8)
        parts = [g_in[pl.ds(at, step), :], g_out[pl.ds(at, step), :], g_down[pl.ds(fat, fstep + 4), :]]
        target = high_ref if spot >= CHUNKS // 2 else low_ref
        target[spot % (CHUNKS // 2)] = fold(parts).astype(BF)


def attend_back_kernel(q_ref, kn_ref, kf_ref, vn_ref, vf_ref, da_ref, dat_ref, at_ref, lse_ref, cos_ref, sin_ref, dq_ref, dkv_ref):
    q, k, v = q_ref[...], both_halves(kn_ref, kf_ref), both_halves(vn_ref, vf_ref)
    own = q.shape[0]
    da = da_ref[0, :own, :]
    prod = dat_ref[...].astype(F32) * at_ref[...]
    d_key, d_value, d_query = 0.0, 0.0, []
    for h in range(2):
        cut = slice(HEAD_DIM * h, HEAD_DIM * h + HEAD_DIM)
        q_scaled = fold_scale(q, h)
        da_head = jnp.where(head_mask(da.shape, h), da, jnp.zeros_like(da))
        probs = jnp.exp(dot(k, q_scaled, NT) - lse_ref[0, h : h + 1, :])
        delta = jnp.sum(prod[cut, :], axis=0, keepdims=True)
        d_scores = (probs * (dot(v, da_head, NT) - delta)).astype(BF)
        d_value += dot(probs.astype(BF), da_head)
        d_key += dot(d_scores, q_scaled)
        d_query.append(dot(d_scores, k, TN))
    dkv_ref[0] = rotate_back(d_key, cos_ref[...], sin_ref[...]).astype(BF)
    dkv_ref[1] = d_value.astype(BF)
    d_q = jnp.where(head_mask(q.shape, 0), d_query[0], d_query[1]) * (HEAD_DIM**-0.5)
    dq_ref[...] = rotate_back(d_q, cos_ref[:own, :], sin_ref[:own, :]).astype(BF)


def attend_keys_kernel(q_ref, k_ref, v_ref, near_ref, far_ref, cos_ref, sin_ref, dk_ref, dv_ref):
    k, v, q = k_ref[...], v_ref[...], q_ref[...]
    own = k.shape[0]
    both = [(r, i) for r in (near_ref, far_ref) for i in range(near_ref.shape[0])]
    da = jnp.concatenate([r[i, :own, :] for r, i in both], axis=0)
    stats = jnp.concatenate([r[i, own:, :].astype(F32) for r, i in both], axis=1)
    d_key, d_value = [], []
    for h in range(2):
        lse = stats[4 * h : 4 * h + 1] + stats[4 * h + 1 : 4 * h + 2]
        delta = stats[4 * h + 2 : 4 * h + 3] + stats[4 * h + 3 : 4 * h + 4]
        v_head = jnp.where(head_mask(v.shape, h), v, jnp.zeros_like(v))
        probs = jnp.exp(dot(fold_scale(k, h), q, NT) - lse)
        d_scores = (probs * (dot(v_head, da, NT) - delta)).astype(BF)
        d_value.append(dot(probs.astype(BF), da))
        d_key.append(dot(d_scores, q))
    first = head_mask(k.shape, 0)
    d_k = jnp.where(first, d_key[0], d_key[1]) * (HEAD_DIM**-0.5)
    dk_ref[...] = rotate_back(d_k, cos_ref[...], sin_ref[...]).astype(BF)
    dv_ref[...] = jnp.where(first, d_value[0], d_value[1]).astype(BF)


def qkv_grad_kernel(svec, near_ref, far_ref, dkv_ref, dq_ref, keep_low, keep_high, send_low, send_high, acc):
    width = near_ref.shape[1]
    rows = width // 4
    step = rows // CHUNKS
    own = dq_ref.shape[0]
    at = pl.program_id(0)
    normed = jnp.where(at >= pl.num_programs(0) // 2, far_ref[...], near_ref[...])
    first = at == 0

    @pl.when(first)
    def _():
        acc[:, :width] = dot(normed[:own], dq_ref[...], TN)
        for b in range(2):
            acc[:, (b + 1) * width : (b + 2) * width] = dot(normed, dkv_ref[b], TN)

    @pl.when(jnp.logical_not(first))
    def _():
        for b in range(2):
            acc[:, (b + 1) * width : (b + 2) * width] += dot(normed, dkv_ref[b], TN)

    @pl.when(pl.program_id(0) == pl.num_programs(0) - 1)
    def _():
        for keep, low_ref, high_ref in ((1, send_low, send_high), (0, keep_low, keep_high)):
            for spot in range(2 * CHUNKS):
                u, c = chunk_at(svec, keep, spot)
                at = pl.multiple_of((svec[0] ^ (2 * u + keep)) * rows + c * step, 8)
                target = high_ref if spot >= CHUNKS else low_ref
                target[spot % CHUNKS] = fold([acc[pl.ds(at, step), :]]).astype(BF)


def tokens_grad_kernel(x_ref, dq_ref, dk_ref, dv_ref, w_ref, gains_ref, dm_ref, out_ref):
    d_proj = jnp.concatenate([dq_ref[...], dk_ref[...], dv_ref[...]], axis=1)
    d_normed = dot(d_proj, w_ref[...], NT)
    xhat, scale = normalise(x_ref[...].astype(F32))
    out_ref[...] = dm_ref[...] + norm_back(d_normed, xhat, scale, gains_ref[0:1, :])


def chunk_of(mark, keep_ref, recv_ref, chunk):
    there = (chunk ^ mark) >= CHUNKS // 2
    return jnp.where(there, recv_ref[0].astype(F32), keep_ref[0].astype(F32))


def gain_rows(product, gain, gain_ref):
    at, rows, cols = pl.program_id(0), product.shape[0], gain_ref.shape[1]
    total = jnp.sum(product, axis=1, keepdims=True)
    row = lax.broadcasted_iota(jnp.int32, (rows, cols), 0)
    col = lax.broadcasted_iota(jnp.int32, (rows, cols), 1)
    part = jnp.sum(jnp.where(col == row + at * rows, total, 0.0), axis=0, keepdims=True) / gain

    @pl.when(at == 0)
    def _():
        gain_ref[...] = part

    @pl.when(at > 0)
    def _():
        gain_ref[...] += part


def finish_first_kernel(svec, ka, ra, kb, rb, w_ref, own_gain, in_ref, out_ref, down_ref, gain_ref, *, step, fstep, width):
    shapes = ((step, 3 * width), (step, width), (fstep + 4, width))
    at = 2 * pl.program_id(0)
    parts_a = unfold(chunk_of(svec[2], ka, ra, at), shapes)
    parts_b = unfold(chunk_of(svec[2], kb, rb, at + 1), shapes)
    both = [jnp.concatenate([a, b], axis=0) for a, b in zip(parts_a[:2], parts_b[:2])]
    in_ref[...] = both[0]
    out_ref[...] = both[1]
    down_ref[...] = jnp.concatenate([parts_a[2], parts_b[2][8:]], axis=0)
    gain_rows(w_ref[...].astype(F32) * both[0], own_gain[1:2, :], gain_ref)


def finish_second_kernel(svec, ka, ra, kb, rb, w_ref, own_gain, out_ref, gain_ref, *, step, width):
    shapes = ((step, 3 * width),)
    at = 2 * pl.program_id(0)
    chunks = [chunk_of(svec[3], ka, ra, at), chunk_of(svec[3], kb, rb, at + 1)]
    grad = jnp.concatenate([unfold(c, shapes)[0] for c in chunks], axis=0)
    out_ref[...] = grad
    gain_rows(w_ref[...].astype(F32) * grad, own_gain[0:1, :], gain_ref)


class Links:
    def __init__(self, n_dp, n_ctx):
        self.n_dp, self.n_ctx = n_dp, n_ctx
        self.bits = n_ctx.bit_length() - 1
        rise = list(range(self.bits))
        self.orders = (rise, rise[1:] + rise[:1])

    def swap(self, value, dims):
        pairs = []
        for d in range(self.n_dp):
            dim = dims[d & 1]
            for c in range(self.n_ctx):
                if dim == "core":
                    to = (d ^ 1, c)
                elif dim == "y":
                    to = (d ^ 2, c)
                else:
                    to = (d, c ^ (1 << dim))
                pairs.append((d * self.n_ctx + c, to[0] * self.n_ctx + to[1]))
        return lax.ppermute(value, ("dp", "ctx"), pairs)

    def both(self, step):
        return (self.orders[0][step], self.orders[1][step])


def add_low(left, right):
    return (left.astype(F32) + right.astype(F32)).astype(BF)


def after(value, *others):
    return lax.optimization_barrier((value,) + others)[0]


class Chain:
    def __init__(self, links, walks, keep, send):
        self.links = links
        self.halvings = list(zip(*walks))
        self.whole = [(b, b) for b in range(CHUNK_BITS, links.bits)]
        self.doublings = list(zip(*[[d for d in reversed(w) if d != "y"] for w in walks]))
        self.keep = keep
        if isinstance(keep, tuple):
            high = links.swap(send[1], ("core", "core"))
            self.recv = (links.swap(send[0], ("core", "core")), high)
            self.at = 0
        else:
            self.recv = links.swap(send, self.halvings[0])
            self.at = 1

    def step(self, *others):
        keep, recv, links, at = self.keep, self.recv, self.links, self.at
        if others:
            keep = after(keep, *others) if at else (keep[0], after(keep[1], *others))
        self.at += 1
        if at == 0:
            send = add_low(keep[1], recv[1])
            self.keep = add_low(keep[0], recv[0])
            self.recv = links.swap(send, self.halvings[0])
            return send
        if at < len(self.halvings):
            half = keep.shape[0] // 2
            send = add_low(keep[half:], recv[half:])
            self.keep = add_low(after(keep, send)[:half], recv[:half])
            self.recv = links.swap(send, self.halvings[at])
            return send
        at -= len(self.halvings)
        if at <= len(self.whole):
            self.keep = add_low(keep, recv)
        else:
            self.keep = jnp.concatenate([keep, recv], axis=0)
        self.recv = links.swap(self.keep, (self.whole + self.doublings)[at])
        return self.keep

    def more(self):
        return self.at < len(self.halvings + self.whole + self.doublings)


def on_device(tokens, w_qkv, w_attn_out, w_in, w_down, gain_attn, gain_mlp, cotangent, *, n_dp, n_ctx):
    links = Links(n_dp, n_ctx)
    own, width = tokens.shape
    rows = w_qkv.shape[0]
    frows = w_down.shape[0]
    ff = frows * n_dp
    seq = own * n_ctx
    groups = width // 128
    step, fstep = rows // CHUNKS, frows // CHUNKS
    dp_at = lax.axis_index("dp")
    ctx_at = lax.axis_index("ctx")
    core = dp_at & 1
    upper = dp_at >> 1

    marks = []
    for walks in (FIRST_WALKS, SECOND_WALKS):
        both = []
        for walk in walks:
            bits = [b for b in walk if b != "y"]
            both.append(sum(((ctx_at >> b) & 1) << (CHUNK_BITS - 1 - i) for i, b in enumerate(bits)))
        marks += [jnp.where(core == 0, both[0], both[1]), jnp.where(core == 0, both[1], both[0])]
    z_at = (ctx_at >> 1) & 1
    svec = jnp.stack([dp_at, z_at, marks[0], marks[2], marks[3]]).astype(jnp.int32)

    half_rows = rows // 2
    near_sides = ("core", "core")

    def z_half(cols):
        return pl.BlockSpec((half_rows, cols), lambda i, s: (s[1], 0))

    qkv_y = links.swap(w_qkv, ("y", "y"))
    pair = jnp.concatenate([tokens, links.swap(tokens, links.both(links.bits - 1))], axis=0)
    qkv_c = links.swap(w_qkv, near_sides)
    gains = jnp.stack([gain_attn, gain_mlp]).astype(F32)
    gains_c = links.swap(gains, near_sides)
    gains_y = links.swap(gains, ("y", "y"))
    gains_cy = links.swap(gains_y, near_sides)

    flips = []
    for order in links.orders:
        at = np.arange(n_ctx)
        flips.append(sum(((at >> i) & 1) << order[links.bits - 1 - i] for i in range(links.bits)).astype(np.int32))
    owner = ctx_at ^ jnp.where(core == 0, jnp.asarray(flips[0]), jnp.asarray(flips[1]))
    owner = after(owner, pair)
    positions = (owner[:, None] * own + jnp.arange(own, dtype=jnp.int32)[None, :]).reshape(seq).astype(F32)
    half = HEAD_DIM // 2
    frequencies = jnp.exp(jnp.arange(half, dtype=F32) * (-2.0 * math.log(THETA) / HEAD_DIM))
    angles = positions[:, None] * frequencies[None, :]
    cos, sin = jnp.cos(angles), jnp.sin(angles)
    cos = jnp.concatenate([cos] * 4, axis=1)
    sin = jnp.concatenate([-sin, sin, -sin, sin], axis=1)

    half_up = pl.pallas_call(
        pack_up_kernel,
        grid_spec=pltpu.PrefetchScalarGridSpec(
            num_scalar_prefetch=1,
            grid=(1,),
            in_specs=[z_half(3 * width), z_half(width)],
            out_specs=whole((4 * half_rows, width)),
        ),
        out_shape=jax.ShapeDtypeStruct((4 * half_rows, width), BF),
        compiler_params=params(),
        cost_estimate=cost(COSTS["pack_up"]),
        name="pack_up",
    )(svec, after(w_in, cos, sin), w_attn_out)
    everyone = pair
    for i in reversed(range(1, links.bits - 1)):
        come = after(links.swap(everyone, links.both(i)), half_up, gains_y)
        everyone = jnp.concatenate([everyone, come], axis=0)
    far = links.swap(everyone, links.both(0))
    qkv_y = after(qkv_y, everyone)
    qkv_cy = links.swap(qkv_y, near_sides)
    up_first = links.swap(after(half_up, qkv_y), ("y", "y"))

    block = math.gcd(seq // 2, 256)
    turn = seq // 2 // block
    table = pl.BlockSpec((block, 128), lambda i, *_: (i, 0))
    rows_of = pl.BlockSpec((block, width), lambda i, *_: (i, 0))
    half_seq = jax.ShapeDtypeStruct((seq // 2, width), BF)
    normed_near, queries, keys_near, values_near, full_qkv, gains_full = pl.pallas_call(
        functools.partial(qkv_near_kernel, own=own),
        grid_spec=pltpu.PrefetchScalarGridSpec(
            num_scalar_prefetch=1,
            grid=(turn,),
            in_specs=[rows_of] + [whole(w_qkv.shape)] * 4 + [whole((2, rows))] * 4 + [table] * 2,
            out_specs=[rows_of, whole((own, width)), rows_of, rows_of, whole((width, 3 * width)), whole((2, width))],
        ),
        out_shape=[
            half_seq,
            jax.ShapeDtypeStruct((own, width), BF),
            half_seq,
            half_seq,
            jax.ShapeDtypeStruct((width, 3 * width), BF),
            jax.ShapeDtypeStruct((2, width), F32),
        ],
        compiler_params=params(),
        cost_estimate=cost(COSTS["qkv_near"]),
        name="qkv_near",
    )(svec, everyone, w_qkv, qkv_c, qkv_y, qkv_cy, gains, gains_c, gains_y, gains_cy, cos, sin)
    in_c, out_c, down_c = (links.swap(after(w, everyone), near_sides) for w in (w_in, w_attn_out, w_down))

    far_table = pl.BlockSpec((block, 128), lambda i, *_: (i + turn, 0))
    up_first = after(up_first, full_qkv)
    up_second = links.swap(up_first, (1, 1))
    down_y = links.swap(after(w_down, up_first), ("y", "y"))
    up_cf = links.swap(up_first, near_sides)
    normed_far, keys_far, values_far = pl.pallas_call(
        qkv_far_kernel,
        grid=(turn,),
        in_specs=[rows_of, pl.BlockSpec((width, 3 * width), lambda i: (0, 0)), whole((2, width)), far_table, far_table],
        out_specs=[rows_of] * 3,
        out_shape=[half_seq] * 3,
        compiler_params=params(),
        cost_estimate=cost(COSTS["qkv_far"]),
        name="qkv_far",
    )(after(far, up_first, in_c, out_c, down_c), full_qkv, gains_full, cos, sin)
    keys = (keys_near, keys_far)
    values = (values_near, values_far)

    own_pair = pl.BlockSpec((own, 128), lambda g: (0, g))
    seq_pair = pl.BlockSpec((seq, 128), lambda g: (0, g))
    half_pair = pl.BlockSpec((seq // 2, 128), lambda g: (0, g))
    turned_pair = pl.BlockSpec((128, own), lambda g: (g, 0))
    lse_pair = pl.BlockSpec((1, 8, own), lambda g: (g, 0, 0))
    attn_t, lse = pl.pallas_call(
        attend_kernel,
        grid=(groups,),
        in_specs=[own_pair] + [half_pair] * 4,
        out_specs=[turned_pair, lse_pair],
        out_shape=[jax.ShapeDtypeStruct((width, own), F32), jax.ShapeDtypeStruct((groups, 8, own), F32)],
        compiler_params=params(),
        cost_estimate=cost(COSTS["attend"]),
        name="attend",
    )(queries, *keys, *values)
    up_second = after(up_second, attn_t)
    down_y = after(down_y, attn_t)

    up_cs = links.swap(up_second, near_sides)
    down_cy = links.swap(down_y, near_sides)


    vm = pl.BlockSpec(memory_space=pltpu.VMEM)
    length = (3 * step * 4 * width // 3 + (fstep + 4) * width) // 16
    part = 2 * rows + frows
    layer_out, d_mid, payload, d_attn_t, share_mine, share_core, share_y = pl.pallas_call(
        middle_kernel,
        in_specs=[pl.BlockSpec(memory_space=pltpu.SMEM)] + [vm] * 17,
        out_specs=[vm] * 7,
        out_shape=[
            jax.ShapeDtypeStruct((own, width), BF),
            jax.ShapeDtypeStruct((own, width), F32),
            jax.ShapeDtypeStruct((1, own + 16, width), BF),
            jax.ShapeDtypeStruct((width, own), BF),
            jax.ShapeDtypeStruct((part, own), BF),
            jax.ShapeDtypeStruct((part + 5 * width, own), BF),
            jax.ShapeDtypeStruct((2 * part + 5 * width, own), BF),
        ],
        scratch_shapes=[
            pltpu.VMEM((width, 3 * width), BF),
            pltpu.VMEM((width, width), BF),
            pltpu.VMEM((ff, width), BF),
            pltpu.VMEM((width, own), BF),
            pltpu.VMEM((width, own), BF),
            pltpu.VMEM((ff, own), BF),
        ],
        compiler_params=params(),
        cost_estimate=cost(COSTS["middle"]),
        name="middle",
    )(
        svec, tokens, attn_t, lse, w_in, in_c, w_attn_out, out_c, up_first, up_second, up_cf, up_cs,
        w_down, down_c, down_y, down_cy, cotangent, gains_full,
    )

    come_y = links.swap(share_y, ("y", "y"))
    come_c = links.swap(share_core, near_sides)

    d_query, d_kv = pl.pallas_call(
        attend_back_kernel,
        grid=(groups,),
        in_specs=[
            own_pair, half_pair, half_pair, half_pair, half_pair,
            pl.BlockSpec((1, own + 16, 128), lambda g: (0, 0, g)), turned_pair, turned_pair, lse_pair,
            whole((seq, 128)), whole((seq, 128)),
        ],
        out_specs=[own_pair, pl.BlockSpec((2, seq, 128), lambda g: (0, 0, g))],
        out_shape=[jax.ShapeDtypeStruct((own, width), BF), jax.ShapeDtypeStruct((2, seq, width), BF)],
        compiler_params=params(),
        cost_estimate=cost(COSTS["attend_back"]),
        name="attend_back",
    )(queries, *keys, *values, payload, d_attn_t, attn_t, lse, cos, sin)

    deep = math.gcd(seq // 2, 1024)
    turns = seq // 2 // deep
    second_parts = pl.pallas_call(
        qkv_grad_kernel,
        grid_spec=pltpu.PrefetchScalarGridSpec(
            num_scalar_prefetch=1,
            grid=(2 * turns,),
            in_specs=[
                pl.BlockSpec((deep, width), lambda i, s: (jnp.minimum(i, turns - 1), 0)),
                pl.BlockSpec((deep, width), lambda i, s: (jnp.maximum(i - turns, 0), 0)),
                pl.BlockSpec((2, deep, width), lambda i, s: (0, i, 0)),
                whole((own, width)),
            ],
            out_specs=[whole((CHUNKS, 16, step * 3 * width // 16))] * 4,
            scratch_shapes=[pltpu.VMEM((width, 3 * width), F32)],
        ),
        out_shape=[jax.ShapeDtypeStruct((CHUNKS, 16, step * 3 * width // 16), BF)] * 4,
        compiler_params=params(),
        cost_estimate=cost(COSTS["qkv_grad"]),
        name="qkv_grad",
    )(svec, normed_near, normed_far, d_kv, d_query)

    second = Chain(links, SECOND_WALKS, second_parts[:2], second_parts[2:])
    every_query = pl.pallas_call(
        queries_kernel,
        grid=(2 * turn,),
        in_specs=[
            pl.BlockSpec((block, width), lambda i: (jnp.minimum(i, turn - 1), 0)),
            pl.BlockSpec((block, width), lambda i: (jnp.maximum(i - turn, 0), 0)),
            pl.BlockSpec((width, width), lambda i: (0, 0)),
            table,
            table,
        ],
        out_specs=rows_of,
        out_shape=jax.ShapeDtypeStruct((seq, width), BF),
        compiler_params=params(),
        cost_estimate=cost(COSTS["every_query"]),
        name="every_query",
    )(after(normed_near, second_parts[0]), normed_far, full_qkv, cos, sin)
    come_y = after(come_y, every_query)
    come_cy = links.swap(come_y, near_sides)
    sent = second.step(come_y)
    first_low, first_high = pl.pallas_call(
        middle_grad_kernel,
        in_specs=[pl.BlockSpec(memory_space=pltpu.SMEM)] + [vm] * 5,
        out_specs=[vm] * 2,
        out_shape=[jax.ShapeDtypeStruct((CHUNKS // 2, 16, length), BF)] * 2,
        scratch_shapes=[
            pltpu.VMEM((part, n_dp * own), BF),
            pltpu.VMEM((n_dp * own, 5 * width), BF),
            pltpu.VMEM((rows, 3 * width), F32),
            pltpu.VMEM((rows, width), F32),
            pltpu.VMEM((frows, width), F32),
        ],
        compiler_params=params(),
        cost_estimate=cost(COSTS["middle_grad"]),
        name="middle_grad",
    )(svec, after(share_mine, sent), share_core, come_c, come_y, come_cy)
    first = Chain(links, FIRST_WALKS, first_low, first_high)
    gathered = links.swap(payload, links.both(links.bits - 1))
    gathered = jnp.concatenate([payload, after(gathered, first_high)], axis=0)
    late = first.step(second.step(gathered))
    late = first.step(second.step(late))
    for i in reversed(range(1, links.bits - 1)):
        come = links.swap(gathered, links.both(i))
        gathered = jnp.concatenate([gathered, after(come, late)], axis=0)
    gathered_far = links.swap(gathered, links.both(0))
    late = gathered
    while first.more() or second.more():
        for chain in (second, first):
            if chain.more():
                late = chain.step(late)

    d_key, d_value = pl.pallas_call(
        attend_keys_kernel,
        grid=(groups,),
        in_specs=[
            seq_pair, own_pair, own_pair,
            pl.BlockSpec((n_ctx // 2, own + 16, 128), lambda g: (0, 0, g)),
            pl.BlockSpec((n_ctx // 2, own + 16, 128), lambda g: (0, 0, g)),
            whole((own, 128)), whole((own, 128)),
        ],
        out_specs=[own_pair, own_pair],
        out_shape=[jax.ShapeDtypeStruct((own, width), BF)] * 2,
        compiler_params=params(),
        cost_estimate=cost(COSTS["attend_keys"]),
        name="attend_keys",
    )(every_query, keys_near, values_near, gathered, after(gathered_far, late), cos, sin)

    tokens_grad = pl.pallas_call(
        tokens_grad_kernel,
        in_specs=[vm] * 7,
        out_specs=vm,
        out_shape=jax.ShapeDtypeStruct((own, width), F32),
        compiler_params=params(),
        cost_estimate=cost(COSTS["tokens_grad"]),
        name="tokens_grad",
    )(tokens, d_query, d_key, d_value, full_qkv, gains_full, d_mid)
    def pair_specs(length, mark):
        half = CHUNKS // 2
        return [
            pl.BlockSpec((1, 16, length), lambda i, s, c=c: (((2 * i + c) ^ s[mark]) % half, 0, 0)) for c in (0, 0, 1, 1)
        ]

    def row_spec(count, cols):
        return pl.BlockSpec((count, cols), lambda i, s: (i, 0))

    qkv_grad, gain_attn_sum = pl.pallas_call(
        functools.partial(finish_second_kernel, step=step, width=width),
        grid_spec=pltpu.PrefetchScalarGridSpec(
            num_scalar_prefetch=1,
            grid=(CHUNKS // 2,),
            in_specs=pair_specs(step * 3 * width // 16, 3) + [row_spec(2 * step, 3 * width), whole((2, rows))],
            out_specs=[row_spec(2 * step, 3 * width), whole((1, rows))],
        ),
        out_shape=[jax.ShapeDtypeStruct((rows, 3 * width), F32), jax.ShapeDtypeStruct((1, rows), F32)],
        compiler_params=params(),
        cost_estimate=cost(COSTS["finish_second"]),
        name="finish_second",
    )(svec, second.keep, after(second.recv, tokens_grad), second.keep, second.recv, w_qkv, gains)

    in_grad, out_grad, down_grad, gain_mlp_sum = pl.pallas_call(
        functools.partial(finish_first_kernel, step=step, fstep=fstep, width=width),
        grid_spec=pltpu.PrefetchScalarGridSpec(
            num_scalar_prefetch=1,
            grid=(CHUNKS // 2,),
            in_specs=pair_specs(length, 2) + [row_spec(2 * step, 3 * width), whole((2, rows))],
            out_specs=[
                row_spec(2 * step, 3 * width),
                row_spec(2 * step, width),
                row_spec(2 * fstep, width),
                whole((1, rows)),
            ],
        ),
        out_shape=[
            jax.ShapeDtypeStruct((rows, 3 * width), F32),
            jax.ShapeDtypeStruct((rows, width), F32),
            jax.ShapeDtypeStruct((frows, width), F32),
            jax.ShapeDtypeStruct((1, rows), F32),
        ],
        compiler_params=params(),
        cost_estimate=cost(COSTS["finish_first"]),
        name="finish_first",
    )(svec, first.keep, after(first.recv, qkv_grad), first.keep, first.recv, w_in, gains)

    return (
        layer_out,
        tokens_grad,
        qkv_grad,
        out_grad,
        in_grad,
        down_grad,
        gain_attn_sum.reshape(rows),
        gain_mlp_sum.reshape(rows),
    )


def solution(mesh):
    return jax.shard_map(
        functools.partial(on_device, n_dp=mesh.shape["dp"], n_ctx=mesh.shape["ctx"]),
        mesh=mesh,
        in_specs=(
            P(("dp", "ctx"), None),
            P("dp", None),
            P("dp", None),
            P("dp", None),
            P("dp", None),
            P("dp"),
            P("dp"),
            P(("dp", "ctx"), None),
        ),
        out_specs=(
            P(("dp", "ctx"), None),
            P(("dp", "ctx"), None),
            P("dp", None),
            P("dp", None),
            P("dp", None),
            P("dp", None),
            P("dp"),
            P("dp"),
        ),
        check_vma=False,
    )
```

time: 267 us -> 212 us (0.79); the launches traced: 262 us -> 210 us
  waiting for transfers between devices: 128 us -> 68.9 us
  Pallas kernels: 62.7 us -> 85.3 us
  other arithmetic: 21.5 us -> 11.5 us
  starting transfers between devices: 38.3 us -> 32.4 us
    ppermute x28 -> x39, waiting for transfers between devices: 128 us -> 68.9 us  [swap(): return lax.ppermute(value, ('dp', 'ctx'), pairs)]
    pallas_call x4 -> x9, Pallas kernels: 32.8 us -> 57.5 us  [the longest x1 9.92 us: on_device(): pl.pallas_call(attend_back_kernel, grid=(groups,), in_specs=[own_pair, ha...]
    concatenate x10 -> x0, other arithmetic: 6.42 us -> none  [the longest x6 2.67 us: reduce_chunks(): jnp.concatenate([total, links.swap(total, links.both(step))], axis=0)]
    ppermute x28 -> x39, starting transfers between devices: 38.3 us -> 32.4 us  [swap(): return lax.ppermute(value, ('dp', 'ctx'), pairs)]
    unnamed x28 -> x68, local copies, waits for them, and re-layouts: 4.14 us -> 9.03 us
    slice x6 -> x0, local copies, waits for them, and re-layouts: 4.24 us -> none  [the longest x3 1.6 us: on_device(): d_kv = add_low(d_kv[:, :mid], links.swap(d_kv[:, mid:], links.both(i)))]
    pallas_call x1, Pallas kernels: 12.6 us -> 9.14 us  [on_device(): pl.pallas_call(middle_kernel, in_specs=[pl.BlockSpec(memory_space=pltpu.S...]
    convert_element_type x13 -> x14, other arithmetic: 5.77 us -> 6.98 us  [add_low(): return (left.astype(F32) + right.astype(F32)).astype(BF)]
  transfers between devices with their start and end apart: 28 -> 39, of which waited for: 14 -> 17; matrix products, arithmetic and copies ran while one was open for 9% -> 7% of each run, Pallas kernels for 17% -> 34%
where the time goes in v2:
time: 212 us; the launch traced here: 210 us
  Pallas kernels  85.3 us (40%)
  waiting for transfers between devices  68.9 us (33%)
  starting transfers between devices  32.4 us (15%)
  other arithmetic  11.5 us (5%)
  local copies, waits for them, and re-layouts  11.2 us (5%)
    ppermute x39, waiting for transfers between devices, swap(): return lax.ppermute(value, ('dp', 'ctx'), pairs)  68.9 us
    ppermute x39, starting transfers between devices, swap(): return lax.ppermute(value, ('dp', 'ctx'), pairs)  32.4 us
    pallas_call x1, Pallas kernels, on_device(): pl.pallas_call(attend_back_kernel, grid=(groups,), in_specs=[own_pair, ha...  9.92 us
    pallas_call x1, Pallas kernels, on_device(): pl.pallas_call(middle_kernel, in_specs=[pl.BlockSpec(memory_space=pltpu.S...  9.14 us
    unnamed x68, local copies, waits for them, and re-layouts  9.03 us
    pallas_call x1, Pallas kernels, on_device(): pl.pallas_call(functools.partial(qkv_near_kernel, own=own), grid_spec=plt...  8.29 us
    pallas_call x1, Pallas kernels, on_device(): pl.pallas_call(qkv_grad_kernel, grid_spec=pltpu.PrefetchScalarGridSpec(nu...  8.24 us
    pallas_call x1, Pallas kernels, on_device(): pl.pallas_call(attend_kernel, grid=(groups,), in_specs=[own_pair] + [half...  8.24 us
  transfers between devices with their start and end apart: 39, of which 17 were waited for; matrix products, arithmetic and copies ran while one was open for 7% of the time, Pallas kernels for 34%

profile of v2, /device:TPU:0, one launch (start us, length us, event | category | flops | bytes accessed | tf_op | source)
XLA Modules:
  0.0 210.5 jit_solution(2932525686492943886)
XLA Ops:
  0.6 3.0 %collective-permute-start.4 = (bf16[192,2304]{1,0:T(8,128)(2,1)}, bf16[192,2304]{1,0:T(8,128)(2,1)S(1)}, u32[]{:S(2)}, u32[]{:S(2)}) collective-permute-start(bf16[192,2304]{1,0:T(8,128)(2,1)} %w_ref.4), channel_id=1, source_target_pairs={{0,16},{1,17},{2,18},{3,19},{4,20},{5,21},{6,22},{7,23},{8,24},{9,... | collective-permute-start | bytes 2654216 | tf_op jit(solution)/shard_map/ppermute | solution.py:456
  3.7 2.6 %collective-permute-start = (bf16[128,768]{1,0:T(8,128)(2,1)}, bf16[128,768]{1,0:T(8,128)(2,1)S(1)}, u32[]{:S(2)}, u32[]{:S(2)}) collective-permute-start(bf16[128,768]{1,0:T(8,128)(2,1)} %x_ref.3), channel_id=1, source_target_pairs={{0,4},{1,5},{2,6},{3,7},{4,0},{5,1},{6,2},{7,3},{8,9},{9,8},{10,11... | collective-permute-start | bytes 589832 | tf_op jit(solution)/shard_map/ppermute | solution.py:456
  10.5 2.1 collective-permute-done
  13.5 1.9 fusion
  15.4 1.8 pad_maximum_fusion
  17.3 2.7 %pack_up.1 = bf16[384,768]{1,0:T(8,128)(2,1)} custom-call(s32[5]{0:T(128)} %stack.29.svec, bf16[192,2304]{1,0:T(8,128)(2,1)} %w_ref.5, bf16[192,768]{1,0:T(8,128)(2,1)} %o0.1), custom_call_target="tpu_custom_call" | custom-call | flops 575000000 | tf_op jit(solution)/shard_map/pack_up/pallas_call | solution.py:565
  20.0 3.6 %collective-permute-done.2.g2_ref = f32[2,192]{1,0:T(2,128)S(1)} collective-permute-done((f32[2,192]{1,0:T(2,128)S(1)}, f32[2,192]{1,0:T(2,128)S(1)}, u32[]{:S(2)}, u32[]{:S(2)}) %collective-permute-start.2) | collective-permute-done | bytes 1568 | tf_op jit(solution)/shard_map/ppermute | solution.py:456
  23.7 1.8 collective-permute-start.9
  26.0 1.9 collective-permute-done.6.g1_ref
  28.1 1.0 collective-permute-done.7.g3_ref
  29.1 1.5 collective-permute-start.8
  32.4 8.3 %qkv_near.1 = (bf16[512,768]{1,0:T(8,128)(2,1)}, bf16[128,768]{1,0:T(8,128)(2,1)}, bf16[512,768]{1,0:T(8,128)(2,1)}, bf16[512,768]{1,0:T(8,128)(2,1)}, bf16[768,2304]{1,0:T(8,128)(2,1)}, /*index=5*/f32[2,768]{1,0:T(2,128)}) custom-call(s32[5]{0:T(128)} %stack.29.svec, bf16[512,768]{1,0:T(8,128)(2,1)} %copy-done.8, bf16[192,2304]{1,0:T(8,128)(2,1)} %w_ref.4, ...), custom_call_target="tpu_custom_call" | custom-call | flops 575000000 | tf_op jit(solution)/shard_map/qkv_near/pallas_call | solution.py:592
  40.7 1.6 collective-permute-start.13
  42.4 1.2 collective-permute-start.16
  45.4 5.3 %qkv_far.1 = (bf16[512,768]{1,0:T(8,128)(2,1)}, bf16[512,768]{1,0:T(8,128)(2,1)}, bf16[512,768]{1,0:T(8,128)(2,1)}) custom-call(bf16[512,768]{1,0:T(8,128)(2,1)} %copy-done.19, bf16[768,2304]{1,0:T(8,128)(2,1)} %get-tuple-element.87.w_ref, f32[2,768]{1,0:T(2,128)} %get-tuple-element.93.gain_ref.gains_ref, f32[1024,128]{1,0:T(8,128)} %get-tuple-element.163.cos_ref, ...), custom_call_target="tpu_custom_call" | custom-call | flops 575000000 | tf_op jit(solution)/shard_map/qkv_far/pallas_call | solution.py:619
  50.7 8.2 %attend.1 = (f32[768,128]{1,0:T(8,128)}, f32[6,8,128]{2,1,0:T(8,128)}) custom-call(bf16[128,768]{1,0:T(8,128)(2,1)} %get-tuple-element.84.q_ref, bf16[512,768]{1,0:T(8,128)(2,1)} %get-tuple-element.85.kn_ref.k_ref, bf16[512,768]{1,0:T(8,128)(2,1)} %get-tuple-element.94.kf_ref, bf16[512,768]{1,0:T(8,128)(2,1)} %get-tuple-element.95.vn_ref.v_ref, ...), custom_call_target="tpu_custom_call" | custom-call | flops 575000000 | tf_op jit(solution)/shard_map/attend/pallas_call | solution.py:637
  59.5 2.1 %collective-permute-done.17.b3 = bf16[288,768]{1,0:T(8,128)(2,1)S(1)} collective-permute-done((bf16[288,768]{1,0:T(8,128)(2,1)S(1)}, bf16[288,768]{1,0:T(8,128)(2,1)S(1)}, u32[]{:S(2)}, u32[]{:S(2)}) %collective-permute-start.17) | collective-permute-done | bytes 442400 | tf_op jit(solution)/shard_map/ppermute | solution.py:456
  62.6 9.1 %middle.1 = (bf16[128,768]{1,0:T(8,128)(2,1)}, f32[128,768]{1,0:T(8,128)}, bf16[1,144,768]{2,1,0:T(8,128)(2,1)}, bf16[768,128]{1,0:T(8,128)(2,1)}, bf16[672,128]...) custom-call(s32[5]{0:T(128)} %stack.29.svec, bf16[128,768]{1,0:T(8,128)(2,1)} %x_ref.3, ...), custom_call_target="tpu_custom_call" | custom-call | flops 575000000 | tf_op jit(solution)/shard_map/middle/pallas_call | solution.py:657
  71.7 1.3 collective-permute-start.19
  73.0 9.9 %attend_back.1 = (bf16[128,768]{1,0:T(8,128)(2,1)}, bf16[2,1024,768]{2,1,0:T(8,128)(2,1)}) custom-call(bf16[128,768]{1,0:T(8,128)(2,1)} %get-tuple-element.84.q_ref, bf16[512,768]{1,0:T(8,128)(2,1)} %get-tuple-element.85.kn_ref.k_ref, bf16[512,768]{1,0:T(8,128)(2,1)} %get-tuple-element.94.kf_ref, bf16[512,768]{1,0:T(8,128)(2,1)} %get-tuple-element.95.vn_ref.v_ref, ...), custom_call_target="tpu_custom_call" | custom-call | flops 575000000 | tf_op jit(solution)/shard_map/attend_back/pallas_call | solution.py:689
  82.9 8.2 %qkv_grad.1 = (bf16[8,16,3456]{2,1,0:T(8,128)(2,1)}, bf16[8,16,3456]{2,1,0:T(8,128)(2,1)}, bf16[8,16,3456]{2,1,0:T(8,128)(2,1)}, bf16[8,16,3456]{2,1,0:T(8,128)(2,1)}) custom-call(s32[5]{0:T(128)} %stack.29.svec, bf16[512,768]{1,0:T(8,128)(2,1)} %get-tuple-element.110.near_ref, bf16[512,768]{1,0:T(8,128)(2,1)} %get-tuple-element.107.far_ref, ...), custom_call_target="tpu_custom_call" | custom-call | flops 575000000 | tf_op jit(solution)/shard_map/qkv_grad/pallas_call | solution.py:706
  91.3 2.6 %collective-permute-start.18 = (bf16[1,144,768]{2,1,0:T(8,128)(2,1)S(1)}, bf16[1,144,768]{2,1,0:T(8,128)(2,1)S(1)}, u32[]{:S(2)}, u32[]{:S(2)}) collective-permute-start(bf16[1,144,768]{2,1,0:T(8,128)(2,1)S(1)} %copy-done.13), channel_id=1, source_target_pairs={{0,4},{1,5},{2,6},{3,7},{4,0},{5,1},{6,2},{7,3},{8,9},{9,8},{10,11... | collective-permute-start | bytes 663560 | tf_op jit(solution)/shard_map/ppermute | solution.py:456
  94.4 5.9 %every_query.1.q_ref = bf16[1024,768]{1,0:T(8,128)(2,1)} custom-call(bf16[512,768]{1,0:T(8,128)(2,1)} %get-tuple-element.110.near_ref, bf16[512,768]{1,0:T(8,128)(2,1)} %get-tuple-element.107.far_ref, bf16[768,2304]{1,0:T(8,128)(2,1)} %get-tuple-element.87.w_ref, f32[1024,128]{1,0:T(8,128)} %get-tuple-element.163.cos_ref, f32[1024,128]{1,0:T(8,128)} %get-tuple-element.164.sin_ref), custom_call_target="tpu_custom_call" | custom-call | flops 575000000 | tf_op jit(solution)/shard_map/every_query/pallas_call | solution.py:727
  101.0 2.4 %collective-permute-done.19.y_ref = bf16[5184,128]{1,0:T(8,128)(2,1)S(1)} collective-permute-done((bf16[5184,128]{1,0:T(8,128)(2,1)}, bf16[5184,128]{1,0:T(8,128)(2,1)S(1)}, u32[]{:S(2)}, u32[]{:S(2)}) %collective-permute-start.19) | collective-permute-done | bytes 1327136 | tf_op jit(solution)/shard_map/ppermute | solution.py:456
  103.4 2.8 %add_convert_fusion.1 = bf16[8,16,3456]{2,1,0:T(8,128)(2,1)} fusion(bf16[8,16,3456]{2,1,0:T(8,128)(2,1)} %collective-permute-done.20, bf16[8,16,3456]{2,1,0:T(8,128)(2,1)S(1)} %copy-done.12), kind=kLoop, calls=%fused_computation.1 | loop fusion | flops 1769472 | bytes 2654208 | tf_op jit(solution)/shard_map/convert_element_type | solution.py:463
  106.2 1.2 collective-permute-start.25
  107.4 1.4 add_convert_fusion
  108.8 1.1 copy-done.7
  109.9 5.2 %middle_grad.1 = (bf16[4,16,6528]{2,1,0:T(8,128)(2,1)}, bf16[4,16,6528]{2,1,0:T(8,128)(2,1)}) custom-call(s32[5]{0:T(128)} %stack.29.svec, bf16[672,128]{1,0:T(8,128)(2,1)} %get-tuple-element.117.mine_ref, bf16[4512,128]{1,0:T(8,128)(2,1)} %get-tuple-element.118.core_ref, bf16[4512,128]{1,0:T(8,128)(2,1)} %collective-permute-done.21.c_ref, ...), custom_call_target="tpu_custom_call" | custom-call | flops 575000000 | tf_op jit(solution)/shard_map/middle_grad/pallas_call | solution.py:746
  115.1 1.0 collective-permute-start.26
  116.2 3.4 %collective-permute-done.25 = bf16[8,16,3456]{2,1,0:T(8,128)(2,1)} collective-permute-done((bf16[8,16,3456]{2,1,0:T(8,128)(2,1)}, bf16[8,16,3456]{2,1,0:T(8,128)(2,1)}, u32[]{:S(2)}, u32[]{:S(2)}) %collective-permute-start.25) | collective-permute-done | bytes 884768 | tf_op jit(solution)/shard_map/ppermute | solution.py:456
  119.6 1.1 add_convert_fusion.3
  122.0 1.1 add_convert_fusion.2
  123.1 4.7 %collective-permute-done.26 = bf16[4,16,6528]{2,1,0:T(8,128)(2,1)S(1)} collective-permute-done((bf16[4,16,6528]{2,1,0:T(8,128)(2,1)}, bf16[4,16,6528]{2,1,0:T(8,128)(2,1)S(1)}, u32[]{:S(2)}, u32[]{:S(2)}) %collective-permute-start.26) | collective-permute-done | bytes 835616 | tf_op jit(solution)/shard_map/ppermute | solution.py:456
  128.5 4.1 %collective-permute-done.27 = bf16[4,16,3456]{2,1,0:T(8,128)(2,1)S(1)} collective-permute-done((bf16[4,16,3456]{2,1,0:T(8,128)(2,1)S(1)}, bf16[4,16,3456]{2,1,0:T(8,128)(2,1)S(1)}, u32[]{:S(2)}, u32[]{:S(2)}) %collective-permute-start.27) | collective-permute-done | bytes 442400 | tf_op jit(solution)/shard_map/ppermute | solution.py:456
  133.4 8.0 %collective-permute-done.28 = bf16[2,16,6528]{2,1,0:T(8,128)(2,1)S(1)} collective-permute-done((bf16[2,16,6528]{2,1,0:T(8,128)(2,1)S(1)}, bf16[2,16,6528]{2,1,0:T(8,128)(2,1)S(1)}, u32[]{:S(2)}, u32[]{:S(2)}) %collective-permute-start.28) | collective-permute-done | bytes 417824 | tf_op jit(solution)/shard_map/ppermute | solution.py:456
  141.5 2.7 %collective-permute-start.31 = (bf16[1,16,6528]{2,1,0:T(8,128)(2,1)S(1)}, bf16[1,16,6528]{2,1,0:T(8,128)(2,1)S(1)}, u32[]{:S(2)}, u32[]{:S(2)}) collective-permute-start(bf16[1,16,6528]{2,1,0:T(8,128)(2,1)S(1)} %add_convert_fusion.10), channel_id=1, source_target_pairs={{0,4},{1,5},{2,6},{3,7},{4,0},{5,1},{6,2},{7,3},{8,12},{9,13},{10,... | collective-permute-start | bytes 626696 | tf_op jit(solution)/shard_map/ppermute | solution.py:456
  144.2 2.3 %collective-permute-start.32 = (bf16[1,16,3456]{2,1,0:T(8,128)(2,1)S(1)}, bf16[1,16,3456]{2,1,0:T(8,128)(2,1)S(1)}, u32[]{:S(2)}, u32[]{:S(2)}) collective-permute-start(bf16[1,16,3456]{2,1,0:T(8,128)(2,1)S(1)} %add_convert_fusion.13), channel_id=1, source_target_pairs={{0,4},{1,5},{2,6},{3,7},{4,0},{5,1},{6,2},{7,3},{8,12},{9,13},{10,... | collective-permute-start | bytes 331784 | tf_op jit(solution)/shard_map/ppermute | solution.py:456
  147.5 9.8 %collective-permute-done.31 = bf16[1,16,6528]{2,1,0:T(8,128)(2,1)S(1)} collective-permute-done((bf16[1,16,6528]{2,1,0:T(8,128)(2,1)S(1)}, bf16[1,16,6528]{2,1,0:T(8,128)(2,1)S(1)}, u32[]{:S(2)}, u32[]{:S(2)}) %collective-permute-start.31) | collective-permute-done | bytes 208928 | tf_op jit(solution)/shard_map/ppermute | solution.py:456
  157.4 2.2 %collective-permute-done.32 = bf16[1,16,3456]{2,1,0:T(8,128)(2,1)S(1)} collective-permute-done((bf16[1,16,3456]{2,1,0:T(8,128)(2,1)S(1)}, bf16[1,16,3456]{2,1,0:T(8,128)(2,1)S(1)}, u32[]{:S(2)}, u32[]{:S(2)}) %collective-permute-start.32) | collective-permute-done | bytes 110624 | tf_op jit(solution)/shard_map/ppermute | solution.py:456
  160.4 12.3 %collective-permute-done.33 = bf16[1,16,6528]{2,1,0:T(8,128)(2,1)S(1)} collective-permute-done((bf16[1,16,6528]{2,1,0:T(8,128)(2,1)S(1)}, bf16[1,16,6528]{2,1,0:T(8,128)(2,1)S(1)}, u32[]{:S(2)}, u32[]{:S(2)}) %collective-permute-start.33) | collective-permute-done | bytes 208928 | tf_op jit(solution)/shard_map/ppermute | solution.py:456
  172.8 1.8 collective-permute-done.34
  175.0 5.9 %collective-permute-done.35 = bf16[2,16,6528]{2,1,0:T(8,128)(2,1)S(1)} collective-permute-done((bf16[2,16,6528]{2,1,0:T(8,128)(2,1)S(1)}, bf16[2,16,6528]{2,1,0:T(8,128)(2,1)S(1)}, u32[]{:S(2)}, u32[]{:S(2)}) %collective-permute-start.35) | collective-permute-done | bytes 417824 | tf_op jit(solution)/shard_map/ppermute | solution.py:456
  181.7 2.7 %collective-permute-done.36 = bf16[2,16,3456]{2,1,0:T(8,128)(2,1)S(1)} collective-permute-done((bf16[2,16,3456]{2,1,0:T(8,128)(2,1)S(1)}, bf16[2,16,3456]{2,1,0:T(8,128)(2,1)S(1)}, u32[]{:S(2)}, u32[]{:S(2)}) %collective-permute-start.36) | collective-permute-done | bytes 221216 | tf_op jit(solution)/shard_map/ppermute | solution.py:456
  186.3 7.3 %attend_keys.1 = (bf16[128,768]{1,0:T(8,128)(2,1)}, bf16[128,768]{1,0:T(8,128)(2,1)}) custom-call(bf16[1024,768]{1,0:T(8,128)(2,1)} %every_query.1.q_ref, bf16[512,768]{1,0:T(8,128)(2,1)} %get-tuple-element.85.kn_ref.k_ref, bf16[512,768]{1,0:T(8,128)(2,1)} %get-tuple-element.95.vn_ref.v_ref, bf16[4,144,768]{2,1,0:T(8,128)(2,1)} %copy-done.5, ...), custom_call_target="tpu_custom_call" | custom-call | flops 575000000 | tf_op jit(solution)/shard_map/attend_keys/pallas_call | solution.py:777
  193.7 4.6 %tokens_grad.1 = f32[128,768]{1,0:T(8,128)} custom-call(bf16[128,768]{1,0:T(8,128)(2,1)} %x_ref.3, bf16[128,768]{1,0:T(8,128)(2,1)} %get-tuple-element.105.dq_ref, bf16[128,768]{1,0:T(8,128)(2,1)} %get-tuple-element.141.dk_ref, bf16[128,768]{1,0:T(8,128)(2,1)} %get-tuple-element.142.dv_ref, bf16[768,2304]{1,0:T(8,128)(2,1)} %get-tuple-element.87.w_ref, ...), custom_call_target="tpu_custom_call" | custom-call | flops 575000000 | tf_op jit(solution)/shard_map/tokens_grad/pallas_call | solution.py:793
  199.0 4.9 %finish_second.1 = (f32[192,2304]{1,0:T(8,128)}, f32[1,192]{1,0:T(1,128)}) custom-call(s32[5]{0:T(128)} %stack.29.svec, bf16[4,16,3456]{2,1,0:T(8,128)(2,1)} %copy-done.3, bf16[4,16,3456]{2,1,0:T(8,128)(2,1)} %copy-done.4, bf16[4,16,3456]{2,1,0:T(8,128)(2,1)} %copy-done.3, bf16[4,16,3456]{2,1,0:T(8,128)(2,1)} %copy-done.4, bf16[192,2304]{1,0:T(8,128)(2,1)} %w_ref.4, ...), custom_call_target="tpu_custom_call" | custom-call | flops 575000000 | tf_op jit(solution)/shard_map/finish_second/pallas_call | solution.py:811
  204.8 5.5 %finish_first.1 = (f32[192,2304]{1,0:T(8,128)}, f32[192,768]{1,0:T(8,128)}, f32[288,768]{1,0:T(8,128)}, f32[1,192]{1,0:T(1,128)}) custom-call(s32[5]{0:T(128)} %stack.29.svec, bf16[4,16,6528]{2,1,0:T(8,128)(2,1)} %copy-done, bf16[4,16,6528]{2,1,0:T(8,128)(2,1)} %copy-done.2, bf16[4,16,6528]{2,1,0:T(8,128)(2,1)} %copy-done, bf16[4,16,6528]{2,1,0:T(8,128)(2,1)} %copy-done.2, ...), custom_call_target="tpu_custom_call" | custom-call | flops 575000000 | tf_op jit(solution)/shard_map/finish_first/pallas_call | solution.py:825
  (143 shorter events, 22.0 us)
Async XLA Ops:
  0.6 23.0 %collective-permute-start.4 = (bf16[192,2304]{1,0:T(8,128)(2,1)}, bf16[192,2304]{1,0:T(8,128)(2,1)S(1)}, u32[]{:S(2)}, u32[]{:S(2)}) collective-permute-start(bf16[192,2304]{1,0:T(8,128)(2,1)} %w_ref.4), channel_id=1, source_target_pairs={{0,16},{1,17},{2,18},{3,19},{4,20},{5,21},{6,22},{7,23},{8,24},{9,... | collective-permute-start | bytes 2654216 | tf_op jit(solution)/shard_map/ppermute | solution.py:456
  3.7 26.9 %collective-permute-start.3 = (bf16[192,2304]{1,0:T(8,128)(2,1)}, bf16[192,2304]{1,0:T(8,128)(2,1)S(1)}, u32[]{:S(2)}, u32[]{:S(2)}) collective-permute-start(bf16[192,2304]{1,0:T(8,128)(2,1)} %w_ref.4), channel_id=1, source_target_pairs={{0,8},{1,9},{2,10},{3,11},{4,12},{5,13},{6,14},{7,15},{8,0},{9,1},... | collective-permute-start | bytes 2654216 | tf_op jit(solution)/shard_map/ppermute | solution.py:456
  3.7 8.9 %collective-permute-start = (bf16[128,768]{1,0:T(8,128)(2,1)}, bf16[128,768]{1,0:T(8,128)(2,1)S(1)}, u32[]{:S(2)}, u32[]{:S(2)}) collective-permute-start(bf16[128,768]{1,0:T(8,128)(2,1)} %x_ref.3), channel_id=1, source_target_pairs={{0,4},{1,5},{2,6},{3,7},{4,0},{5,1},{6,2},{7,3},{8,9},{9,8},{10,11... | collective-permute-start | bytes 589832 | tf_op jit(solution)/shard_map/ppermute | solution.py:456
  7.6 18.1 %copy-start.27 = (f32[2,192]{1,0:T(2,128)}, f32[2,192]{1,0:T(2,128)S(1)}, u32[]{:S(2)}) copy-start(f32[2,192]{1,0:T(2,128)S(1)} %maximum_convert_fusion.g0_ref.own_gain) | copy-start | bytes 4612
  7.6 16.0 %collective-permute-start.2 = (f32[2,192]{1,0:T(2,128)S(1)}, f32[2,192]{1,0:T(2,128)S(1)}, u32[]{:S(2)}, u32[]{:S(2)}) collective-permute-start(f32[2,192]{1,0:T(2,128)S(1)} %maximum_convert_fusion.g0_ref.own_gain), channel_id=1, source_target_pairs={{0,16},{1,17},{2,18},{3,19},{4,20},{5,21},{6,22},{7,23},{8,24},{9,... | collective-permute-start | bytes 4616 | tf_op jit(solution)/shard_map/ppermute | solution.py:456
  12.6 11.0 %collective-permute-start.1 = (bf16[256,768]{1,0:T(8,128)(2,1)S(1)}, bf16[256,768]{1,0:T(8,128)(2,1)S(1)}, u32[]{:S(2)}, u32[]{:S(2)}) collective-permute-start(bf16[256,768]{1,0:T(8,128)(2,1)S(1)} %get-tuple-element.156), channel_id=1, source_target_pairs={{0,2},{1,3},{2,0},{3,1},{4,6},{5,7},{6,4},{7,5},{8,12},{9,13},{10,... | collective-permute-start | bytes 1179656 | tf_op jit(solution)/shard_map/ppermute | solution.py:456
  23.6 7.0 %collective-permute-start.5 = (bf16[192,2304]{1,0:T(8,128)(2,1)S(1)}, bf16[192,2304]{1,0:T(8,128)(2,1)S(1)}, u32[]{:S(2)}, u32[]{:S(2)}) collective-permute-start(bf16[192,2304]{1,0:T(8,128)(2,1)S(1)} %collective-permute-done.4.w2), channel_id=1, source_target_pairs={{0,8},{1,9},{2,10},{3,11},{4,12},{5,13},{6,14},{7,15},{8,0},{9,1},... | collective-permute-start | bytes 2654216 | tf_op jit(solution)/shard_map/ppermute | solution.py:456
  23.7 17.0 %collective-permute-start.9 = (bf16[384,768]{1,0:T(8,128)(2,1)}, bf16[384,768]{1,0:T(8,128)(2,1)}, u32[]{:S(2)}, u32[]{:S(2)}) collective-permute-start(bf16[384,768]{1,0:T(8,128)(2,1)} %pack_up.1), channel_id=1, source_target_pairs={{0,16},{1,17},{2,18},{3,19},{4,20},{5,21},{6,22},{7,23},{8,24},{9,... | collective-permute-start | bytes 1769480 | tf_op jit(solution)/shard_map/ppermute | solution.py:456
  25.5 19.0 %collective-permute-start.10 = (bf16[192,2304]{1,0:T(8,128)(2,1)S(1)}, bf16[192,2304]{1,0:T(8,128)(2,1)S(1)}, u32[]{:S(2)}, u32[]{:S(2)}) collective-permute-start(bf16[192,2304]{1,0:T(8,128)(2,1)S(1)} %copy-done.1), channel_id=1, source_target_pairs={{0,8},{1,9},{2,10},{3,11},{4,12},{5,13},{6,14},{7,15},{8,0},{9,1},... | collective-permute-start | bytes 2654216 | tf_op jit(solution)/shard_map/ppermute | solution.py:456
  25.7 2.3 %collective-permute-start.6 = (f32[2,192]{1,0:T(2,128)S(1)}, f32[2,192]{1,0:T(2,128)S(1)}, u32[]{:S(2)}, u32[]{:S(2)}) collective-permute-start(f32[2,192]{1,0:T(2,128)S(1)} %maximum_convert_fusion.g0_ref.own_gain), channel_id=1, source_target_pairs={{0,8},{1,9},{2,10},{3,11},{4,12},{5,13},{6,14},{7,15},{8,0},{9,1},... | collective-permute-start | bytes 4616 | tf_op jit(solution)/shard_map/ppermute | solution.py:456
  28.0 1.2 collective-permute-start.7
  29.1 15.4 %collective-permute-start.8 = (bf16[512,768]{1,0:T(8,128)(2,1)S(1)}, bf16[512,768]{1,0:T(8,128)(2,1)S(1)}, u32[]{:S(2)}, u32[]{:S(2)}) collective-permute-start(bf16[512,768]{1,0:T(8,128)(2,1)S(1)} %constant_dynamic-update-slice_fusion.2.x_ref), channel_id=1, source_target_pairs={{0,1},{1,0},{2,3},{3,2},{4,5},{5,4},{6,7},{7,6},{8,10},{9,11},{10,... | collective-permute-start | bytes 2359304 | tf_op jit(solution)/shard_map/ppermute | solution.py:456
  30.6 11.8 %collective-permute-start.11 = (bf16[192,768]{1,0:T(8,128)(2,1)}, bf16[192,768]{1,0:T(8,128)(2,1)}, u32[]{:S(2)}, u32[]{:S(2)}) collective-permute-start(bf16[192,768]{1,0:T(8,128)(2,1)} %o0.1), channel_id=1, source_target_pairs={{0,8},{1,9},{2,10},{3,11},{4,12},{5,13},{6,14},{7,15},{8,0},{9,1},... | collective-permute-start | bytes 884744 | tf_op jit(solution)/shard_map/ppermute | solution.py:456
  40.7 18.2 %collective-permute-start.13 = (bf16[384,768]{1,0:T(8,128)(2,1)}, bf16[384,768]{1,0:T(8,128)(2,1)S(1)}, u32[]{:S(2)}, u32[]{:S(2)}) collective-permute-start(bf16[384,768]{1,0:T(8,128)(2,1)} %collective-permute-done.9.af), channel_id=1, source_target_pairs={{0,2},{1,3},{2,0},{3,1},{4,6},{5,7},{6,4},{7,5},{8,10},{9,11},{10,... | collective-permute-start | bytes 1769480 | tf_op jit(solution)/shard_map/ppermute | solution.py:456
  42.4 2.0 collective-permute-start.12
  42.4 17.0 %collective-permute-start.16 = (bf16[288,768]{1,0:T(8,128)(2,1)}, bf16[288,768]{1,0:T(8,128)(2,1)S(1)}, u32[]{:S(2)}, u32[]{:S(2)}) collective-permute-start(bf16[288,768]{1,0:T(8,128)(2,1)} %b0.1), channel_id=1, source_target_pairs={{0,16},{1,17},{2,18},{3,19},{4,20},{5,21},{6,22},{7,23},{8,24},{9,... | collective-permute-start | bytes 1327112 | tf_op jit(solution)/shard_map/ppermute | solution.py:456
  44.4 17.3 %copy-start.23 = (bf16[288,768]{1,0:T(8,128)(2,1)}, bf16[288,768]{1,0:T(8,128)(2,1)S(1)}, u32[]{:S(2)}) copy-start(bf16[288,768]{1,0:T(8,128)(2,1)S(1)} %collective-permute-done.12.b1) | copy-start | bytes 1327108
  44.4 15.1 %collective-permute-start.14 = (bf16[384,768]{1,0:T(8,128)(2,1)}, bf16[384,768]{1,0:T(8,128)(2,1)S(1)}, u32[]{:S(2)}, u32[]{:S(2)}) collective-permute-start(bf16[384,768]{1,0:T(8,128)(2,1)} %collective-permute-done.9.af), channel_id=1, source_target_pairs={{0,8},{1,9},{2,10},{3,11},{4,12},{5,13},{6,14},{7,15},{8,0},{9,1},... | collective-permute-start | bytes 1769480 | tf_op jit(solution)/shard_map/ppermute | solution.py:456
  58.9 2.7 %collective-permute-start.15 = (bf16[384,768]{1,0:T(8,128)(2,1)S(1)}, bf16[384,768]{1,0:T(8,128)(2,1)S(1)}, u32[]{:S(2)}, u32[]{:S(2)}) collective-permute-start(bf16[384,768]{1,0:T(8,128)(2,1)S(1)} %collective-permute-done.13.as_), channel_id=1, source_target_pairs={{0,8},{1,9},{2,10},{3,11},{4,12},{5,13},{6,14},{7,15},{8,0},{9,1},... | collective-permute-start | bytes 1769480 | tf_op jit(solution)/shard_map/ppermute | solution.py:456
  59.4 2.3 %collective-permute-start.17 = (bf16[288,768]{1,0:T(8,128)(2,1)S(1)}, bf16[288,768]{1,0:T(8,128)(2,1)S(1)}, u32[]{:S(2)}, u32[]{:S(2)}) collective-permute-start(bf16[288,768]{1,0:T(8,128)(2,1)S(1)} %collective-permute-done.16.b2), channel_id=1, source_target_pairs={{0,8},{1,9},{2,10},{3,11},{4,12},{5,13},{6,14},{7,15},{8,0},{9,1},... | collective-permute-start | bytes 1327112 | tf_op jit(solution)/shard_map/ppermute | solution.py:456
  71.7 31.7 %collective-permute-start.19 = (bf16[5184,128]{1,0:T(8,128)(2,1)}, bf16[5184,128]{1,0:T(8,128)(2,1)S(1)}, u32[]{:S(2)}, u32[]{:S(2)}) collective-permute-start(bf16[5184,128]{1,0:T(8,128)(2,1)} %get-tuple-element.113), channel_id=1, source_target_pairs={{0,16},{1,17},{2,18},{3,19},{4,20},{5,21},{6,22},{7,23},{8,24},{9,... | collective-permute-start | bytes 3981320 | tf_op jit(solution)/shard_map/ppermute | solution.py:456
  82.9 8.3 %copy-start.13 = (bf16[1,144,768]{2,1,0:T(8,128)(2,1)S(1)}, bf16[1,144,768]{2,1,0:T(8,128)(2,1)}, u32[]{:S(2)}) copy-start(bf16[1,144,768]{2,1,0:T(8,128)(2,1)} %get-tuple-element.103.da_ref) | copy-start | bytes 663556
  82.9 10.9 %copy-start.9 = (bf16[4512,128]{1,0:T(8,128)(2,1)S(1)}, bf16[4512,128]{1,0:T(8,128)(2,1)}, u32[]{:S(2)}) copy-start(bf16[4512,128]{1,0:T(8,128)(2,1)} %get-tuple-element.118.core_ref) | copy-start | bytes 3465220
  91.2 12.2 %collective-permute-start.20 = (bf16[8,16,3456]{2,1,0:T(8,128)(2,1)}, bf16[8,16,3456]{2,1,0:T(8,128)(2,1)}, u32[]{:S(2)}, u32[]{:S(2)}) collective-permute-start(bf16[8,16,3456]{2,1,0:T(8,128)(2,1)} %get-tuple-element.116), channel_id=1, source_target_pairs={{0,8},{1,9},{2,10},{3,11},{4,12},{5,13},{6,14},{7,15},{8,0},{9,1},... | collective-permute-start | bytes 2654216 | tf_op jit(solution)/shard_map/ppermute | solution.py:456
  91.3 24.9 %collective-permute-start.18 = (bf16[1,144,768]{2,1,0:T(8,128)(2,1)S(1)}, bf16[1,144,768]{2,1,0:T(8,128)(2,1)S(1)}, u32[]{:S(2)}, u32[]{:S(2)}) collective-permute-start(bf16[1,144,768]{2,1,0:T(8,128)(2,1)S(1)} %copy-done.13), channel_id=1, source_target_pairs={{0,4},{1,5},{2,6},{3,7},{4,0},{5,1},{6,2},{7,3},{8,9},{9,8},{10,11... | collective-permute-start | bytes 663560 | tf_op jit(solution)/shard_map/ppermute | solution.py:456
  93.9 13.5 %collective-permute-start.24 = (bf16[8,16,3456]{2,1,0:T(8,128)(2,1)}, bf16[8,16,3456]{2,1,0:T(8,128)(2,1)}, u32[]{:S(2)}, u32[]{:S(2)}) collective-permute-start(bf16[8,16,3456]{2,1,0:T(8,128)(2,1)} %get-tuple-element.122), channel_id=1, source_target_pairs={{0,8},{1,9},{2,10},{3,11},{4,12},{5,13},{6,14},{7,15},{8,0},{9,1},... | collective-permute-start | bytes 2654216 | tf_op jit(solution)/shard_map/ppermute | solution.py:456
  93.9 9.6 %copy-start.12 = (bf16[8,16,3456]{2,1,0:T(8,128)(2,1)S(1)}, bf16[8,16,3456]{2,1,0:T(8,128)(2,1)}, u32[]{:S(2)}) copy-start(bf16[8,16,3456]{2,1,0:T(8,128)(2,1)} %get-tuple-element.115) | copy-start | bytes 2654212
  93.9 14.9 %collective-permute-start.21 = (bf16[4512,128]{1,0:T(8,128)(2,1)S(1)}, bf16[4512,128]{1,0:T(8,128)(2,1)}, u32[]{:S(2)}, u32[]{:S(2)}) collective-permute-start(bf16[4512,128]{1,0:T(8,128)(2,1)S(1)} %copy-done.9), channel_id=1, source_target_pairs={{0,8},{1,9},{2,10},{3,11},{4,12},{5,13},{6,14},{7,15},{8,0},{9,1},... | collective-permute-start | bytes 3465224 | tf_op jit(solution)/shard_map/ppermute | solution.py:456
  103.4 5.4 %collective-permute-start.22 = (bf16[5184,128]{1,0:T(8,128)(2,1)S(1)}, bf16[5184,128]{1,0:T(8,128)(2,1)S(1)}, u32[]{:S(2)}, u32[]{:S(2)}) collective-permute-start(bf16[5184,128]{1,0:T(8,128)(2,1)S(1)} %collective-permute-done.19.y_ref), channel_id=1, source_target_pairs={{0,8},{1,9},{2,10},{3,11},{4,12},{5,13},{6,14},{7,15},{8,0},{9,1},... | collective-permute-start | bytes 3981320 | tf_op jit(solution)/shard_map/ppermute | solution.py:456
  106.2 13.4 %collective-permute-start.25 = (bf16[8,16,3456]{2,1,0:T(8,128)(2,1)}, bf16[8,16,3456]{2,1,0:T(8,128)(2,1)}, u32[]{:S(2)}, u32[]{:S(2)}) collective-permute-start(bf16[8,16,3456]{2,1,0:T(8,128)(2,1)} %add_convert_fusion.1), channel_id=1, source_target_pairs={{0,16},{1,17},{2,18},{3,19},{4,20},{5,21},{6,22},{7,23},{8,10},{9,... | collective-permute-start | bytes 2654216 | tf_op jit(solution)/shard_map/ppermute | solution.py:456
  115.1 12.7 %copy-start.18 = (bf16[4,16,6528]{2,1,0:T(8,128)(2,1)S(1)}, bf16[4,16,6528]{2,1,0:T(8,128)(2,1)}, u32[]{:S(2)}) copy-start(bf16[4,16,6528]{2,1,0:T(8,128)(2,1)} %get-tuple-element.125) | copy-start | bytes 2506756
  115.1 12.7 %collective-permute-start.26 = (bf16[4,16,6528]{2,1,0:T(8,128)(2,1)}, bf16[4,16,6528]{2,1,0:T(8,128)(2,1)S(1)}, u32[]{:S(2)}, u32[]{:S(2)}) collective-permute-start(bf16[4,16,6528]{2,1,0:T(8,128)(2,1)} %get-tuple-element.119), channel_id=1, source_target_pairs={{0,1},{1,0},{2,3},{3,2},{4,5},{5,4},{6,7},{7,6},{8,10},{9,11},{10,... | collective-permute-start | bytes 2506760 | tf_op jit(solution)/shard_map/ppermute | solution.py:456
  120.7 11.9 %collective-permute-start.27 = (bf16[4,16,3456]{2,1,0:T(8,128)(2,1)S(1)}, bf16[4,16,3456]{2,1,0:T(8,128)(2,1)S(1)}, u32[]{:S(2)}, u32[]{:S(2)}) collective-permute-start(bf16[4,16,3456]{2,1,0:T(8,128)(2,1)S(1)} %add_convert_fusion.3), channel_id=1, source_target_pairs={{0,1},{1,0},{2,3},{3,2},{4,5},{5,4},{6,7},{7,6},{8,24},{9,25},{10,... | collective-permute-start | bytes 1327112 | tf_op jit(solution)/shard_map/ppermute | solution.py:456
  121.4 22.7 %collective-permute-start.23 = (bf16[2,144,768]{2,1,0:T(8,128)(2,1)S(1)}, bf16[2,144,768]{2,1,0:T(8,128)(2,1)S(1)}, u32[]{:S(2)}, u32[]{:S(2)}) collective-permute-start(bf16[2,144,768]{2,1,0:T(8,128)(2,1)S(1)} %get-tuple-element.152), channel_id=1, source_target_pairs={{0,2},{1,3},{2,0},{3,1},{4,6},{5,7},{6,4},{7,5},{8,12},{9,13},{10,... | collective-permute-start | bytes 1327112 | tf_op jit(solution)/shard_map/ppermute | solution.py:456
  128.0 13.4 %collective-permute-start.28 = (bf16[2,16,6528]{2,1,0:T(8,128)(2,1)S(1)}, bf16[2,16,6528]{2,1,0:T(8,128)(2,1)S(1)}, u32[]{:S(2)}, u32[]{:S(2)}) collective-permute-start(bf16[2,16,6528]{2,1,0:T(8,128)(2,1)S(1)} %add_convert_fusion.5), channel_id=1, source_target_pairs={{0,2},{1,3},{2,0},{3,1},{4,6},{5,7},{6,4},{7,5},{8,9},{9,8},{10,11... | collective-permute-start | bytes 1253384 | tf_op jit(solution)/shard_map/ppermute | solution.py:456
  132.7 11.5 %collective-permute-start.30 = (bf16[2,16,3456]{2,1,0:T(8,128)(2,1)S(1)}, bf16[2,16,3456]{2,1,0:T(8,128)(2,1)S(1)}, u32[]{:S(2)}, u32[]{:S(2)}) collective-permute-start(bf16[2,16,3456]{2,1,0:T(8,128)(2,1)S(1)} %add_convert_fusion.7), channel_id=1, source_target_pairs={{0,2},{1,3},{2,0},{3,1},{4,6},{5,7},{6,4},{7,5},{8,9},{9,8},{10,11... | collective-permute-start | bytes 663560 | tf_op jit(solution)/shard_map/ppermute | solution.py:456
  141.5 15.8 %collective-permute-start.31 = (bf16[1,16,6528]{2,1,0:T(8,128)(2,1)S(1)}, bf16[1,16,6528]{2,1,0:T(8,128)(2,1)S(1)}, u32[]{:S(2)}, u32[]{:S(2)}) collective-permute-start(bf16[1,16,6528]{2,1,0:T(8,128)(2,1)S(1)} %add_convert_fusion.10), channel_id=1, source_target_pairs={{0,4},{1,5},{2,6},{3,7},{4,0},{5,1},{6,2},{7,3},{8,12},{9,13},{10,... | collective-permute-start | bytes 626696 | tf_op jit(solution)/shard_map/ppermute | solution.py:456
  144.2 30.8 %copy-start.5 = (bf16[4,144,768]{2,1,0:T(8,128)(2,1)}, bf16[4,144,768]{2,1,0:T(8,128)(2,1)S(1)}, u32[]{:S(2)}) copy-start(bf16[4,144,768]{2,1,0:T(8,128)(2,1)S(1)} %constant_dynamic-update-slice_fusion.7.near_ref) | copy-start | bytes 2654212
  144.2 15.4 %collective-permute-start.32 = (bf16[1,16,3456]{2,1,0:T(8,128)(2,1)S(1)}, bf16[1,16,3456]{2,1,0:T(8,128)(2,1)S(1)}, u32[]{:S(2)}, u32[]{:S(2)}) collective-permute-start(bf16[1,16,3456]{2,1,0:T(8,128)(2,1)S(1)} %add_convert_fusion.13), channel_id=1, source_target_pairs={{0,4},{1,5},{2,6},{3,7},{4,0},{5,1},{6,2},{7,3},{8,12},{9,13},{10,... | collective-permute-start | bytes 331784 | tf_op jit(solution)/shard_map/ppermute | solution.py:456
  146.5 38.9 %collective-permute-start.29 = (bf16[4,144,768]{2,1,0:T(8,128)(2,1)S(1)}, bf16[4,144,768]{2,1,0:T(8,128)(2,1)S(1)}, u32[]{:S(2)}, u32[]{:S(2)}) collective-permute-start(bf16[4,144,768]{2,1,0:T(8,128)(2,1)S(1)} %constant_dynamic-update-slice_fusion.7.near_ref), channel_id=1, source_target_pairs={{0,1},{1,0},{2,3},{3,2},{4,5},{5,4},{6,7},{7,6},{8,10},{9,11},{10,... | collective-permute-start | bytes 2654216 | tf_op jit(solution)/shard_map/ppermute | solution.py:456
  157.3 15.4 %collective-permute-start.33 = (bf16[1,16,6528]{2,1,0:T(8,128)(2,1)S(1)}, bf16[1,16,6528]{2,1,0:T(8,128)(2,1)S(1)}, u32[]{:S(2)}, u32[]{:S(2)}) collective-permute-start(bf16[1,16,6528]{2,1,0:T(8,128)(2,1)S(1)} %add_convert_fusion.8), channel_id=1, source_target_pairs={{0,4},{1,5},{2,6},{3,7},{4,0},{5,1},{6,2},{7,3},{8,12},{9,13},{10,... | collective-permute-start | bytes 626696 | tf_op jit(solution)/shard_map/ppermute | solution.py:456
  159.7 15.0 %collective-permute-start.34 = (bf16[1,16,3456]{2,1,0:T(8,128)(2,1)S(1)}, bf16[1,16,3456]{2,1,0:T(8,128)(2,1)S(1)}, u32[]{:S(2)}, u32[]{:S(2)}) collective-permute-start(bf16[1,16,3456]{2,1,0:T(8,128)(2,1)S(1)} %add_convert_fusion.11), channel_id=1, source_target_pairs={{0,4},{1,5},{2,6},{3,7},{4,0},{5,1},{6,2},{7,3},{8,12},{9,13},{10,... | collective-permute-start | bytes 331784 | tf_op jit(solution)/shard_map/ppermute | solution.py:456
  172.8 8.1 %collective-permute-start.35 = (bf16[2,16,6528]{2,1,0:T(8,128)(2,1)S(1)}, bf16[2,16,6528]{2,1,0:T(8,128)(2,1)S(1)}, u32[]{:S(2)}, u32[]{:S(2)}) collective-permute-start(bf16[2,16,6528]{2,1,0:T(8,128)(2,1)S(1)} %constant_dynamic-update-slice_fusion.10), channel_id=1, source_target_pairs={{0,2},{1,3},{2,0},{3,1},{4,6},{5,7},{6,4},{7,5},{8,9},{9,8},{10,11... | collective-permute-start | bytes 1253384 | tf_op jit(solution)/shard_map/ppermute | solution.py:456
  174.7 9.7 %collective-permute-start.36 = (bf16[2,16,3456]{2,1,0:T(8,128)(2,1)S(1)}, bf16[2,16,3456]{2,1,0:T(8,128)(2,1)S(1)}, u32[]{:S(2)}, u32[]{:S(2)}) collective-permute-start(bf16[2,16,3456]{2,1,0:T(8,128)(2,1)S(1)} %constant_dynamic-update-slice_fusion.12), channel_id=1, source_target_pairs={{0,2},{1,3},{2,0},{3,1},{4,6},{5,7},{6,4},{7,5},{8,9},{9,8},{10,11... | collective-permute-start | bytes 663560 | tf_op jit(solution)/shard_map/ppermute | solution.py:456
  180.9 12.8 %copy-start = (bf16[4,16,6528]{2,1,0:T(8,128)(2,1)}, bf16[4,16,6528]{2,1,0:T(8,128)(2,1)S(1)}, u32[]{:S(2)}) copy-start(bf16[4,16,6528]{2,1,0:T(8,128)(2,1)S(1)} %constant_dynamic-update-slice_fusion.14.ka.kb) | copy-start | bytes 2506756
  180.9 23.0 %collective-permute-start.38 = (bf16[4,16,6528]{2,1,0:T(8,128)(2,1)S(1)}, bf16[4,16,6528]{2,1,0:T(8,128)(2,1)S(1)}, u32[]{:S(2)}, u32[]{:S(2)}) collective-permute-start(bf16[4,16,6528]{2,1,0:T(8,128)(2,1)S(1)} %constant_dynamic-update-slice_fusion.14.ka.kb), channel_id=1, source_target_pairs={{0,1},{1,0},{2,3},{3,2},{4,5},{5,4},{6,7},{7,6},{8,10},{9,11},{10,... | collective-permute-start | bytes 2506760 | tf_op jit(solution)/shard_map/ppermute | solution.py:456
  184.4 9.2 %copy-start.3 = (bf16[4,16,3456]{2,1,0:T(8,128)(2,1)}, bf16[4,16,3456]{2,1,0:T(8,128)(2,1)S(1)}, u32[]{:S(2)}) copy-start(bf16[4,16,3456]{2,1,0:T(8,128)(2,1)S(1)} %constant_dynamic-update-slice_fusion.16.ka.kb) | copy-start | bytes 1327108
  184.4 13.9 %collective-permute-start.37 = (bf16[4,16,3456]{2,1,0:T(8,128)(2,1)S(1)}, bf16[4,16,3456]{2,1,0:T(8,128)(2,1)S(1)}, u32[]{:S(2)}, u32[]{:S(2)}) collective-permute-start(bf16[4,16,3456]{2,1,0:T(8,128)(2,1)S(1)} %constant_dynamic-update-slice_fusion.16.ka.kb), channel_id=1, source_target_pairs={{0,1},{1,0},{2,3},{3,2},{4,5},{5,4},{6,7},{7,6},{8,10},{9,11},{10,... | collective-permute-start | bytes 1327112 | tf_op jit(solution)/shard_map/ppermute | solution.py:456
  (22 other events, 74.9 us)

commit v3 on v2

--- a/solution.py
+++ b/solution.py
@@ -13,7 +13,7 @@
 HEAD_DIM = 64
 THETA = 160000.0
 EPS = 1e-05
-CHUNK_BITS = 3
+CHUNK_BITS = 2
 CHUNKS = 1 << CHUNK_BITS
 BF = jnp.bfloat16
 F32 = jnp.float32
@@ -32,8 +32,8 @@
     "finish_first": 0.5,
     "finish_second": 0.5,
 }
-FIRST_WALKS = ((0, 1, 2), (1, 0, 2))
-SECOND_WALKS = (("y", 0, 1, 2), (1, "y", 0, 2))
+FIRST_WALKS = ((0, 1), (1, 0))
+SECOND_WALKS = (("y", 0, 1), (1, "y", 0))
 VMEM_LIMIT = 58 * 1024 * 1024
 
 
@@ -306,8 +306,8 @@
     for spot in reversed(range(CHUNKS)):
         c = spot ^ svec[2]
         at = pl.multiple_of(c * step, 8)
-        fat = pl.multiple_of(2 * fstep * (c >> 1) + (fstep - 4) * (c & 1), 8)
-        parts = [g_in[pl.ds(at, step), :], g_out[pl.ds(at, step), :], g_down[pl.ds(fat, fstep + 4), :]]
+        fat = pl.multiple_of(c * fstep, 8)
+        parts = [g_in[pl.ds(at, step), :], g_out[pl.ds(at, step), :], g_down[pl.ds(fat, fstep), :]]
         target = high_ref if spot >= CHUNKS // 2 else low_ref
         target[spot % (CHUNKS // 2)] = fold(parts).astype(BF)
 
@@ -392,46 +392,31 @@
     out_ref[...] = dm_ref[...] + norm_back(d_normed, xhat, scale, gains_ref[0:1, :])
 
 
-def chunk_of(mark, keep_ref, recv_ref, chunk):
-    there = (chunk ^ mark) >= CHUNKS // 2
-    return jnp.where(there, recv_ref[0].astype(F32), keep_ref[0].astype(F32))
-
-
-def gain_rows(product, gain, gain_ref):
-    at, rows, cols = pl.program_id(0), product.shape[0], gain_ref.shape[1]
+def gain_rows(product, gain, chunk, before, gain_ref):
+    rows, cols = product.shape[0], gain_ref.shape[1]
     total = jnp.sum(product, axis=1, keepdims=True)
     row = lax.broadcasted_iota(jnp.int32, (rows, cols), 0)
     col = lax.broadcasted_iota(jnp.int32, (rows, cols), 1)
-    part = jnp.sum(jnp.where(col == row + at * rows, total, 0.0), axis=0, keepdims=True) / gain
-
-    @pl.when(at == 0)
+    part = jnp.sum(jnp.where(col == row + chunk * rows, total, 0.0), axis=0, keepdims=True) / gain
+    first = pl.program_id(0) == 0
+
+    @pl.when(first)
     def _():
-        gain_ref[...] = part
-
-    @pl.when(at > 0)
+        gain_ref[...] = part + before
+
+    @pl.when(jnp.logical_not(first))
     def _():
         gain_ref[...] += part
 
 
-def finish_first_kernel(svec, ka, ra, kb, rb, w_ref, own_gain, in_ref, out_ref, down_ref, gain_ref, *, step, fstep, width):
-    shapes = ((step, 3 * width), (step, width), (fstep + 4, width))
-    at = 2 * pl.program_id(0)
-    parts_a = unfold(chunk_of(svec[2], ka, ra, at), shapes)
-    parts_b = unfold(chunk_of(svec[2], kb, rb, at + 1), shapes)
-    both = [jnp.concatenate([a, b], axis=0) for a, b in zip(parts_a[:2], parts_b[:2])]
-    in_ref[...] = both[0]
-    out_ref[...] = both[1]
-    down_ref[...] = jnp.concatenate([parts_a[2], parts_b[2][8:]], axis=0)
-    gain_rows(w_ref[...].astype(F32) * both[0], own_gain[1:2, :], gain_ref)
-
-
-def finish_second_kernel(svec, ka, ra, kb, rb, w_ref, own_gain, out_ref, gain_ref, *, step, width):
-    shapes = ((step, 3 * width),)
-    at = 2 * pl.program_id(0)
-    chunks = [chunk_of(svec[3], ka, ra, at), chunk_of(svec[3], kb, rb, at + 1)]
-    grad = jnp.concatenate([unfold(c, shapes)[0] for c in chunks], axis=0)
-    out_ref[...] = grad
-    gain_rows(w_ref[...].astype(F32) * grad, own_gain[0:1, :], gain_ref)
+def finish_kernel(svec, part_ref, w_ref, own_gain, *refs, shapes, mark, row, begin):
+    grads = unfold(part_ref[0].astype(F32), shapes)
+    outs = refs[1 + len(shapes) :] if begin else refs
+    for out_ref, grad in zip(outs, grads):
+        out_ref[...] = grad
+    before = refs[0][...] if begin else 0.0
+    chunk = (pl.program_id(0) + begin) ^ svec[mark]
+    gain_rows(w_ref[...].astype(F32) * grads[0], own_gain[row : row + 1, :], chunk, before, outs[-1])
 
 
 class Links:
@@ -652,7 +637,7 @@
 
 
     vm = pl.BlockSpec(memory_space=pltpu.VMEM)
-    length = (3 * step * 4 * width // 3 + (fstep + 4) * width) // 16
+    length = (4 * step + fstep) * width // 16
     part = 2 * rows + frows
     layer_out, d_mid, payload, d_attn_t, share_mine, share_core, share_y = pl.pallas_call(
         middle_kernel,
@@ -762,17 +747,12 @@
     first = Chain(links, FIRST_WALKS, first_low, first_high)
     gathered = links.swap(payload, links.both(links.bits - 1))
     gathered = jnp.concatenate([payload, after(gathered, first_high)], axis=0)
-    late = first.step(second.step(gathered))
-    late = first.step(second.step(late))
+    late = first.step(second.step(first.step(second.step(gathered))))
     for i in reversed(range(1, links.bits - 1)):
         come = links.swap(gathered, links.both(i))
         gathered = jnp.concatenate([gathered, after(come, late)], axis=0)
     gathered_far = links.swap(gathered, links.both(0))
-    late = gathered
-    while first.more() or second.more():
-        for chain in (second, first):
-            if chain.more():
-                late = chain.step(late)
+    late = second.step(first.step(gathered))
 
     d_key, d_value = pl.pallas_call(
         attend_keys_kernel,
@@ -790,6 +770,8 @@
         name="attend_keys",
     )(every_query, keys_near, values_near, gathered, after(gathered_far, late), cos, sin)
 
+    late = second.step(first.step(d_key))
+
     tokens_grad = pl.pallas_call(
         tokens_grad_kernel,
         in_specs=[vm] * 7,
@@ -798,53 +780,46 @@
         compiler_params=params(),
         cost_estimate=cost(COSTS["tokens_grad"]),
         name="tokens_grad",
-    )(tokens, d_query, d_key, d_value, full_qkv, gains_full, d_mid)
-    def pair_specs(length, mark):
+    )(after(tokens, late), d_query, d_key, d_value, full_qkv, gains_full, d_mid)
+    late = tokens_grad
+    while first.more() or second.more():
+        for chain in (first, second):
+            if chain.more():
+                late = chain.step(late)
+
+    def finish(chain, weight, shapes, mark, row, name):
         half = CHUNKS // 2
-        return [
-            pl.BlockSpec((1, 16, length), lambda i, s, c=c: (((2 * i + c) ^ s[mark]) % half, 0, 0)) for c in (0, 0, 1, 1)
-        ]
-
-    def row_spec(count, cols):
-        return pl.BlockSpec((count, cols), lambda i, s: (i, 0))
-
-    qkv_grad, gain_attn_sum = pl.pallas_call(
-        functools.partial(finish_second_kernel, step=step, width=width),
-        grid_spec=pltpu.PrefetchScalarGridSpec(
-            num_scalar_prefetch=1,
-            grid=(CHUNKS // 2,),
-            in_specs=pair_specs(step * 3 * width // 16, 3) + [row_spec(2 * step, 3 * width), whole((2, rows))],
-            out_specs=[row_spec(2 * step, 3 * width), whole((1, rows))],
-        ),
-        out_shape=[jax.ShapeDtypeStruct((rows, 3 * width), F32), jax.ShapeDtypeStruct((1, rows), F32)],
-        compiler_params=params(),
-        cost_estimate=cost(COSTS["finish_second"]),
-        name="finish_second",
-    )(svec, second.keep, after(second.recv, tokens_grad), second.keep, second.recv, w_qkv, gains)
-
-    in_grad, out_grad, down_grad, gain_mlp_sum = pl.pallas_call(
-        functools.partial(finish_first_kernel, step=step, fstep=fstep, width=width),
-        grid_spec=pltpu.PrefetchScalarGridSpec(
-            num_scalar_prefetch=1,
-            grid=(CHUNKS // 2,),
-            in_specs=pair_specs(length, 2) + [row_spec(2 * step, 3 * width), whole((2, rows))],
-            out_specs=[
-                row_spec(2 * step, 3 * width),
-                row_spec(2 * step, width),
-                row_spec(2 * fstep, width),
-                whole((1, rows)),
-            ],
-        ),
-        out_shape=[
-            jax.ShapeDtypeStruct((rows, 3 * width), F32),
-            jax.ShapeDtypeStruct((rows, width), F32),
-            jax.ShapeDtypeStruct((frows, width), F32),
-            jax.ShapeDtypeStruct((1, rows), F32),
-        ],
-        compiler_params=params(),
-        cost_estimate=cost(COSTS["finish_first"]),
-        name="finish_first",
-    )(svec, first.keep, after(first.recv, qkv_grad), first.keep, first.recv, w_in, gains)
+        done = ()
+        for begin, part in ((0, chain.keep), (half, chain.recv)):
+
+            def rows_at(count, cols, begin=begin):
+                return pl.BlockSpec((count, cols), lambda i, s: ((i + begin) ^ s[mark], 0))
+
+            big = [jax.ShapeDtypeStruct((r * CHUNKS, c), F32) for r, c in shapes]
+            done = pl.pallas_call(
+                functools.partial(finish_kernel, shapes=shapes, mark=mark, row=row, begin=begin),
+                grid_spec=pltpu.PrefetchScalarGridSpec(
+                    num_scalar_prefetch=1,
+                    grid=(half,),
+                    in_specs=[
+                        pl.BlockSpec((1, 16, part.shape[2]), lambda i, s: (i, 0, 0)),
+                        rows_at(*shapes[0]),
+                        whole((2, rows)),
+                    ]
+                    + ([whole((1, rows))] + [pl.BlockSpec(memory_space=pl.ANY)] * len(shapes) if begin else []),
+                    out_specs=[rows_at(*shape) for shape in shapes] + [whole((1, rows))],
+                ),
+                out_shape=big + [jax.ShapeDtypeStruct((1, rows), F32)],
+                input_output_aliases={5 + i: i for i in range(len(shapes))} if begin else {},
+                compiler_params=params(),
+                cost_estimate=cost(COSTS[name]),
+                name=name,
+            )(svec, part, weight, gains, *((done[-1], *done[:-1]) if begin else ()))
+        return done
+
+    first_shapes = ((step, 3 * width), (step, width), (fstep, width))
+    in_grad, out_grad, down_grad, gain_mlp_sum = finish(first, w_in, first_shapes, 2, 1, "finish_first")
+    qkv_grad, gain_attn_sum = finish(second, w_qkv, ((step, 3 * width),), 3, 0, "finish_second")
 
     return (
         layer_out,

time: 212 us -> 203 us (0.958)
  waiting for transfers between devices: 68.9 us -> 59.9 us
    ppermute x39 -> x37, waiting for transfers between devices: 68.9 us -> 59.9 us  [swap(): return lax.ppermute(value, ('dp', 'ctx'), pairs)]
    pallas_call x2 -> x4, Pallas kernels: 10.4 us -> 11.9 us  [finish(): pl.pallas_call(functools.partial(finish_kernel, shapes=shapes, mark=mark,...]
    ppermute x39 -> x37, starting transfers between devices: 32.4 us -> 31.5 us  [swap(): return lax.ppermute(value, ('dp', 'ctx'), pairs)]
    unnamed x68 -> x67, local copies, waits for them, and re-layouts: 9.03 us -> 9.04 us
    convert_element_type x14 -> x12, other arithmetic: 6.98 us -> 6.98 us  [add_low(): return (left.astype(F32) + right.astype(F32)).astype(BF)]
  transfers between devices with their start and end apart: 39 -> 37, of which waited for: 17 -> 16; matrix products, arithmetic and copies ran while one was open for 7% -> 8% of each run, Pallas kernels for 34% -> 37%
where the time goes in v3:
time: 203 us; the launch traced here: 202 us
  Pallas kernels  86.7 us (43%)
  waiting for transfers between devices  59.9 us (30%)
  starting transfers between devices  31.5 us (16%)
  other arithmetic  11.5 us (6%)
  local copies, waits for them, and re-layouts  11.2 us (6%)
    ppermute x37, waiting for transfers between devices, swap(): return lax.ppermute(value, ('dp', 'ctx'), pairs)  59.9 us
    ppermute x37, starting transfers between devices, swap(): return lax.ppermute(value, ('dp', 'ctx'), pairs)  31.5 us
    pallas_call x4, Pallas kernels, finish(): pl.pallas_call(functools.partial(finish_kernel, shapes=shapes, mark=mark,...  11.9 us
    pallas_call x1, Pallas kernels, on_device(): pl.pallas_call(attend_back_kernel, grid=(groups,), in_specs=[own_pair, ha...  9.93 us
    pallas_call x1, Pallas kernels, on_device(): pl.pallas_call(middle_kernel, in_specs=[pl.BlockSpec(memory_space=pltpu.S...  9.14 us
    unnamed x67, local copies, waits for them, and re-layouts  9.04 us
    pallas_call x1, Pallas kernels, on_device(): pl.pallas_call(functools.partial(qkv_near_kernel, own=own), grid_spec=plt...  8.29 us
    pallas_call x1, Pallas kernels, on_device(): pl.pallas_call(attend_kernel, grid=(groups,), in_specs=[own_pair] + [half...  8.24 us
  transfers between devices with their start and end apart: 37, of which 16 were waited for; matrix products, arithmetic and copies ran while one was open for 8% of the time, Pallas kernels for 37%

profile of v3, /device:TPU:0, one launch (start us, length us, event | category | flops | bytes accessed | tf_op | source)
XLA Modules:
  0.0 202.0 jit_solution(1843881502002074851)
XLA Ops:
  0.6 3.0 %collective-permute-start.4 = (bf16[192,2304]{1,0:T(8,128)(2,1)}, bf16[192,2304]{1,0:T(8,128)(2,1)S(1)}, u32[]{:S(2)}, u32[]{:S(2)}) collective-permute-start(bf16[192,2304]{1,0:T(8,128)(2,1)} %w_ref.7), channel_id=1, source_target_pairs={{0,16},{1,17},{2,18},{3,19},{4,20},{5,21},{6,22},{7,23},{8,24},{9,... | collective-permute-start | bytes 2654216 | tf_op jit(solution)/shard_map/ppermute | solution.py:441
  3.7 2.6 %collective-permute-start = (bf16[128,768]{1,0:T(8,128)(2,1)}, bf16[128,768]{1,0:T(8,128)(2,1)S(1)}, u32[]{:S(2)}, u32[]{:S(2)}) collective-permute-start(bf16[128,768]{1,0:T(8,128)(2,1)} %x_ref.2), channel_id=1, source_target_pairs={{0,4},{1,5},{2,6},{3,7},{4,0},{5,1},{6,2},{7,3},{8,9},{9,8},{10,11... | collective-permute-start | bytes 589832 | tf_op jit(solution)/shard_map/ppermute | solution.py:441
  10.5 2.1 %collective-permute-done = bf16[128,768]{1,0:T(8,128)(2,1)S(1)} collective-permute-done((bf16[128,768]{1,0:T(8,128)(2,1)}, bf16[128,768]{1,0:T(8,128)(2,1)S(1)}, u32[]{:S(2)}, u32[]{:S(2)}) %collective-permute-start) | collective-permute-done | bytes 196640 | tf_op jit(solution)/shard_map/ppermute | solution.py:441
  13.5 1.9 fusion
  15.4 1.8 pad_maximum_fusion
  17.3 2.7 %pack_up.1 = bf16[384,768]{1,0:T(8,128)(2,1)} custom-call(s32[5]{0:T(128)} %stack.29.svec, bf16[192,2304]{1,0:T(8,128)(2,1)} %w_ref.9, bf16[192,768]{1,0:T(8,128)(2,1)} %o0.1), custom_call_target="tpu_custom_call" | custom-call | flops 575000000 | tf_op jit(solution)/shard_map/pack_up/pallas_call | solution.py:550
  20.0 3.6 %collective-permute-done.2.g2_ref = f32[2,192]{1,0:T(2,128)S(1)} collective-permute-done((f32[2,192]{1,0:T(2,128)S(1)}, f32[2,192]{1,0:T(2,128)S(1)}, u32[]{:S(2)}, u32[]{:S(2)}) %collective-permute-start.2) | collective-permute-done | bytes 1568 | tf_op jit(solution)/shard_map/ppermute | solution.py:441
  23.7 1.8 collective-permute-start.9
  26.0 1.9 collective-permute-done.6.g1_ref
  29.1 1.5 collective-permute-start.8
  32.4 8.3 %qkv_near.1 = (bf16[512,768]{1,0:T(8,128)(2,1)}, bf16[128,768]{1,0:T(8,128)(2,1)}, bf16[512,768]{1,0:T(8,128)(2,1)}, bf16[512,768]{1,0:T(8,128)(2,1)}, bf16[768,2304]{1,0:T(8,128)(2,1)}, /*index=5*/f32[2,768]{1,0:T(2,128)}) custom-call(s32[5]{0:T(128)} %stack.29.svec, bf16[512,768]{1,0:T(8,128)(2,1)} %copy-done.4, bf16[192,2304]{1,0:T(8,128)(2,1)} %w_ref.7, ...), custom_call_target="tpu_custom_call" | custom-call | flops 575000000 | tf_op jit(solution)/shard_map/qkv_near/pallas_call | solution.py:577
  40.7 1.6 collective-permute-start.13
  42.4 1.2 collective-permute-start.16
  45.4 5.3 %qkv_far.1 = (bf16[512,768]{1,0:T(8,128)(2,1)}, bf16[512,768]{1,0:T(8,128)(2,1)}, bf16[512,768]{1,0:T(8,128)(2,1)}) custom-call(bf16[512,768]{1,0:T(8,128)(2,1)} %copy-done.16, bf16[768,2304]{1,0:T(8,128)(2,1)} %get-tuple-element.88.w_ref, f32[2,768]{1,0:T(2,128)} %get-tuple-element.94.gain_ref.gains_ref, f32[1024,128]{1,0:T(8,128)} %get-tuple-element.165.cos_ref, ...), custom_call_target="tpu_custom_call" | custom-call | flops 575000000 | tf_op jit(solution)/shard_map/qkv_far/pallas_call | solution.py:604
  50.7 8.2 %attend.1 = (f32[768,128]{1,0:T(8,128)}, f32[6,8,128]{2,1,0:T(8,128)}) custom-call(bf16[128,768]{1,0:T(8,128)(2,1)} %get-tuple-element.85.q_ref, bf16[512,768]{1,0:T(8,128)(2,1)} %get-tuple-element.86.kn_ref.k_ref, bf16[512,768]{1,0:T(8,128)(2,1)} %get-tuple-element.95.kf_ref, bf16[512,768]{1,0:T(8,128)(2,1)} %get-tuple-element.96.vn_ref.v_ref, ...), custom_call_target="tpu_custom_call" | custom-call | flops 575000000 | tf_op jit(solution)/shard_map/attend/pallas_call | solution.py:622
  59.5 2.1 %collective-permute-done.17.b3 = bf16[288,768]{1,0:T(8,128)(2,1)S(1)} collective-permute-done((bf16[288,768]{1,0:T(8,128)(2,1)S(1)}, bf16[288,768]{1,0:T(8,128)(2,1)S(1)}, u32[]{:S(2)}, u32[]{:S(2)}) %collective-permute-start.17) | collective-permute-done | bytes 442400 | tf_op jit(solution)/shard_map/ppermute | solution.py:441
  62.6 9.1 %middle.1 = (bf16[128,768]{1,0:T(8,128)(2,1)}, f32[128,768]{1,0:T(8,128)}, bf16[1,144,768]{2,1,0:T(8,128)(2,1)}, bf16[768,128]{1,0:T(8,128)(2,1)}, bf16[672,128]...) custom-call(s32[5]{0:T(128)} %stack.29.svec, bf16[128,768]{1,0:T(8,128)(2,1)} %x_ref.2, ...), custom_call_target="tpu_custom_call" | custom-call | flops 575000000 | tf_op jit(solution)/shard_map/middle/pallas_call | solution.py:642
  71.7 1.3 collective-permute-start.20
  73.0 9.9 %attend_back.1 = (bf16[128,768]{1,0:T(8,128)(2,1)}, bf16[2,1024,768]{2,1,0:T(8,128)(2,1)}) custom-call(bf16[128,768]{1,0:T(8,128)(2,1)} %get-tuple-element.85.q_ref, bf16[512,768]{1,0:T(8,128)(2,1)} %get-tuple-element.86.kn_ref.k_ref, bf16[512,768]{1,0:T(8,128)(2,1)} %get-tuple-element.95.kf_ref, bf16[512,768]{1,0:T(8,128)(2,1)} %get-tuple-element.96.vn_ref.v_ref, ...), custom_call_target="tpu_custom_call" | custom-call | flops 575000000 | tf_op jit(solution)/shard_map/attend_back/pallas_call | solution.py:674
  83.0 8.2 %qkv_grad.1 = (bf16[4,16,6912]{2,1,0:T(8,128)(2,1)}, bf16[4,16,6912]{2,1,0:T(8,128)(2,1)}, bf16[4,16,6912]{2,1,0:T(8,128)(2,1)}, bf16[4,16,6912]{2,1,0:T(8,128)(2,1)}) custom-call(s32[5]{0:T(128)} %stack.29.svec, bf16[512,768]{1,0:T(8,128)(2,1)} %get-tuple-element.115.near_ref, bf16[512,768]{1,0:T(8,128)(2,1)} %get-tuple-element.105.far_ref, ...), custom_call_target="tpu_custom_call" | custom-call | flops 575000000 | tf_op jit(solution)/shard_map/qkv_grad/pallas_call | solution.py:691
  91.3 2.6 %collective-permute-start.19 = (bf16[1,144,768]{2,1,0:T(8,128)(2,1)S(1)}, bf16[1,144,768]{2,1,0:T(8,128)(2,1)S(1)}, u32[]{:S(2)}, u32[]{:S(2)}) collective-permute-start(bf16[1,144,768]{2,1,0:T(8,128)(2,1)S(1)} %copy-done.9), channel_id=1, source_target_pairs={{0,4},{1,5},{2,6},{3,7},{4,0},{5,1},{6,2},{7,3},{8,9},{9,8},{10,11... | collective-permute-start | bytes 663560 | tf_op jit(solution)/shard_map/ppermute | solution.py:441
  94.4 5.9 %every_query.1.q_ref = bf16[1024,768]{1,0:T(8,128)(2,1)} custom-call(bf16[512,768]{1,0:T(8,128)(2,1)} %get-tuple-element.115.near_ref, bf16[512,768]{1,0:T(8,128)(2,1)} %get-tuple-element.105.far_ref, bf16[768,2304]{1,0:T(8,128)(2,1)} %get-tuple-element.88.w_ref, f32[1024,128]{1,0:T(8,128)} %get-tuple-element.165.cos_ref, f32[1024,128]{1,0:T(8,128)} %get-tuple-element.166.sin_ref), custom_call_target="tpu_custom_call" | custom-call | flops 575000000 | tf_op jit(solution)/shard_map/every_query/pallas_call | solution.py:712
  101.0 2.4 %collective-permute-done.20.y_ref = bf16[5184,128]{1,0:T(8,128)(2,1)S(1)} collective-permute-done((bf16[5184,128]{1,0:T(8,128)(2,1)}, bf16[5184,128]{1,0:T(8,128)(2,1)S(1)}, u32[]{:S(2)}, u32[]{:S(2)}) %collective-permute-start.20) | collective-permute-done | bytes 1327136 | tf_op jit(solution)/shard_map/ppermute | solution.py:441
  103.4 2.8 %add_convert_fusion = bf16[4,16,6912]{2,1,0:T(8,128)(2,1)} fusion(bf16[4,16,6912]{2,1,0:T(8,128)(2,1)} %collective-permute-done.21, bf16[4,16,6912]{2,1,0:T(8,128)(2,1)S(1)} %copy-done.8), kind=kLoop, calls=%fused_computation | loop fusion | flops 1769472 | bytes 2654208 | tf_op jit(solution)/shard_map/convert_element_type | solution.py:448
  106.2 1.2 collective-permute-start.24
  107.4 1.4 add_convert_fusion.1
  108.8 1.1 copy-done.3
  109.9 5.2 %middle_grad.1 = (bf16[2,16,12672]{2,1,0:T(8,128)(2,1)}, bf16[2,16,12672]{2,1,0:T(8,128)(2,1)}) custom-call(s32[5]{0:T(128)} %stack.29.svec, bf16[672,128]{1,0:T(8,128)(2,1)} %get-tuple-element.119.mine_ref, bf16[4512,128]{1,0:T(8,128)(2,1)} %get-tuple-element.120.core_ref, bf16[4512,128]{1,0:T(8,128)(2,1)} %collective-permute-done.22.c_ref, ...), custom_call_target="tpu_custom_call" | custom-call | flops 575000000 | tf_op jit(solution)/shard_map/middle_grad/pallas_call | solution.py:731
  115.1 1.0 collective-permute-start.25
  116.2 3.4 %collective-permute-done.24 = bf16[4,16,6912]{2,1,0:T(8,128)(2,1)} collective-permute-done((bf16[4,16,6912]{2,1,0:T(8,128)(2,1)}, bf16[4,16,6912]{2,1,0:T(8,128)(2,1)}, u32[]{:S(2)}, u32[]{:S(2)}) %collective-permute-start.24) | collective-permute-done | bytes 884768 | tf_op jit(solution)/shard_map/ppermute | solution.py:441
  119.6 1.1 add_convert_fusion.3
  122.0 1.1 add_convert_fusion.2
  123.1 4.4 %collective-permute-done.25 = bf16[2,16,12672]{2,1,0:T(8,128)(2,1)S(1)} collective-permute-done((bf16[2,16,12672]{2,1,0:T(8,128)(2,1)}, bf16[2,16,12672]{2,1,0:T(8,128)(2,1)S(1)}, u32[]{:S(2)}, u32[]{:S(2)}) %collective-permute-start.25) | collective-permute-done | bytes 811040 | tf_op jit(solution)/shard_map/ppermute | solution.py:441
  128.2 4.1 %collective-permute-done.26 = bf16[2,16,6912]{2,1,0:T(8,128)(2,1)S(1)} collective-permute-done((bf16[2,16,6912]{2,1,0:T(8,128)(2,1)S(1)}, bf16[2,16,6912]{2,1,0:T(8,128)(2,1)S(1)}, u32[]{:S(2)}, u32[]{:S(2)}) %collective-permute-start.26) | collective-permute-done | bytes 442400 | tf_op jit(solution)/shard_map/ppermute | solution.py:441
  133.0 8.1 %collective-permute-done.27 = bf16[1,16,12672]{2,1,0:T(8,128)(2,1)S(1)} collective-permute-done((bf16[1,16,12672]{2,1,0:T(8,128)(2,1)S(1)}, bf16[1,16,12672]{2,1,0:T(8,128)(2,1)S(1)}, u32[]{:S(2)}, u32[]{:S(2)}) %collective-permute-start.27) | collective-permute-done | bytes 405536 | tf_op jit(solution)/shard_map/ppermute | solution.py:441
  141.1 2.7 %collective-permute-start.29 = (bf16[1,16,12672]{2,1,0:T(8,128)(2,1)S(1)}, bf16[1,16,12672]{2,1,0:T(8,128)(2,1)S(1)}, u32[]{:S(2)}, u32[]{:S(2)}) collective-permute-start(bf16[1,16,12672]{2,1,0:T(8,128)(2,1)S(1)} %add_convert_fusion.5), channel_id=1, source_target_pairs={{0,4},{1,5},{2,6},{3,7},{4,0},{5,1},{6,2},{7,3},{8,12},{9,13},{10,... | collective-permute-start | bytes 1216520 | tf_op jit(solution)/shard_map/ppermute | solution.py:441
  144.9 18.1 %collective-permute-done.29 = bf16[1,16,12672]{2,1,0:T(8,128)(2,1)S(1)} collective-permute-done((bf16[1,16,12672]{2,1,0:T(8,128)(2,1)S(1)}, bf16[1,16,12672]{2,1,0:T(8,128)(2,1)S(1)}, u32[]{:S(2)}, u32[]{:S(2)}) %collective-permute-start.29) | collective-permute-done | bytes 405536 | tf_op jit(solution)/shard_map/ppermute | solution.py:441
  163.2 2.3 %collective-permute-start.33 = (bf16[1,16,6912]{2,1,0:T(8,128)(2,1)S(1)}, bf16[1,16,6912]{2,1,0:T(8,128)(2,1)S(1)}, u32[]{:S(2)}, u32[]{:S(2)}) collective-permute-start(bf16[1,16,6912]{2,1,0:T(8,128)(2,1)S(1)} %add_convert_fusion.9), channel_id=1, source_target_pairs={{0,4},{1,5},{2,6},{3,7},{4,0},{5,1},{6,2},{7,3},{8,12},{9,13},{10,... | collective-permute-start | bytes 663560 | tf_op jit(solution)/shard_map/ppermute | solution.py:441
  166.5 7.3 %attend_keys.1 = (bf16[128,768]{1,0:T(8,128)(2,1)}, bf16[128,768]{1,0:T(8,128)(2,1)}) custom-call(bf16[1024,768]{1,0:T(8,128)(2,1)} %every_query.1.q_ref, bf16[512,768]{1,0:T(8,128)(2,1)} %get-tuple-element.86.kn_ref.k_ref, bf16[512,768]{1,0:T(8,128)(2,1)} %get-tuple-element.96.vn_ref.v_ref, bf16[4,144,768]{2,1,0:T(8,128)(2,1)} %copy-done.1, ...), custom_call_target="tpu_custom_call" | custom-call | flops 575000000 | tf_op jit(solution)/shard_map/attend_keys/pallas_call | solution.py:757
  173.9 1.6 collective-permute-done.32
  176.2 4.6 %tokens_grad.1 = f32[128,768]{1,0:T(8,128)} custom-call(bf16[128,768]{1,0:T(8,128)(2,1)} %x_ref.2, bf16[128,768]{1,0:T(8,128)(2,1)} %get-tuple-element.109.dq_ref, bf16[128,768]{1,0:T(8,128)(2,1)} %get-tuple-element.135.dk_ref, bf16[128,768]{1,0:T(8,128)(2,1)} %get-tuple-element.139.dv_ref, bf16[768,2304]{1,0:T(8,128)(2,1)} %get-tuple-element.88.w_ref, ...), custom_call_target="tpu_custom_call" | custom-call | flops 575000000 | tf_op jit(solution)/shard_map/tokens_grad/pallas_call | solution.py:775
  180.8 3.7 %collective-permute-done.34 = bf16[1,16,6912]{2,1,0:T(8,128)(2,1)S(1)} collective-permute-done((bf16[1,16,6912]{2,1,0:T(8,128)(2,1)S(1)}, bf16[1,16,6912]{2,1,0:T(8,128)(2,1)S(1)}, u32[]{:S(2)}, u32[]{:S(2)}) %collective-permute-start.34) | collective-permute-done | bytes 221216 | tf_op jit(solution)/shard_map/ppermute | solution.py:441
  184.6 1.6 collective-permute-start.35
  186.2 3.1 %finish_first.2 = (f32[192,2304]{1,0:T(8,128)}, f32[192,768]{1,0:T(8,128)}, f32[288,768]{1,0:T(8,128)}, f32[1,192]{1,0:T(1,128)}) custom-call(s32[5]{0:T(128)} %stack.29.svec, bf16[2,16,12672]{2,1,0:T(8,128)(2,1)} %copy-done.24, bf16[192,2304]{1,0:T(8,128)(2,1)} %w_ref.9, f32[2,192]{1,0:T(2,128)} %copy-done.27), custom_call_target="tpu_custom_call" | custom-call | flops 575000000 | tf_op jit(solution)/shard_map/finish_first/pallas_call | solution.py:799
  189.3 2.9 %finish_second.2 = (f32[192,2304]{1,0:T(8,128)}, f32[1,192]{1,0:T(1,128)}) custom-call(s32[5]{0:T(128)} %stack.29.svec, bf16[2,16,6912]{2,1,0:T(8,128)(2,1)} %copy-done.25, bf16[192,2304]{1,0:T(8,128)(2,1)} %w_ref.7, f32[2,192]{1,0:T(2,128)} %copy-done.27), custom_call_target="tpu_custom_call" | custom-call | flops 575000000 | tf_op jit(solution)/shard_map/finish_second/pallas_call | solution.py:799
  192.2 2.0 %collective-permute-done.35.part_ref = bf16[2,16,6912]{2,1,0:T(8,128)(2,1)S(1)} collective-permute-done((bf16[2,16,6912]{2,1,0:T(8,128)(2,1)S(1)}, bf16[2,16,6912]{2,1,0:T(8,128)(2,1)S(1)}, u32[]{:S(2)}, u32[]{:S(2)}) %collective-permute-start.35) | collective-permute-done | bytes 442400 | tf_op jit(solution)/shard_map/ppermute | solution.py:441
  195.0 2.9 %finish_second.3 = (f32[192,2304]{1,0:T(8,128)}, f32[1,192]{1,0:T(1,128)}) custom-call(s32[5]{0:T(128)} %stack.29.svec, bf16[2,16,6912]{2,1,0:T(8,128)(2,1)} %copy-done.23, bf16[192,2304]{1,0:T(8,128)(2,1)} %w_ref.7, f32[2,192]{1,0:T(2,128)} %copy-done.27, f32[1,192]{1,0:T(1,128)} %get-tuple-element.142.refs_0_, ...), custom_call_target="tpu_custom_call", output_to_operand_aliasing={{0}: (5, {})} | custom-call | flops 575000000 | tf_op jit(solution)/shard_map/finish_second/pallas_call | solution.py:799
  198.8 3.1 %finish_first.3 = (f32[192,2304]{1,0:T(8,128)}, f32[192,768]{1,0:T(8,128)}, f32[288,768]{1,0:T(8,128)}, f32[1,192]{1,0:T(1,128)}) custom-call(s32[5]{0:T(128)} %stack.29.svec, bf16[2,16,12672]{2,1,0:T(8,128)(2,1)} %copy-done.15, bf16[192,2304]{1,0:T(8,128)(2,1)} %w_ref.9, ...), custom_call_target="tpu_custom_call", output_to_operand_aliasing={{0}: (5, {}), {1}: (6, {}), {2}: (7, {})} | custom-call | flops 575000000 | tf_op jit(solution)/shard_map/finish_first/pallas_call | solution.py:799
  (135 shorter events, 20.8 us)
Async XLA Ops:
  0.6 23.0 %collective-permute-start.4 = (bf16[192,2304]{1,0:T(8,128)(2,1)}, bf16[192,2304]{1,0:T(8,128)(2,1)S(1)}, u32[]{:S(2)}, u32[]{:S(2)}) collective-permute-start(bf16[192,2304]{1,0:T(8,128)(2,1)} %w_ref.7), channel_id=1, source_target_pairs={{0,16},{1,17},{2,18},{3,19},{4,20},{5,21},{6,22},{7,23},{8,24},{9,... | collective-permute-start | bytes 2654216 | tf_op jit(solution)/shard_map/ppermute | solution.py:441
  3.7 26.9 %collective-permute-start.3 = (bf16[192,2304]{1,0:T(8,128)(2,1)}, bf16[192,2304]{1,0:T(8,128)(2,1)S(1)}, u32[]{:S(2)}, u32[]{:S(2)}) collective-permute-start(bf16[192,2304]{1,0:T(8,128)(2,1)} %w_ref.7), channel_id=1, source_target_pairs={{0,8},{1,9},{2,10},{3,11},{4,12},{5,13},{6,14},{7,15},{8,0},{9,1},... | collective-permute-start | bytes 2654216 | tf_op jit(solution)/shard_map/ppermute | solution.py:441
  3.7 8.9 %collective-permute-start = (bf16[128,768]{1,0:T(8,128)(2,1)}, bf16[128,768]{1,0:T(8,128)(2,1)S(1)}, u32[]{:S(2)}, u32[]{:S(2)}) collective-permute-start(bf16[128,768]{1,0:T(8,128)(2,1)} %x_ref.2), channel_id=1, source_target_pairs={{0,4},{1,5},{2,6},{3,7},{4,0},{5,1},{6,2},{7,3},{8,9},{9,8},{10,11... | collective-permute-start | bytes 589832 | tf_op jit(solution)/shard_map/ppermute | solution.py:441
  7.6 18.1 %copy-start.27 = (f32[2,192]{1,0:T(2,128)}, f32[2,192]{1,0:T(2,128)S(1)}, u32[]{:S(2)}) copy-start(f32[2,192]{1,0:T(2,128)S(1)} %maximum_convert_fusion.g0_ref.own_gain) | copy-start | bytes 4612
  7.6 16.0 %collective-permute-start.2 = (f32[2,192]{1,0:T(2,128)S(1)}, f32[2,192]{1,0:T(2,128)S(1)}, u32[]{:S(2)}, u32[]{:S(2)}) collective-permute-start(f32[2,192]{1,0:T(2,128)S(1)} %maximum_convert_fusion.g0_ref.own_gain), channel_id=1, source_target_pairs={{0,16},{1,17},{2,18},{3,19},{4,20},{5,21},{6,22},{7,23},{8,24},{9,... | collective-permute-start | bytes 4616 | tf_op jit(solution)/shard_map/ppermute | solution.py:441
  12.6 11.0 %collective-permute-start.1 = (bf16[256,768]{1,0:T(8,128)(2,1)S(1)}, bf16[256,768]{1,0:T(8,128)(2,1)S(1)}, u32[]{:S(2)}, u32[]{:S(2)}) collective-permute-start(bf16[256,768]{1,0:T(8,128)(2,1)S(1)} %get-tuple-element.158), channel_id=1, source_target_pairs={{0,2},{1,3},{2,0},{3,1},{4,6},{5,7},{6,4},{7,5},{8,12},{9,13},{10,... | collective-permute-start | bytes 1179656 | tf_op jit(solution)/shard_map/ppermute | solution.py:441
  17.3 8.3 %copy-start = (bf16[192,2304]{1,0:T(8,128)(2,1)S(1)}, bf16[192,2304]{1,0:T(8,128)(2,1)}, u32[]{:S(2)}) copy-start(bf16[192,2304]{1,0:T(8,128)(2,1)} %w_ref.9) | copy-start | bytes 2654212
  23.6 7.1 %copy-start.28 = (f32[2,192]{1,0:T(2,128)}, f32[2,192]{1,0:T(2,128)S(1)}, u32[]{:S(2)}) copy-start(f32[2,192]{1,0:T(2,128)S(1)} %collective-permute-done.2.g2_ref) | copy-start | bytes 4612
  23.6 7.0 %collective-permute-start.5 = (bf16[192,2304]{1,0:T(8,128)(2,1)S(1)}, bf16[192,2304]{1,0:T(8,128)(2,1)S(1)}, u32[]{:S(2)}, u32[]{:S(2)}) collective-permute-start(bf16[192,2304]{1,0:T(8,128)(2,1)S(1)} %collective-permute-done.4.w2), channel_id=1, source_target_pairs={{0,8},{1,9},{2,10},{3,11},{4,12},{5,13},{6,14},{7,15},{8,0},{9,1},... | collective-permute-start | bytes 2654216 | tf_op jit(solution)/shard_map/ppermute | solution.py:441
  23.7 17.0 %collective-permute-start.9 = (bf16[384,768]{1,0:T(8,128)(2,1)}, bf16[384,768]{1,0:T(8,128)(2,1)}, u32[]{:S(2)}, u32[]{:S(2)}) collective-permute-start(bf16[384,768]{1,0:T(8,128)(2,1)} %pack_up.1), channel_id=1, source_target_pairs={{0,16},{1,17},{2,18},{3,19},{4,20},{5,21},{6,22},{7,23},{8,24},{9,... | collective-permute-start | bytes 1769480 | tf_op jit(solution)/shard_map/ppermute | solution.py:441
  25.5 19.0 %collective-permute-start.10 = (bf16[192,2304]{1,0:T(8,128)(2,1)S(1)}, bf16[192,2304]{1,0:T(8,128)(2,1)S(1)}, u32[]{:S(2)}, u32[]{:S(2)}) collective-permute-start(bf16[192,2304]{1,0:T(8,128)(2,1)S(1)} %copy-done), channel_id=1, source_target_pairs={{0,8},{1,9},{2,10},{3,11},{4,12},{5,13},{6,14},{7,15},{8,0},{9,1},... | collective-permute-start | bytes 2654216 | tf_op jit(solution)/shard_map/ppermute | solution.py:441
  25.7 2.3 %collective-permute-start.6 = (f32[2,192]{1,0:T(2,128)S(1)}, f32[2,192]{1,0:T(2,128)S(1)}, u32[]{:S(2)}, u32[]{:S(2)}) collective-permute-start(f32[2,192]{1,0:T(2,128)S(1)} %maximum_convert_fusion.g0_ref.own_gain), channel_id=1, source_target_pairs={{0,8},{1,9},{2,10},{3,11},{4,12},{5,13},{6,14},{7,15},{8,0},{9,1},... | collective-permute-start | bytes 4616 | tf_op jit(solution)/shard_map/ppermute | solution.py:441
  28.0 1.2 collective-permute-start.7
  29.1 15.4 %collective-permute-start.8 = (bf16[512,768]{1,0:T(8,128)(2,1)S(1)}, bf16[512,768]{1,0:T(8,128)(2,1)S(1)}, u32[]{:S(2)}, u32[]{:S(2)}) collective-permute-start(bf16[512,768]{1,0:T(8,128)(2,1)S(1)} %constant_dynamic-update-slice_fusion.2.x_ref), channel_id=1, source_target_pairs={{0,1},{1,0},{2,3},{3,2},{4,5},{5,4},{6,7},{7,6},{8,10},{9,11},{10,... | collective-permute-start | bytes 2359304 | tf_op jit(solution)/shard_map/ppermute | solution.py:441
  30.6 11.8 %collective-permute-start.11 = (bf16[192,768]{1,0:T(8,128)(2,1)}, bf16[192,768]{1,0:T(8,128)(2,1)}, u32[]{:S(2)}, u32[]{:S(2)}) collective-permute-start(bf16[192,768]{1,0:T(8,128)(2,1)} %o0.1), channel_id=1, source_target_pairs={{0,8},{1,9},{2,10},{3,11},{4,12},{5,13},{6,14},{7,15},{8,0},{9,1},... | collective-permute-start | bytes 884744 | tf_op jit(solution)/shard_map/ppermute | solution.py:441
  40.7 18.2 %collective-permute-start.13 = (bf16[384,768]{1,0:T(8,128)(2,1)}, bf16[384,768]{1,0:T(8,128)(2,1)S(1)}, u32[]{:S(2)}, u32[]{:S(2)}) collective-permute-start(bf16[384,768]{1,0:T(8,128)(2,1)} %collective-permute-done.9.af), channel_id=1, source_target_pairs={{0,2},{1,3},{2,0},{3,1},{4,6},{5,7},{6,4},{7,5},{8,10},{9,11},{10,... | collective-permute-start | bytes 1769480 | tf_op jit(solution)/shard_map/ppermute | solution.py:441
  42.4 2.0 collective-permute-start.12
  42.4 17.0 %collective-permute-start.16 = (bf16[288,768]{1,0:T(8,128)(2,1)}, bf16[288,768]{1,0:T(8,128)(2,1)S(1)}, u32[]{:S(2)}, u32[]{:S(2)}) collective-permute-start(bf16[288,768]{1,0:T(8,128)(2,1)} %b0.1), channel_id=1, source_target_pairs={{0,16},{1,17},{2,18},{3,19},{4,20},{5,21},{6,22},{7,23},{8,24},{9,... | collective-permute-start | bytes 1327112 | tf_op jit(solution)/shard_map/ppermute | solution.py:441
  44.4 17.3 %copy-start.20 = (bf16[288,768]{1,0:T(8,128)(2,1)}, bf16[288,768]{1,0:T(8,128)(2,1)S(1)}, u32[]{:S(2)}) copy-start(bf16[288,768]{1,0:T(8,128)(2,1)S(1)} %collective-permute-done.12.b1) | copy-start | bytes 1327108
  44.4 15.1 %collective-permute-start.14 = (bf16[384,768]{1,0:T(8,128)(2,1)}, bf16[384,768]{1,0:T(8,128)(2,1)S(1)}, u32[]{:S(2)}, u32[]{:S(2)}) collective-permute-start(bf16[384,768]{1,0:T(8,128)(2,1)} %collective-permute-done.9.af), channel_id=1, source_target_pairs={{0,8},{1,9},{2,10},{3,11},{4,12},{5,13},{6,14},{7,15},{8,0},{9,1},... | collective-permute-start | bytes 1769480 | tf_op jit(solution)/shard_map/ppermute | solution.py:441
  58.9 2.7 %collective-permute-start.15 = (bf16[384,768]{1,0:T(8,128)(2,1)S(1)}, bf16[384,768]{1,0:T(8,128)(2,1)S(1)}, u32[]{:S(2)}, u32[]{:S(2)}) collective-permute-start(bf16[384,768]{1,0:T(8,128)(2,1)S(1)} %collective-permute-done.13.as_), channel_id=1, source_target_pairs={{0,8},{1,9},{2,10},{3,11},{4,12},{5,13},{6,14},{7,15},{8,0},{9,1},... | collective-permute-start | bytes 1769480 | tf_op jit(solution)/shard_map/ppermute | solution.py:441
  59.4 2.3 %collective-permute-start.17 = (bf16[288,768]{1,0:T(8,128)(2,1)S(1)}, bf16[288,768]{1,0:T(8,128)(2,1)S(1)}, u32[]{:S(2)}, u32[]{:S(2)}) collective-permute-start(bf16[288,768]{1,0:T(8,128)(2,1)S(1)} %collective-permute-done.16.b2), channel_id=1, source_target_pairs={{0,8},{1,9},{2,10},{3,11},{4,12},{5,13},{6,14},{7,15},{8,0},{9,1},... | collective-permute-start | bytes 1327112 | tf_op jit(solution)/shard_map/ppermute | solution.py:441
  71.7 31.7 %collective-permute-start.20 = (bf16[5184,128]{1,0:T(8,128)(2,1)}, bf16[5184,128]{1,0:T(8,128)(2,1)S(1)}, u32[]{:S(2)}, u32[]{:S(2)}) collective-permute-start(bf16[5184,128]{1,0:T(8,128)(2,1)} %get-tuple-element.114), channel_id=1, source_target_pairs={{0,16},{1,17},{2,18},{3,19},{4,20},{5,21},{6,22},{7,23},{8,24},{9,... | collective-permute-start | bytes 3981320 | tf_op jit(solution)/shard_map/ppermute | solution.py:441
  82.9 8.3 %copy-start.9 = (bf16[1,144,768]{2,1,0:T(8,128)(2,1)S(1)}, bf16[1,144,768]{2,1,0:T(8,128)(2,1)}, u32[]{:S(2)}) copy-start(bf16[1,144,768]{2,1,0:T(8,128)(2,1)} %get-tuple-element.106.da_ref) | copy-start | bytes 663556
  82.9 10.9 %copy-start.5 = (bf16[4512,128]{1,0:T(8,128)(2,1)S(1)}, bf16[4512,128]{1,0:T(8,128)(2,1)}, u32[]{:S(2)}) copy-start(bf16[4512,128]{1,0:T(8,128)(2,1)} %get-tuple-element.120.core_ref) | copy-start | bytes 3465220
  91.2 12.2 %collective-permute-start.21 = (bf16[4,16,6912]{2,1,0:T(8,128)(2,1)}, bf16[4,16,6912]{2,1,0:T(8,128)(2,1)}, u32[]{:S(2)}, u32[]{:S(2)}) collective-permute-start(bf16[4,16,6912]{2,1,0:T(8,128)(2,1)} %get-tuple-element.118), channel_id=1, source_target_pairs={{0,8},{1,9},{2,10},{3,11},{4,12},{5,13},{6,14},{7,15},{8,0},{9,1},... | collective-permute-start | bytes 2654216 | tf_op jit(solution)/shard_map/ppermute | solution.py:441
  91.3 24.9 %collective-permute-start.19 = (bf16[1,144,768]{2,1,0:T(8,128)(2,1)S(1)}, bf16[1,144,768]{2,1,0:T(8,128)(2,1)S(1)}, u32[]{:S(2)}, u32[]{:S(2)}) collective-permute-start(bf16[1,144,768]{2,1,0:T(8,128)(2,1)S(1)} %copy-done.9), channel_id=1, source_target_pairs={{0,4},{1,5},{2,6},{3,7},{4,0},{5,1},{6,2},{7,3},{8,9},{9,8},{10,11... | collective-permute-start | bytes 663560 | tf_op jit(solution)/shard_map/ppermute | solution.py:441
  93.9 14.9 %collective-permute-start.22 = (bf16[4512,128]{1,0:T(8,128)(2,1)S(1)}, bf16[4512,128]{1,0:T(8,128)(2,1)}, u32[]{:S(2)}, u32[]{:S(2)}) collective-permute-start(bf16[4512,128]{1,0:T(8,128)(2,1)S(1)} %copy-done.5), channel_id=1, source_target_pairs={{0,8},{1,9},{2,10},{3,11},{4,12},{5,13},{6,14},{7,15},{8,0},{9,1},... | collective-permute-start | bytes 3465224 | tf_op jit(solution)/shard_map/ppermute | solution.py:441
  93.9 9.6 %copy-start.8 = (bf16[4,16,6912]{2,1,0:T(8,128)(2,1)S(1)}, bf16[4,16,6912]{2,1,0:T(8,128)(2,1)}, u32[]{:S(2)}) copy-start(bf16[4,16,6912]{2,1,0:T(8,128)(2,1)} %get-tuple-element.117) | copy-start | bytes 2654212
  93.9 13.5 %collective-permute-start.18 = (bf16[4,16,6912]{2,1,0:T(8,128)(2,1)}, bf16[4,16,6912]{2,1,0:T(8,128)(2,1)}, u32[]{:S(2)}, u32[]{:S(2)}) collective-permute-start(bf16[4,16,6912]{2,1,0:T(8,128)(2,1)} %get-tuple-element.111), channel_id=1, source_target_pairs={{0,8},{1,9},{2,10},{3,11},{4,12},{5,13},{6,14},{7,15},{8,0},{9,1},... | collective-permute-start | bytes 2654216 | tf_op jit(solution)/shard_map/ppermute | solution.py:441
  100.3 7.1 %copy-start.7 = (bf16[4,16,6912]{2,1,0:T(8,128)(2,1)S(1)}, bf16[4,16,6912]{2,1,0:T(8,128)(2,1)}, u32[]{:S(2)}) copy-start(bf16[4,16,6912]{2,1,0:T(8,128)(2,1)} %get-tuple-element.110) | copy-start | bytes 2654212
  103.4 5.4 %collective-permute-start.23 = (bf16[5184,128]{1,0:T(8,128)(2,1)S(1)}, bf16[5184,128]{1,0:T(8,128)(2,1)S(1)}, u32[]{:S(2)}, u32[]{:S(2)}) collective-permute-start(bf16[5184,128]{1,0:T(8,128)(2,1)S(1)} %collective-permute-done.20.y_ref), channel_id=1, source_target_pairs={{0,8},{1,9},{2,10},{3,11},{4,12},{5,13},{6,14},{7,15},{8,0},{9,1},... | collective-permute-start | bytes 3981320 | tf_op jit(solution)/shard_map/ppermute | solution.py:441
  106.2 13.4 %collective-permute-start.24 = (bf16[4,16,6912]{2,1,0:T(8,128)(2,1)}, bf16[4,16,6912]{2,1,0:T(8,128)(2,1)}, u32[]{:S(2)}, u32[]{:S(2)}) collective-permute-start(bf16[4,16,6912]{2,1,0:T(8,128)(2,1)} %add_convert_fusion), channel_id=1, source_target_pairs={{0,16},{1,17},{2,18},{3,19},{4,20},{5,21},{6,22},{7,23},{8,10},{9,... | collective-permute-start | bytes 2654216 | tf_op jit(solution)/shard_map/ppermute | solution.py:441
  108.8 7.3 %copy-start.26 = (bf16[2,144,768]{2,1,0:T(8,128)(2,1)S(1)}, bf16[2,144,768]{2,1,0:T(8,128)(2,1)}, u32[]{:S(2)}) copy-start(bf16[2,144,768]{2,1,0:T(8,128)(2,1)} %get-tuple-element.157) | copy-start | bytes 1327108
  115.1 12.5 %copy-start.14 = (bf16[2,16,12672]{2,1,0:T(8,128)(2,1)S(1)}, bf16[2,16,12672]{2,1,0:T(8,128)(2,1)}, u32[]{:S(2)}) copy-start(bf16[2,16,12672]{2,1,0:T(8,128)(2,1)} %get-tuple-element.129) | copy-start | bytes 2433028
  115.1 12.5 %collective-permute-start.25 = (bf16[2,16,12672]{2,1,0:T(8,128)(2,1)}, bf16[2,16,12672]{2,1,0:T(8,128)(2,1)S(1)}, u32[]{:S(2)}, u32[]{:S(2)}) collective-permute-start(bf16[2,16,12672]{2,1,0:T(8,128)(2,1)} %get-tuple-element.121), channel_id=1, source_target_pairs={{0,1},{1,0},{2,3},{3,2},{4,5},{5,4},{6,7},{7,6},{8,10},{9,11},{10,... | collective-permute-start | bytes 2433032 | tf_op jit(solution)/shard_map/ppermute | solution.py:441
  120.7 11.6 %collective-permute-start.26 = (bf16[2,16,6912]{2,1,0:T(8,128)(2,1)S(1)}, bf16[2,16,6912]{2,1,0:T(8,128)(2,1)S(1)}, u32[]{:S(2)}, u32[]{:S(2)}) collective-permute-start(bf16[2,16,6912]{2,1,0:T(8,128)(2,1)S(1)} %add_convert_fusion.3), channel_id=1, source_target_pairs={{0,1},{1,0},{2,3},{3,2},{4,5},{5,4},{6,7},{7,6},{8,24},{9,25},{10,... | collective-permute-start | bytes 1327112 | tf_op jit(solution)/shard_map/ppermute | solution.py:441
  121.4 22.4 %collective-permute-start.28 = (bf16[2,144,768]{2,1,0:T(8,128)(2,1)S(1)}, bf16[2,144,768]{2,1,0:T(8,128)(2,1)S(1)}, u32[]{:S(2)}, u32[]{:S(2)}) collective-permute-start(bf16[2,144,768]{2,1,0:T(8,128)(2,1)S(1)} %get-tuple-element.155), channel_id=1, source_target_pairs={{0,2},{1,3},{2,0},{3,1},{4,6},{5,7},{6,4},{7,5},{8,12},{9,13},{10,... | collective-permute-start | bytes 1327112 | tf_op jit(solution)/shard_map/ppermute | solution.py:441
  127.7 13.4 %collective-permute-start.27 = (bf16[1,16,12672]{2,1,0:T(8,128)(2,1)S(1)}, bf16[1,16,12672]{2,1,0:T(8,128)(2,1)S(1)}, u32[]{:S(2)}, u32[]{:S(2)}) collective-permute-start(bf16[1,16,12672]{2,1,0:T(8,128)(2,1)S(1)} %add_convert_fusion.7), channel_id=1, source_target_pairs={{0,2},{1,3},{2,0},{3,1},{4,6},{5,7},{6,4},{7,5},{8,9},{9,8},{10,11... | collective-permute-start | bytes 1216520 | tf_op jit(solution)/shard_map/ppermute | solution.py:441
  132.4 30.8 %collective-permute-start.30 = (bf16[1,16,6912]{2,1,0:T(8,128)(2,1)S(1)}, bf16[1,16,6912]{2,1,0:T(8,128)(2,1)S(1)}, u32[]{:S(2)}, u32[]{:S(2)}) collective-permute-start(bf16[1,16,6912]{2,1,0:T(8,128)(2,1)S(1)} %add_convert_fusion.11), channel_id=1, source_target_pairs={{0,2},{1,3},{2,0},{3,1},{4,6},{5,7},{6,4},{7,5},{8,9},{9,8},{10,11... | collective-permute-start | bytes 663560 | tf_op jit(solution)/shard_map/ppermute | solution.py:441
  141.1 21.9 %collective-permute-start.29 = (bf16[1,16,12672]{2,1,0:T(8,128)(2,1)S(1)}, bf16[1,16,12672]{2,1,0:T(8,128)(2,1)S(1)}, u32[]{:S(2)}, u32[]{:S(2)}) collective-permute-start(bf16[1,16,12672]{2,1,0:T(8,128)(2,1)S(1)} %add_convert_fusion.5), channel_id=1, source_target_pairs={{0,4},{1,5},{2,6},{3,7},{4,0},{5,1},{6,2},{7,3},{8,12},{9,13},{10,... | collective-permute-start | bytes 1216520 | tf_op jit(solution)/shard_map/ppermute | solution.py:441
  143.9 21.7 %copy-start.1 = (bf16[4,144,768]{2,1,0:T(8,128)(2,1)}, bf16[4,144,768]{2,1,0:T(8,128)(2,1)S(1)}, u32[]{:S(2)}) copy-start(bf16[4,144,768]{2,1,0:T(8,128)(2,1)S(1)} %constant_dynamic-update-slice_fusion.7.near_ref) | copy-start | bytes 2654212
  143.9 21.7 %collective-permute-start.31 = (bf16[4,144,768]{2,1,0:T(8,128)(2,1)S(1)}, bf16[4,144,768]{2,1,0:T(8,128)(2,1)S(1)}, u32[]{:S(2)}, u32[]{:S(2)}) collective-permute-start(bf16[4,144,768]{2,1,0:T(8,128)(2,1)S(1)} %constant_dynamic-update-slice_fusion.7.near_ref), channel_id=1, source_target_pairs={{0,1},{1,0},{2,3},{3,2},{4,5},{5,4},{6,7},{7,6},{8,10},{9,11},{10,... | collective-permute-start | bytes 2654216 | tf_op jit(solution)/shard_map/ppermute | solution.py:441
  163.1 12.4 %collective-permute-start.32 = (bf16[1,16,12672]{2,1,0:T(8,128)(2,1)S(1)}, bf16[1,16,12672]{2,1,0:T(8,128)(2,1)S(1)}, u32[]{:S(2)}, u32[]{:S(2)}) collective-permute-start(bf16[1,16,12672]{2,1,0:T(8,128)(2,1)S(1)} %add_convert_fusion.4), channel_id=1, source_target_pairs={{0,2},{1,3},{2,0},{3,1},{4,6},{5,7},{6,4},{7,5},{8,9},{9,8},{10,11... | collective-permute-start | bytes 1216520 | tf_op jit(solution)/shard_map/ppermute | solution.py:441
  163.2 12.8 %collective-permute-start.33 = (bf16[1,16,6912]{2,1,0:T(8,128)(2,1)S(1)}, bf16[1,16,6912]{2,1,0:T(8,128)(2,1)S(1)}, u32[]{:S(2)}, u32[]{:S(2)}) collective-permute-start(bf16[1,16,6912]{2,1,0:T(8,128)(2,1)S(1)} %add_convert_fusion.9), channel_id=1, source_target_pairs={{0,4},{1,5},{2,6},{3,7},{4,0},{5,1},{6,2},{7,3},{8,12},{9,13},{10,... | collective-permute-start | bytes 663560 | tf_op jit(solution)/shard_map/ppermute | solution.py:441
  175.5 22.4 %collective-permute-start.36 = (bf16[2,16,12672]{2,1,0:T(8,128)(2,1)S(1)}, bf16[2,16,12672]{2,1,0:T(8,128)(2,1)S(1)}, u32[]{:S(2)}, u32[]{:S(2)}) collective-permute-start(bf16[2,16,12672]{2,1,0:T(8,128)(2,1)S(1)} %constant_dynamic-update-slice_fusion.10.part_ref), channel_id=1, source_target_pairs={{0,1},{1,0},{2,3},{3,2},{4,5},{5,4},{6,7},{7,6},{8,10},{9,11},{10,... | collective-permute-start | bytes 2433032 | tf_op jit(solution)/shard_map/ppermute | solution.py:441
  176.1 8.4 %collective-permute-start.34 = (bf16[1,16,6912]{2,1,0:T(8,128)(2,1)S(1)}, bf16[1,16,6912]{2,1,0:T(8,128)(2,1)S(1)}, u32[]{:S(2)}, u32[]{:S(2)}) collective-permute-start(bf16[1,16,6912]{2,1,0:T(8,128)(2,1)S(1)} %add_convert_fusion.8), channel_id=1, source_target_pairs={{0,2},{1,3},{2,0},{3,1},{4,6},{5,7},{6,4},{7,5},{8,9},{9,8},{10,11... | collective-permute-start | bytes 663560 | tf_op jit(solution)/shard_map/ppermute | solution.py:441
  184.6 9.6 %collective-permute-start.35 = (bf16[2,16,6912]{2,1,0:T(8,128)(2,1)S(1)}, bf16[2,16,6912]{2,1,0:T(8,128)(2,1)S(1)}, u32[]{:S(2)}, u32[]{:S(2)}) collective-permute-start(bf16[2,16,6912]{2,1,0:T(8,128)(2,1)S(1)} %constant_dynamic-update-slice_fusion.12.part_ref), channel_id=1, source_target_pairs={{0,1},{1,0},{2,3},{3,2},{4,5},{5,4},{6,7},{7,6},{8,10},{9,11},{10,... | collective-permute-start | bytes 1327112 | tf_op jit(solution)/shard_map/ppermute | solution.py:441
  (20 other events, 55.1 us)

commit v4 on v3

--- a/solution.py
+++ b/solution.py
@@ -34,15 +34,27 @@
 }
 FIRST_WALKS = ((0, 1), (1, 0))
 SECOND_WALKS = (("y", 0, 1), (1, "y", 0))
-VMEM_LIMIT = 58 * 1024 * 1024
+VMEM = {
+    "pack_up": 8,
+    "qkv_near": 26,
+    "qkv_far": 26,
+    "attend": 12,
+    "middle": 26,
+    "middle_grad": 26,
+    "every_query": 16,
+    "attend_back": 20,
+    "qkv_grad": 26,
+    "attend_keys": 20,
+    "tokens_grad": 16,
+    "finish_first": 12,
+    "finish_second": 12,
+}
+VMEM_LONG = 58
+SHORT = 1024
 
 
 def whole(shape):
     return pl.BlockSpec(shape, lambda *_: (0,) * len(shape))
-
-
-def params(limit=VMEM_LIMIT):
-    return pltpu.CompilerParams(vmem_limit_bytes=limit)
 
 
 def cost(micros):
@@ -503,6 +515,11 @@
     ff = frows * n_dp
     seq = own * n_ctx
     groups = width // 128
+
+    def room(name):
+        size = VMEM[name] if seq <= SHORT else VMEM_LONG
+        return pltpu.CompilerParams(vmem_limit_bytes=size * 1024 * 1024)
+
     step, fstep = rows // CHUNKS, frows // CHUNKS
     dp_at = lax.axis_index("dp")
     ctx_at = lax.axis_index("ctx")
@@ -556,7 +573,7 @@
             out_specs=whole((4 * half_rows, width)),
         ),
         out_shape=jax.ShapeDtypeStruct((4 * half_rows, width), BF),
-        compiler_params=params(),
+        compiler_params=room("pack_up"),
         cost_estimate=cost(COSTS["pack_up"]),
         name="pack_up",
     )(svec, after(w_in, cos, sin), w_attn_out)
@@ -590,7 +607,7 @@
             jax.ShapeDtypeStruct((width, 3 * width), BF),
             jax.ShapeDtypeStruct((2, width), F32),
         ],
-        compiler_params=params(),
+        compiler_params=room("qkv_near"),
         cost_estimate=cost(COSTS["qkv_near"]),
         name="qkv_near",
     )(svec, everyone, w_qkv, qkv_c, qkv_y, qkv_cy, gains, gains_c, gains_y, gains_cy, cos, sin)
@@ -607,7 +624,7 @@
         in_specs=[rows_of, pl.BlockSpec((width, 3 * width), lambda i: (0, 0)), whole((2, width)), far_table, far_table],
         out_specs=[rows_of] * 3,
         out_shape=[half_seq] * 3,
-        compiler_params=params(),
+        compiler_params=room("qkv_far"),
         cost_estimate=cost(COSTS["qkv_far"]),
         name="qkv_far",
     )(after(far, up_first, in_c, out_c, down_c), full_qkv, gains_full, cos, sin)
@@ -625,7 +642,7 @@
         in_specs=[own_pair] + [half_pair] * 4,
         out_specs=[turned_pair, lse_pair],
         out_shape=[jax.ShapeDtypeStruct((width, own), F32), jax.ShapeDtypeStruct((groups, 8, own), F32)],
-        compiler_params=params(),
+        compiler_params=room("attend"),
         cost_estimate=cost(COSTS["attend"]),
         name="attend",
     )(queries, *keys, *values)
@@ -660,7 +677,7 @@
             pltpu.VMEM((width, own), BF),
             pltpu.VMEM((ff, own), BF),
         ],
-        compiler_params=params(),
+        compiler_params=room("middle"),
         cost_estimate=cost(COSTS["middle"]),
         name="middle",
     )(
@@ -681,7 +698,7 @@
         ],
         out_specs=[own_pair, pl.BlockSpec((2, seq, 128), lambda g: (0, 0, g))],
         out_shape=[jax.ShapeDtypeStruct((own, width), BF), jax.ShapeDtypeStruct((2, seq, width), BF)],
-        compiler_params=params(),
+        compiler_params=room("attend_back"),
         cost_estimate=cost(COSTS["attend_back"]),
         name="attend_back",
     )(queries, *keys, *values, payload, d_attn_t, attn_t, lse, cos, sin)
@@ -703,7 +720,7 @@
             scratch_shapes=[pltpu.VMEM((width, 3 * width), F32)],
         ),
         out_shape=[jax.ShapeDtypeStruct((CHUNKS, 16, step * 3 * width // 16), BF)] * 4,
-        compiler_params=params(),
+        compiler_params=room("qkv_grad"),
         cost_estimate=cost(COSTS["qkv_grad"]),
         name="qkv_grad",
     )(svec, normed_near, normed_far, d_kv, d_query)
@@ -721,7 +738,7 @@
         ],
         out_specs=rows_of,
         out_shape=jax.ShapeDtypeStruct((seq, width), BF),
-        compiler_params=params(),
+        compiler_params=room("every_query"),
         cost_estimate=cost(COSTS["every_query"]),
         name="every_query",
     )(after(normed_near, second_parts[0]), normed_far, full_qkv, cos, sin)
@@ -740,7 +757,7 @@
             pltpu.VMEM((rows, width), F32),
             pltpu.VMEM((frows, width), F32),
         ],
-        compiler_params=params(),
+        compiler_params=room("middle_grad"),
         cost_estimate=cost(COSTS["middle_grad"]),
         name="middle_grad",
     )(svec, after(share_mine, sent), share_core, come_c, come_y, come_cy)
@@ -765,7 +782,7 @@
         ],
         out_specs=[own_pair, own_pair],
         out_shape=[jax.ShapeDtypeStruct((own, width), BF)] * 2,
-        compiler_params=params(),
+        compiler_params=room("attend_keys"),
         cost_estimate=cost(COSTS["attend_keys"]),
         name="attend_keys",
     )(every_query, keys_near, values_near, gathered, after(gathered_far, late), cos, sin)
@@ -777,7 +794,7 @@
         in_specs=[vm] * 7,
         out_specs=vm,
         out_shape=jax.ShapeDtypeStruct((own, width), F32),
-        compiler_params=params(),
+        compiler_params=room("tokens_grad"),
         cost_estimate=cost(COSTS["tokens_grad"]),
         name="tokens_grad",
     )(after(tokens, late), d_query, d_key, d_value, full_qkv, gains_full, d_mid)
@@ -811,7 +828,7 @@
                 ),
                 out_shape=big + [jax.ShapeDtypeStruct((1, rows), F32)],
                 input_output_aliases={5 + i: i for i in range(len(shapes))} if begin else {},
-                compiler_params=params(),
+                compiler_params=room(name),
                 cost_estimate=cost(COSTS[name]),
                 name=name,
             )(svec, part, weight, gains, *((done[-1], *done[:-1]) if begin else ()))

time: 203 us -> 187 us (0.921)
  Pallas kernels: 86.7 us -> 52.2 us
  starting transfers between devices: 31.5 us -> 49.2 us
  waiting for transfers between devices: 59.9 us -> 77.3 us
  local copies, waits for them, and re-layouts: 11.2 us -> 2.62 us
  other arithmetic: 11.5 us -> 4.8 us
    ppermute x37, starting transfers between devices: 31.5 us -> 49.2 us  [swap(): return lax.ppermute(value, ('dp', 'ctx'), pairs)]
    ppermute x37, waiting for transfers between devices: 59.9 us -> 77.3 us  [swap(): return lax.ppermute(value, ('dp', 'ctx'), pairs)]
    unnamed x67 -> x17, local copies, waits for them, and re-layouts: 9.04 us -> 1.09 us
    convert_element_type x12, other arithmetic: 6.98 us -> 1.26 us  [add_low(): return (left.astype(F32) + right.astype(F32)).astype(BF)]
    pallas_call x1, Pallas kernels: 8.29 us -> 3.58 us  [on_device(): pl.pallas_call(functools.partial(qkv_near_kernel, own=own), grid_spec=plt...]
    pallas_call x4, Pallas kernels: 11.9 us -> 7.2 us  [finish(): pl.pallas_call(functools.partial(finish_kernel, shapes=shapes, mark=mark,...]
    pallas_call x1, Pallas kernels: 8.24 us -> 4.46 us  [on_device(): pl.pallas_call(qkv_grad_kernel, grid_spec=pltpu.PrefetchScalarGridSpec(nu...]
    pallas_call x1, Pallas kernels: 9.14 us -> 5.69 us  [on_device(): pl.pallas_call(middle_kernel, in_specs=[pl.BlockSpec(memory_space=pltpu.S...]
  transfers between devices with their start and end apart: 37 -> 37, of which waited for: 16 -> 17; matrix products, arithmetic and copies ran while one was open for 8% -> 4% of each run, Pallas kernels for 37% -> 24%
where the time goes in v4:
time: 187 us
  waiting for transfers between devices  77.3 us (41%)
  Pallas kernels  52.2 us (28%)
  starting transfers between devices  49.2 us (26%)
  other arithmetic  4.8 us (3%)
  local copies, waits for them, and re-layouts  2.62 us (1%)
    ppermute x37, waiting for transfers between devices, swap(): return lax.ppermute(value, ('dp', 'ctx'), pairs)  77.3 us
    ppermute x37, starting transfers between devices, swap(): return lax.ppermute(value, ('dp', 'ctx'), pairs)  49.2 us
    pallas_call x1, Pallas kernels, on_device(): pl.pallas_call(attend_back_kernel, grid=(groups,), in_specs=[own_pair, ha...  8.46 us
    pallas_call x4, Pallas kernels, finish(): pl.pallas_call(functools.partial(finish_kernel, shapes=shapes, mark=mark,...  7.2 us
    pallas_call x1, Pallas kernels, on_device(): pl.pallas_call(attend_kernel, grid=(groups,), in_specs=[own_pair] + [half...  6.87 us
    pallas_call x1, Pallas kernels, on_device(): pl.pallas_call(middle_kernel, in_specs=[pl.BlockSpec(memory_space=pltpu.S...  5.69 us
    pallas_call x1, Pallas kernels, on_device(): pl.pallas_call(attend_keys_kernel, grid=(groups,), in_specs=[seq_pair, ow...  5.63 us
    pallas_call x1, Pallas kernels, on_device(): pl.pallas_call(qkv_grad_kernel, grid_spec=pltpu.PrefetchScalarGridSpec(nu...  4.46 us
  transfers between devices with their start and end apart: 37, of which 17 were waited for; matrix products, arithmetic and copies ran while one was open for 4% of the time, Pallas kernels for 24%

profile of v4, /device:TPU:0, one launch (start us, length us, event | category | flops | bytes accessed | tf_op | source)
XLA Modules:
  0.0 187.2 jit_solution(14179530994745422338)
XLA Ops:
  0.6 3.0 %collective-permute-start.4 = (bf16[192,2304]{1,0:T(8,128)(2,1)}, bf16[192,2304]{1,0:T(8,128)(2,1)S(1)}, u32[]{:S(2)}, u32[]{:S(2)}) collective-permute-start(bf16[192,2304]{1,0:T(8,128)(2,1)} %w_ref.7), channel_id=1, source_target_pairs={{0,16},{1,17},{2,18},{3,19},{4,20},{5,21},{6,22},{7,23},{8,24},{9,... | collective-permute-start | bytes 2654216 | tf_op jit(solution)/shard_map/ppermute | solution.py:453
  3.7 2.6 %collective-permute-start = (bf16[128,768]{1,0:T(8,128)(2,1)}, bf16[128,768]{1,0:T(8,128)(2,1)S(1)}, u32[]{:S(2)}, u32[]{:S(2)}) collective-permute-start(bf16[128,768]{1,0:T(8,128)(2,1)} %x_ref.2), channel_id=1, source_target_pairs={{0,4},{1,5},{2,6},{3,7},{4,0},{5,1},{6,2},{7,3},{8,9},{9,8},{10,11... | collective-permute-start | bytes 589832 | tf_op jit(solution)/shard_map/ppermute | solution.py:453
  9.9 2.7 %collective-permute-done = bf16[128,768]{1,0:T(8,128)(2,1)S(1)} collective-permute-done((bf16[128,768]{1,0:T(8,128)(2,1)}, bf16[128,768]{1,0:T(8,128)(2,1)S(1)}, u32[]{:S(2)}, u32[]{:S(2)}) %collective-permute-start) | collective-permute-done | bytes 196640 | tf_op jit(solution)/shard_map/ppermute | solution.py:453
  13.5 1.9 %fusion = (f32[1024,32]{1,0:T(8,128)S(1)}, f32[1024,32]{1,0:T(8,128)S(1)}, f32[1024,32]{1,0:T(8,128)S(1)}) fusion(f32[32]{0:T(128)S(1)} %multiply_exponential_fusion, f32[1024]{0:T(1024)S(1)} %convert_bitcast_fusion), kind=kLoop, calls=%fused_computation.16 | loop fusion | flops 65536 | bytes 397440 | tf_op jit(solution)/shard_map/neg | solution.py:565
  16.9 6.6 %collective-permute-done.2.g2_ref = f32[2,192]{1,0:T(2,128)S(1)} collective-permute-done((f32[2,192]{1,0:T(2,128)S(1)}, f32[2,192]{1,0:T(2,128)S(1)}, u32[]{:S(2)}, u32[]{:S(2)}) %collective-permute-start.2) | collective-permute-done | bytes 1568 | tf_op jit(solution)/shard_map/ppermute | solution.py:453
  23.7 1.8 collective-permute-start.9
  26.0 1.9 %collective-permute-done.6.g1_ref = f32[2,192]{1,0:T(2,128)S(1)} collective-permute-done((f32[2,192]{1,0:T(2,128)S(1)}, f32[2,192]{1,0:T(2,128)S(1)}, u32[]{:S(2)}, u32[]{:S(2)}) %collective-permute-start.6) | collective-permute-done | bytes 1568 | tf_op jit(solution)/shard_map/ppermute | solution.py:453
  29.1 1.5 collective-permute-start.8
  30.6 3.6 %qkv_near.1 = (bf16[512,768]{1,0:T(8,128)(2,1)S(1)}, bf16[128,768]{1,0:T(8,128)(2,1)S(1)}, bf16[512,768]{1,0:T(8,128)(2,1)S(1)}, bf16[512,768]{1,0:T(8,128)(2,1)...) custom-call(s32[5]{0:T(128)S(1)} %stack.29.svec, ...), custom_call_target="tpu_custom_call" | custom-call | flops 575000000 | tf_op jit(solution)/shard_map/qkv_near/pallas_call | solution.py:594
  34.2 5.3 %collective-permute-done.9.af = bf16[384,768]{1,0:T(8,128)(2,1)S(1)} collective-permute-done((bf16[384,768]{1,0:T(8,128)(2,1)S(1)}, bf16[384,768]{1,0:T(8,128)(2,1)S(1)}, u32[]{:S(2)}, u32[]{:S(2)}) %collective-permute-start.9) | collective-permute-done | bytes 589856 | tf_op jit(solution)/shard_map/ppermute | solution.py:453
  39.4 1.8 collective-permute-start.13
  41.3 1.6 collective-permute-start.16
  43.2 2.1 %qkv_far.1 = (bf16[512,768]{1,0:T(8,128)(2,1)S(1)}, bf16[512,768]{1,0:T(8,128)(2,1)S(1)}, bf16[512,768]{1,0:T(8,128)(2,1)S(1)}) custom-call(bf16[512,768]{1,0:T(8,128)(2,1)S(1)} %collective-permute-done.8.x_ref, bf16[768,2304]{1,0:T(8,128)(2,1)S(1)} %get-tuple-element.88.w_ref, f32[2,768]{1,0:T(2,128)S(1)} %get-tuple-element.94.gain_ref.gains_ref, ...), custom_call_target="tpu_custom_call" | custom-call | flops 575000000 | tf_op jit(solution)/shard_map/qkv_far/pallas_call | solution.py:621
  45.3 6.9 %attend.1 = (f32[768,128]{1,0:T(8,128)S(1)}, f32[6,8,128]{2,1,0:T(8,128)S(1)}) custom-call(bf16[128,768]{1,0:T(8,128)(2,1)S(1)} %get-tuple-element.85.q_ref, bf16[512,768]{1,0:T(8,128)(2,1)S(1)} %get-tuple-element.86.kn_ref.k_ref, bf16[512,768]{1,0:T(8,128)(2,1)S(1)} %get-tuple-element.95.kf_ref, bf16[512,768]{1,0:T(8,128)(2,1)S(1)} %get-tuple-element.96.vn_ref.v_ref, ...), custom_call_target="tpu_custom_call" | custom-call | flops 575000000 | tf_op jit(solution)/shard_map/attend/pallas_call | solution.py:639
  52.2 2.2 %collective-permute-done.13.as_ = bf16[384,768]{1,0:T(8,128)(2,1)S(1)} collective-permute-done((bf16[384,768]{1,0:T(8,128)(2,1)S(1)}, bf16[384,768]{1,0:T(8,128)(2,1)S(1)}, u32[]{:S(2)}, u32[]{:S(2)}) %collective-permute-start.13) | collective-permute-done | bytes 589856 | tf_op jit(solution)/shard_map/ppermute | solution.py:453
  54.9 2.1 %collective-permute-done.17.b3 = bf16[288,768]{1,0:T(8,128)(2,1)S(1)} collective-permute-done((bf16[288,768]{1,0:T(8,128)(2,1)S(1)}, bf16[288,768]{1,0:T(8,128)(2,1)S(1)}, u32[]{:S(2)}, u32[]{:S(2)}) %collective-permute-start.17) | collective-permute-done | bytes 442400 | tf_op jit(solution)/shard_map/ppermute | solution.py:453
  57.0 5.7 %middle.1 = (bf16[128,768]{1,0:T(8,128)(2,1)}, f32[128,768]{1,0:T(8,128)S(1)}, bf16[1,144,768]{2,1,0:T(8,128)(2,1)S(1)}, bf16[768,128]{1,0:T(8,128)(2,1)S(1)}, b...) custom-call(s32[5]{0:T(128)S(1)} %stack.29.svec, ...), custom_call_target="tpu_custom_call" | custom-call | flops 575000000 | tf_op jit(solution)/shard_map/middle/pallas_call | solution.py:659
  62.7 1.7 collective-permute-start.20
  64.4 8.5 %attend_back.1 = (bf16[128,768]{1,0:T(8,128)(2,1)S(1)}, bf16[2,1024,768]{2,1,0:T(8,128)(2,1)S(1)}) custom-call(bf16[128,768]{1,0:T(8,128)(2,1)S(1)} %get-tuple-element.85.q_ref, bf16[512,768]{1,0:T(8,128)(2,1)S(1)} %get-tuple-element.86.kn_ref.k_ref, bf16[512,768]{1,0:T(8,128)(2,1)S(1)} %get-tuple-element.95.kf_ref, ...), custom_call_target="tpu_custom_call" | custom-call | flops 575000000 | tf_op jit(solution)/shard_map/attend_back/pallas_call | solution.py:691
  72.9 4.5 %qkv_grad.1 = (bf16[4,16,6912]{2,1,0:T(8,128)(2,1)S(1)}, bf16[4,16,6912]{2,1,0:T(8,128)(2,1)S(1)}, bf16[4,16,6912]{2,1,0:T(8,128)(2,1)S(1)}, bf16[4,16,6912]{2,1,0:T(8,128)(2,1)S(1)}) custom-call(s32[5]{0:T(128)S(1)} %stack.29.svec, bf16[512,768]{1,0:T(8,128)(2,1)S(1)} %get-tuple-element.115.near_ref, bf16[512,768]{1,0:T(8,128)(2,1)S(1)} %get-tuple-element.105.far_ref, ...), custom_call_target="tpu_custom_call" | custom-call | flops 575000000 | tf_op jit(solution)/shard_map/qkv_grad/pallas_call | solution.py:708
  77.4 2.7 %collective-permute-start.19 = (bf16[1,144,768]{2,1,0:T(8,128)(2,1)S(1)}, bf16[1,144,768]{2,1,0:T(8,128)(2,1)S(1)}, u32[]{:S(2)}, u32[]{:S(2)}) collective-permute-start(bf16[1,144,768]{2,1,0:T(8,128)(2,1)S(1)} %get-tuple-element.106.da_ref), channel_id=1, source_target_pairs={{0,4},{1,5},{2,6},{3,7},{4,0},{5,1},{6,2},{7,3},{8,9},{9,8},{10,11... | collective-permute-start | bytes 663560 | tf_op jit(solution)/shard_map/ppermute | solution.py:453
  80.6 3.2 %every_query.1.q_ref = bf16[1024,768]{1,0:T(8,128)(2,1)S(1)} custom-call(bf16[512,768]{1,0:T(8,128)(2,1)S(1)} %get-tuple-element.115.near_ref, bf16[512,768]{1,0:T(8,128)(2,1)S(1)} %get-tuple-element.105.far_ref, bf16[768,2304]{1,0:T(8,128)(2,1)S(1)} %get-tuple-element.88.w_ref, f32[1024,128]{1,0:T(8,128)S(1)} %get-tuple-element.165.cos_ref, ...), custom_call_target="tpu_custom_call" | custom-call | flops 575000000 | tf_op jit(solution)/shard_map/every_query/pallas_call | solution.py:729
  83.8 10.1 %collective-permute-done.20.y_ref = bf16[5184,128]{1,0:T(8,128)(2,1)S(1)} collective-permute-done((bf16[5184,128]{1,0:T(8,128)(2,1)S(1)}, bf16[5184,128]{1,0:T(8,128)(2,1)S(1)}, u32[]{:S(2)}, u32[]{:S(2)}) %collective-permute-start.20) | collective-permute-done | bytes 1327136 | tf_op jit(solution)/shard_map/ppermute | solution.py:453
  94.1 1.8 collective-permute-start.24
  97.0 2.2 %middle_grad.1 = (bf16[2,16,12672]{2,1,0:T(8,128)(2,1)S(1)}, bf16[2,16,12672]{2,1,0:T(8,128)(2,1)S(1)}) custom-call(s32[5]{0:T(128)S(1)} %stack.29.svec, bf16[672,128]{1,0:T(8,128)(2,1)S(1)} %get-tuple-element.119.mine_ref, bf16[4512,128]{1,0:T(8,128)(2,1)S(1)} %get-tuple-element.120.core_ref, bf16[4512,128]{1,0:T(8,128)(2,1)S(1)} %collective-permute-done.22.c_ref, ...), custom_call_target="tpu_custom_call" | custom-call | flops 575000000 | tf_op jit(solution)/shard_map/middle_grad/pallas_call | solution.py:748
  99.2 1.7 collective-permute-start.25
  101.0 6.3 %collective-permute-done.24 = bf16[4,16,6912]{2,1,0:T(8,128)(2,1)S(1)} collective-permute-done((bf16[4,16,6912]{2,1,0:T(8,128)(2,1)S(1)}, bf16[4,16,6912]{2,1,0:T(8,128)(2,1)S(1)}, u32[]{:S(2)}, u32[]{:S(2)}) %collective-permute-start.24) | collective-permute-done | bytes 884768 | tf_op jit(solution)/shard_map/ppermute | solution.py:453
  107.4 1.7 collective-permute-start.26
  109.1 1.6 collective-permute-start.28
  111.6 1.8 collective-permute-start.27
  113.4 2.8 %collective-permute-done.26 = bf16[2,16,6912]{2,1,0:T(8,128)(2,1)S(1)} collective-permute-done((bf16[2,16,6912]{2,1,0:T(8,128)(2,1)S(1)}, bf16[2,16,6912]{2,1,0:T(8,128)(2,1)S(1)}, u32[]{:S(2)}, u32[]{:S(2)}) %collective-permute-start.26) | collective-permute-done | bytes 442400 | tf_op jit(solution)/shard_map/ppermute | solution.py:453
  116.3 1.8 collective-permute-start.30
  118.2 11.1 %collective-permute-done.27 = bf16[1,16,12672]{2,1,0:T(8,128)(2,1)S(1)} collective-permute-done((bf16[1,16,12672]{2,1,0:T(8,128)(2,1)S(1)}, bf16[1,16,12672]{2,1,0:T(8,128)(2,1)S(1)}, u32[]{:S(2)}, u32[]{:S(2)}) %collective-permute-start.27) | collective-permute-done | bytes 405536 | tf_op jit(solution)/shard_map/ppermute | solution.py:453
  129.4 2.9 %collective-permute-start.29 = (bf16[1,16,12672]{2,1,0:T(8,128)(2,1)S(1)}, bf16[1,16,12672]{2,1,0:T(8,128)(2,1)S(1)}, u32[]{:S(2)}, u32[]{:S(2)}) collective-permute-start(bf16[1,16,12672]{2,1,0:T(8,128)(2,1)S(1)} %add_convert_fusion.5), channel_id=1, source_target_pairs={{0,4},{1,5},{2,6},{3,7},{4,0},{5,1},{6,2},{7,3},{8,12},{9,13},{10,... | collective-permute-start | bytes 1216520 | tf_op jit(solution)/shard_map/ppermute | solution.py:453
  132.4 1.6 collective-permute-start.31
  134.0 16.2 %collective-permute-done.29 = bf16[1,16,12672]{2,1,0:T(8,128)(2,1)S(1)} collective-permute-done((bf16[1,16,12672]{2,1,0:T(8,128)(2,1)S(1)}, bf16[1,16,12672]{2,1,0:T(8,128)(2,1)S(1)}, u32[]{:S(2)}, u32[]{:S(2)}) %collective-permute-start.29) | collective-permute-done | bytes 405536 | tf_op jit(solution)/shard_map/ppermute | solution.py:453
  150.2 2.1 %collective-permute-start.32 = (bf16[1,16,12672]{2,1,0:T(8,128)(2,1)S(1)}, bf16[1,16,12672]{2,1,0:T(8,128)(2,1)S(1)}, u32[]{:S(2)}, u32[]{:S(2)}) collective-permute-start(bf16[1,16,12672]{2,1,0:T(8,128)(2,1)S(1)} %add_convert_fusion.4), channel_id=1, source_target_pairs={{0,2},{1,3},{2,0},{3,1},{4,6},{5,7},{6,4},{7,5},{8,9},{9,8},{10,11... | collective-permute-start | bytes 1216520 | tf_op jit(solution)/shard_map/ppermute | solution.py:453
  152.4 3.5 %collective-permute-start.33 = (bf16[1,16,6912]{2,1,0:T(8,128)(2,1)S(1)}, bf16[1,16,6912]{2,1,0:T(8,128)(2,1)S(1)}, u32[]{:S(2)}, u32[]{:S(2)}) collective-permute-start(bf16[1,16,6912]{2,1,0:T(8,128)(2,1)S(1)} %add_convert_fusion.9), channel_id=1, source_target_pairs={{0,4},{1,5},{2,6},{3,7},{4,0},{5,1},{6,2},{7,3},{8,12},{9,13},{10,... | collective-permute-start | bytes 663560 | tf_op jit(solution)/shard_map/ppermute | solution.py:453
  155.9 5.6 %attend_keys.1 = (bf16[128,768]{1,0:T(8,128)(2,1)S(1)}, bf16[128,768]{1,0:T(8,128)(2,1)S(1)}) custom-call(bf16[1024,768]{1,0:T(8,128)(2,1)S(1)} %every_query.1.q_ref, bf16[512,768]{1,0:T(8,128)(2,1)S(1)} %get-tuple-element.86.kn_ref.k_ref, bf16[512,768]{1,0:T(8,128)(2,1)S(1)} %get-tuple-element.96.vn_ref.v_ref, ...), custom_call_target="tpu_custom_call" | custom-call | flops 575000000 | tf_op jit(solution)/shard_map/attend_keys/pallas_call | solution.py:774
  161.6 3.7 %collective-permute-start.36 = (bf16[2,16,12672]{2,1,0:T(8,128)(2,1)S(1)}, bf16[2,16,12672]{2,1,0:T(8,128)(2,1)S(1)}, u32[]{:S(2)}, u32[]{:S(2)}) collective-permute-start(bf16[2,16,12672]{2,1,0:T(8,128)(2,1)S(1)} %constant_dynamic-update-slice_fusion.10.part_ref), channel_id=1, source_target_pairs={{0,1},{1,0},{2,3},{3,2},{4,5},{5,4},{6,7},{7,6},{8,10},{9,11},{10,... | collective-permute-start | bytes 2433032 | tf_op jit(solution)/shard_map/ppermute | solution.py:453
  165.4 3.5 %collective-permute-start.34 = (bf16[1,16,6912]{2,1,0:T(8,128)(2,1)S(1)}, bf16[1,16,6912]{2,1,0:T(8,128)(2,1)S(1)}, u32[]{:S(2)}, u32[]{:S(2)}) collective-permute-start(bf16[1,16,6912]{2,1,0:T(8,128)(2,1)S(1)} %add_convert_fusion.8), channel_id=1, source_target_pairs={{0,2},{1,3},{2,0},{3,1},{4,6},{5,7},{6,4},{7,5},{8,9},{9,8},{10,11... | collective-permute-start | bytes 663560 | tf_op jit(solution)/shard_map/ppermute | solution.py:453
  169.0 2.2 %tokens_grad.1 = f32[128,768]{1,0:T(8,128)} custom-call(bf16[128,768]{1,0:T(8,128)(2,1)S(1)} %copy-done.2, bf16[128,768]{1,0:T(8,128)(2,1)S(1)} %get-tuple-element.109.dq_ref, bf16[128,768]{1,0:T(8,128)(2,1)S(1)} %get-tuple-element.135.dk_ref, bf16[128,768]{1,0:T(8,128)(2,1)S(1)} %get-tuple-element.139.dv_ref, ...), custom_call_target="tpu_custom_call" | custom-call | flops 575000000 | tf_op jit(solution)/shard_map/tokens_grad/pallas_call | solution.py:792
  171.2 3.9 %collective-permute-done.34 = bf16[1,16,6912]{2,1,0:T(8,128)(2,1)S(1)} collective-permute-done((bf16[1,16,6912]{2,1,0:T(8,128)(2,1)S(1)}, bf16[1,16,6912]{2,1,0:T(8,128)(2,1)S(1)}, u32[]{:S(2)}, u32[]{:S(2)}) %collective-permute-start.34) | collective-permute-done | bytes 221216 | tf_op jit(solution)/shard_map/ppermute | solution.py:453
  176.5 1.9 %finish_first.2 = (f32[192,2304]{1,0:T(8,128)}, f32[192,768]{1,0:T(8,128)}, f32[288,768]{1,0:T(8,128)}, f32[1,192]{1,0:T(1,128)S(1)}) custom-call(s32[5]{0:T(128)S(1)} %stack.29.svec, bf16[2,16,12672]{2,1,0:T(8,128)(2,1)S(1)} %constant_dynamic-update-slice_fusion.10.part_ref, bf16[192,2304]{1,0:T(8,128)(2,1)S(1)} %copy-done.1, ...), custom_call_target="tpu_custom_call" | custom-call | flops 575000000 | tf_op jit(solution)/shard_map/finish_first/pallas_call | solution.py:816
  178.4 1.7 finish_second.2
  180.1 3.4 %collective-permute-done.35.part_ref = bf16[2,16,6912]{2,1,0:T(8,128)(2,1)S(1)} collective-permute-done((bf16[2,16,6912]{2,1,0:T(8,128)(2,1)S(1)}, bf16[2,16,6912]{2,1,0:T(8,128)(2,1)S(1)}, u32[]{:S(2)}, u32[]{:S(2)}) %collective-permute-start.35) | collective-permute-done | bytes 442400 | tf_op jit(solution)/shard_map/ppermute | solution.py:453
  183.4 1.7 finish_second.3
  185.1 1.9 %finish_first.3 = (f32[192,2304]{1,0:T(8,128)}, f32[192,768]{1,0:T(8,128)}, f32[288,768]{1,0:T(8,128)}, f32[1,192]{1,0:T(1,128)}) custom-call(s32[5]{0:T(128)S(1)} %stack.29.svec, bf16[2,16,12672]{2,1,0:T(8,128)(2,1)S(1)} %collective-permute-done.36.part_ref, ...), custom_call_target="tpu_custom_call", output_to_operand_aliasing={{0}: (5, {}), {1}: (6, {}), {2}: (7, {})} | custom-call | flops 575000000 | tf_op jit(solution)/shard_map/finish_first/pallas_call | solution.py:816
  (85 shorter events, 13.7 us)
Async XLA Ops:
  0.6 23.0 %collective-permute-start.4 = (bf16[192,2304]{1,0:T(8,128)(2,1)}, bf16[192,2304]{1,0:T(8,128)(2,1)S(1)}, u32[]{:S(2)}, u32[]{:S(2)}) collective-permute-start(bf16[192,2304]{1,0:T(8,128)(2,1)} %w_ref.7), channel_id=1, source_target_pairs={{0,16},{1,17},{2,18},{3,19},{4,20},{5,21},{6,22},{7,23},{8,24},{9,... | collective-permute-start | bytes 2654216 | tf_op jit(solution)/shard_map/ppermute | solution.py:453
  3.7 26.9 %collective-permute-start.3 = (bf16[192,2304]{1,0:T(8,128)(2,1)}, bf16[192,2304]{1,0:T(8,128)(2,1)S(1)}, u32[]{:S(2)}, u32[]{:S(2)}) collective-permute-start(bf16[192,2304]{1,0:T(8,128)(2,1)} %w_ref.7), channel_id=1, source_target_pairs={{0,8},{1,9},{2,10},{3,11},{4,12},{5,13},{6,14},{7,15},{8,0},{9,1},... | collective-permute-start | bytes 2654216 | tf_op jit(solution)/shard_map/ppermute | solution.py:453
  3.7 8.9 %collective-permute-start = (bf16[128,768]{1,0:T(8,128)(2,1)}, bf16[128,768]{1,0:T(8,128)(2,1)S(1)}, u32[]{:S(2)}, u32[]{:S(2)}) collective-permute-start(bf16[128,768]{1,0:T(8,128)(2,1)} %x_ref.2), channel_id=1, source_target_pairs={{0,4},{1,5},{2,6},{3,7},{4,0},{5,1},{6,2},{7,3},{8,9},{9,8},{10,11... | collective-permute-start | bytes 589832 | tf_op jit(solution)/shard_map/ppermute | solution.py:453
  7.6 16.0 %collective-permute-start.2 = (f32[2,192]{1,0:T(2,128)S(1)}, f32[2,192]{1,0:T(2,128)S(1)}, u32[]{:S(2)}, u32[]{:S(2)}) collective-permute-start(f32[2,192]{1,0:T(2,128)S(1)} %maximum_convert_fusion.g0_ref.own_gain), channel_id=1, source_target_pairs={{0,16},{1,17},{2,18},{3,19},{4,20},{5,21},{6,22},{7,23},{8,24},{9,... | collective-permute-start | bytes 4616 | tf_op jit(solution)/shard_map/ppermute | solution.py:453
  12.6 11.0 %collective-permute-start.1 = (bf16[256,768]{1,0:T(8,128)(2,1)S(1)}, bf16[256,768]{1,0:T(8,128)(2,1)S(1)}, u32[]{:S(2)}, u32[]{:S(2)}) collective-permute-start(bf16[256,768]{1,0:T(8,128)(2,1)S(1)} %get-tuple-element.158), channel_id=1, source_target_pairs={{0,2},{1,3},{2,0},{3,1},{4,6},{5,7},{6,4},{7,5},{8,12},{9,13},{10,... | collective-permute-start | bytes 1179656 | tf_op jit(solution)/shard_map/ppermute | solution.py:453
  13.5 2.8 %copy-start.1 = (bf16[192,2304]{1,0:T(8,128)(2,1)S(1)}, bf16[192,2304]{1,0:T(8,128)(2,1)}, u32[]{:S(2)}) copy-start(bf16[192,2304]{1,0:T(8,128)(2,1)} %w_ref.9) | copy-start | bytes 2654212
  13.5 2.8 %copy-start.4 = (bf16[192,768]{1,0:T(8,128)(2,1)S(1)}, bf16[192,768]{1,0:T(8,128)(2,1)}, u32[]{:S(2)}) copy-start(bf16[192,768]{1,0:T(8,128)(2,1)} %o0.1) | copy-start | bytes 884740
  16.3 14.3 %copy-start = (bf16[192,2304]{1,0:T(8,128)(2,1)S(1)}, bf16[192,2304]{1,0:T(8,128)(2,1)}, u32[]{:S(2)}) copy-start(bf16[192,2304]{1,0:T(8,128)(2,1)} %w_ref.7) | copy-start | bytes 2654212
  23.6 17.6 %copy-start.3 = (bf16[288,768]{1,0:T(8,128)(2,1)S(1)}, bf16[288,768]{1,0:T(8,128)(2,1)}, u32[]{:S(2)}) copy-start(bf16[288,768]{1,0:T(8,128)(2,1)} %b0.1) | copy-start | bytes 1327108
  23.6 7.0 %collective-permute-start.5 = (bf16[192,2304]{1,0:T(8,128)(2,1)S(1)}, bf16[192,2304]{1,0:T(8,128)(2,1)S(1)}, u32[]{:S(2)}, u32[]{:S(2)}) collective-permute-start(bf16[192,2304]{1,0:T(8,128)(2,1)S(1)} %collective-permute-done.4.w2), channel_id=1, source_target_pairs={{0,8},{1,9},{2,10},{3,11},{4,12},{5,13},{6,14},{7,15},{8,0},{9,1},... | collective-permute-start | bytes 2654216 | tf_op jit(solution)/shard_map/ppermute | solution.py:453
  23.7 15.7 %collective-permute-start.9 = (bf16[384,768]{1,0:T(8,128)(2,1)S(1)}, bf16[384,768]{1,0:T(8,128)(2,1)S(1)}, u32[]{:S(2)}, u32[]{:S(2)}) collective-permute-start(bf16[384,768]{1,0:T(8,128)(2,1)S(1)} %pack_up.1), channel_id=1, source_target_pairs={{0,16},{1,17},{2,18},{3,19},{4,20},{5,21},{6,22},{7,23},{8,24},{9,... | collective-permute-start | bytes 1769480 | tf_op jit(solution)/shard_map/ppermute | solution.py:453
  25.5 17.7 %collective-permute-start.10 = (bf16[192,2304]{1,0:T(8,128)(2,1)S(1)}, bf16[192,2304]{1,0:T(8,128)(2,1)S(1)}, u32[]{:S(2)}, u32[]{:S(2)}) collective-permute-start(bf16[192,2304]{1,0:T(8,128)(2,1)S(1)} %copy-done.1), channel_id=1, source_target_pairs={{0,8},{1,9},{2,10},{3,11},{4,12},{5,13},{6,14},{7,15},{8,0},{9,1},... | collective-permute-start | bytes 2654216 | tf_op jit(solution)/shard_map/ppermute | solution.py:453
  25.7 2.3 %collective-permute-start.6 = (f32[2,192]{1,0:T(2,128)S(1)}, f32[2,192]{1,0:T(2,128)S(1)}, u32[]{:S(2)}, u32[]{:S(2)}) collective-permute-start(f32[2,192]{1,0:T(2,128)S(1)} %maximum_convert_fusion.g0_ref.own_gain), channel_id=1, source_target_pairs={{0,8},{1,9},{2,10},{3,11},{4,12},{5,13},{6,14},{7,15},{8,0},{9,1},... | collective-permute-start | bytes 4616 | tf_op jit(solution)/shard_map/ppermute | solution.py:453
  27.9 1.2 collective-permute-start.7
  29.1 14.1 %collective-permute-start.8 = (bf16[512,768]{1,0:T(8,128)(2,1)S(1)}, bf16[512,768]{1,0:T(8,128)(2,1)S(1)}, u32[]{:S(2)}, u32[]{:S(2)}) collective-permute-start(bf16[512,768]{1,0:T(8,128)(2,1)S(1)} %constant_dynamic-update-slice_fusion.2.x_ref), channel_id=1, source_target_pairs={{0,1},{1,0},{2,3},{3,2},{4,5},{5,4},{6,7},{7,6},{8,10},{9,11},{10,... | collective-permute-start | bytes 2359304 | tf_op jit(solution)/shard_map/ppermute | solution.py:453
  30.6 10.7 %collective-permute-start.11 = (bf16[192,768]{1,0:T(8,128)(2,1)S(1)}, bf16[192,768]{1,0:T(8,128)(2,1)S(1)}, u32[]{:S(2)}, u32[]{:S(2)}) collective-permute-start(bf16[192,768]{1,0:T(8,128)(2,1)S(1)} %copy-done.4), channel_id=1, source_target_pairs={{0,8},{1,9},{2,10},{3,11},{4,12},{5,13},{6,14},{7,15},{8,0},{9,1},... | collective-permute-start | bytes 884744 | tf_op jit(solution)/shard_map/ppermute | solution.py:453
  39.4 14.9 %collective-permute-start.13 = (bf16[384,768]{1,0:T(8,128)(2,1)S(1)}, bf16[384,768]{1,0:T(8,128)(2,1)S(1)}, u32[]{:S(2)}, u32[]{:S(2)}) collective-permute-start(bf16[384,768]{1,0:T(8,128)(2,1)S(1)} %collective-permute-done.9.af), channel_id=1, source_target_pairs={{0,2},{1,3},{2,0},{3,1},{4,6},{5,7},{6,4},{7,5},{8,10},{9,11},{10,... | collective-permute-start | bytes 1769480 | tf_op jit(solution)/shard_map/ppermute | solution.py:453
  41.2 1.8 collective-permute-start.12
  41.3 13.1 %collective-permute-start.16 = (bf16[288,768]{1,0:T(8,128)(2,1)S(1)}, bf16[288,768]{1,0:T(8,128)(2,1)S(1)}, u32[]{:S(2)}, u32[]{:S(2)}) collective-permute-start(bf16[288,768]{1,0:T(8,128)(2,1)S(1)} %copy-done.3), channel_id=1, source_target_pairs={{0,16},{1,17},{2,18},{3,19},{4,20},{5,21},{6,22},{7,23},{8,24},{9,... | collective-permute-start | bytes 1327112 | tf_op jit(solution)/shard_map/ppermute | solution.py:453
  43.0 11.9 %collective-permute-start.14 = (bf16[384,768]{1,0:T(8,128)(2,1)S(1)}, bf16[384,768]{1,0:T(8,128)(2,1)S(1)}, u32[]{:S(2)}, u32[]{:S(2)}) collective-permute-start(bf16[384,768]{1,0:T(8,128)(2,1)S(1)} %collective-permute-done.9.af), channel_id=1, source_target_pairs={{0,8},{1,9},{2,10},{3,11},{4,12},{5,13},{6,14},{7,15},{8,0},{9,1},... | collective-permute-start | bytes 1769480 | tf_op jit(solution)/shard_map/ppermute | solution.py:453
  45.3 11.7 %copy-start.2 = (bf16[128,768]{1,0:T(8,128)(2,1)S(1)}, bf16[128,768]{1,0:T(8,128)(2,1)}, u32[]{:S(2)}) copy-start(bf16[128,768]{1,0:T(8,128)(2,1)} %x_ref.2) | copy-start | bytes 589828
  45.3 11.7 %copy-start.5 = (bf16[128,768]{1,0:T(8,128)(2,1)S(1)}, bf16[128,768]{1,0:T(8,128)(2,1)}, u32[]{:S(2)}) copy-start(bf16[128,768]{1,0:T(8,128)(2,1)} %dy_ref.1) | copy-start | bytes 589828
  54.4 2.6 %collective-permute-start.15 = (bf16[384,768]{1,0:T(8,128)(2,1)S(1)}, bf16[384,768]{1,0:T(8,128)(2,1)S(1)}, u32[]{:S(2)}, u32[]{:S(2)}) collective-permute-start(bf16[384,768]{1,0:T(8,128)(2,1)S(1)} %collective-permute-done.13.as_), channel_id=1, source_target_pairs={{0,8},{1,9},{2,10},{3,11},{4,12},{5,13},{6,14},{7,15},{8,0},{9,1},... | collective-permute-start | bytes 1769480 | tf_op jit(solution)/shard_map/ppermute | solution.py:453
  54.4 2.6 %collective-permute-start.17 = (bf16[288,768]{1,0:T(8,128)(2,1)S(1)}, bf16[288,768]{1,0:T(8,128)(2,1)S(1)}, u32[]{:S(2)}, u32[]{:S(2)}) collective-permute-start(bf16[288,768]{1,0:T(8,128)(2,1)S(1)} %collective-permute-done.16.b2), channel_id=1, source_target_pairs={{0,8},{1,9},{2,10},{3,11},{4,12},{5,13},{6,14},{7,15},{8,0},{9,1},... | collective-permute-start | bytes 1327112 | tf_op jit(solution)/shard_map/ppermute | solution.py:453
  62.7 31.2 %collective-permute-start.20 = (bf16[5184,128]{1,0:T(8,128)(2,1)S(1)}, bf16[5184,128]{1,0:T(8,128)(2,1)S(1)}, u32[]{:S(2)}, u32[]{:S(2)}) collective-permute-start(bf16[5184,128]{1,0:T(8,128)(2,1)S(1)} %get-tuple-element.114), channel_id=1, source_target_pairs={{0,16},{1,17},{2,18},{3,19},{4,20},{5,21},{6,22},{7,23},{8,24},{9,... | collective-permute-start | bytes 3981320 | tf_op jit(solution)/shard_map/ppermute | solution.py:453
  77.4 16.6 %collective-permute-start.21 = (bf16[4,16,6912]{2,1,0:T(8,128)(2,1)S(1)}, bf16[4,16,6912]{2,1,0:T(8,128)(2,1)S(1)}, u32[]{:S(2)}, u32[]{:S(2)}) collective-permute-start(bf16[4,16,6912]{2,1,0:T(8,128)(2,1)S(1)} %get-tuple-element.118), channel_id=1, source_target_pairs={{0,8},{1,9},{2,10},{3,11},{4,12},{5,13},{6,14},{7,15},{8,0},{9,1},... | collective-permute-start | bytes 2654216 | tf_op jit(solution)/shard_map/ppermute | solution.py:453
  77.4 23.5 %collective-permute-start.19 = (bf16[1,144,768]{2,1,0:T(8,128)(2,1)S(1)}, bf16[1,144,768]{2,1,0:T(8,128)(2,1)S(1)}, u32[]{:S(2)}, u32[]{:S(2)}) collective-permute-start(bf16[1,144,768]{2,1,0:T(8,128)(2,1)S(1)} %get-tuple-element.106.da_ref), channel_id=1, source_target_pairs={{0,4},{1,5},{2,6},{3,7},{4,0},{5,1},{6,2},{7,3},{8,9},{9,8},{10,11... | collective-permute-start | bytes 663560 | tf_op jit(solution)/shard_map/ppermute | solution.py:453
  80.1 16.0 %collective-permute-start.22 = (bf16[4512,128]{1,0:T(8,128)(2,1)S(1)}, bf16[4512,128]{1,0:T(8,128)(2,1)S(1)}, u32[]{:S(2)}, u32[]{:S(2)}) collective-permute-start(bf16[4512,128]{1,0:T(8,128)(2,1)S(1)} %get-tuple-element.120.core_ref), channel_id=1, source_target_pairs={{0,8},{1,9},{2,10},{3,11},{4,12},{5,13},{6,14},{7,15},{8,0},{9,1},... | collective-permute-start | bytes 3465224 | tf_op jit(solution)/shard_map/ppermute | solution.py:453
  80.1 15.8 %collective-permute-start.18 = (bf16[4,16,6912]{2,1,0:T(8,128)(2,1)S(1)}, bf16[4,16,6912]{2,1,0:T(8,128)(2,1)S(1)}, u32[]{:S(2)}, u32[]{:S(2)}) collective-permute-start(bf16[4,16,6912]{2,1,0:T(8,128)(2,1)S(1)} %get-tuple-element.111), channel_id=1, source_target_pairs={{0,8},{1,9},{2,10},{3,11},{4,12},{5,13},{6,14},{7,15},{8,0},{9,1},... | collective-permute-start | bytes 2654216 | tf_op jit(solution)/shard_map/ppermute | solution.py:453
  93.9 3.1 %collective-permute-start.23 = (bf16[5184,128]{1,0:T(8,128)(2,1)S(1)}, bf16[5184,128]{1,0:T(8,128)(2,1)S(1)}, u32[]{:S(2)}, u32[]{:S(2)}) collective-permute-start(bf16[5184,128]{1,0:T(8,128)(2,1)S(1)} %collective-permute-done.20.y_ref), channel_id=1, source_target_pairs={{0,8},{1,9},{2,10},{3,11},{4,12},{5,13},{6,14},{7,15},{8,0},{9,1},... | collective-permute-start | bytes 3981320 | tf_op jit(solution)/shard_map/ppermute | solution.py:453
  94.1 13.1 %collective-permute-start.24 = (bf16[4,16,6912]{2,1,0:T(8,128)(2,1)S(1)}, bf16[4,16,6912]{2,1,0:T(8,128)(2,1)S(1)}, u32[]{:S(2)}, u32[]{:S(2)}) collective-permute-start(bf16[4,16,6912]{2,1,0:T(8,128)(2,1)S(1)} %add_convert_fusion), channel_id=1, source_target_pairs={{0,16},{1,17},{2,18},{3,19},{4,20},{5,21},{6,22},{7,23},{8,10},{9,... | collective-permute-start | bytes 2654216 | tf_op jit(solution)/shard_map/ppermute | solution.py:453
  99.2 12.3 %collective-permute-start.25 = (bf16[2,16,12672]{2,1,0:T(8,128)(2,1)S(1)}, bf16[2,16,12672]{2,1,0:T(8,128)(2,1)S(1)}, u32[]{:S(2)}, u32[]{:S(2)}) collective-permute-start(bf16[2,16,12672]{2,1,0:T(8,128)(2,1)S(1)} %get-tuple-element.121), channel_id=1, source_target_pairs={{0,1},{1,0},{2,3},{3,2},{4,5},{5,4},{6,7},{7,6},{8,10},{9,11},{10,... | collective-permute-start | bytes 2433032 | tf_op jit(solution)/shard_map/ppermute | solution.py:453
  107.4 8.9 %collective-permute-start.26 = (bf16[2,16,6912]{2,1,0:T(8,128)(2,1)S(1)}, bf16[2,16,6912]{2,1,0:T(8,128)(2,1)S(1)}, u32[]{:S(2)}, u32[]{:S(2)}) collective-permute-start(bf16[2,16,6912]{2,1,0:T(8,128)(2,1)S(1)} %add_convert_fusion.3), channel_id=1, source_target_pairs={{0,1},{1,0},{2,3},{3,2},{4,5},{5,4},{6,7},{7,6},{8,24},{9,25},{10,... | collective-permute-start | bytes 1327112 | tf_op jit(solution)/shard_map/ppermute | solution.py:453
  109.1 23.3 %collective-permute-start.28 = (bf16[2,144,768]{2,1,0:T(8,128)(2,1)S(1)}, bf16[2,144,768]{2,1,0:T(8,128)(2,1)S(1)}, u32[]{:S(2)}, u32[]{:S(2)}) collective-permute-start(bf16[2,144,768]{2,1,0:T(8,128)(2,1)S(1)} %get-tuple-element.155), channel_id=1, source_target_pairs={{0,2},{1,3},{2,0},{3,1},{4,6},{5,7},{6,4},{7,5},{8,12},{9,13},{10,... | collective-permute-start | bytes 1327112 | tf_op jit(solution)/shard_map/ppermute | solution.py:453
  111.6 17.7 %collective-permute-start.27 = (bf16[1,16,12672]{2,1,0:T(8,128)(2,1)S(1)}, bf16[1,16,12672]{2,1,0:T(8,128)(2,1)S(1)}, u32[]{:S(2)}, u32[]{:S(2)}) collective-permute-start(bf16[1,16,12672]{2,1,0:T(8,128)(2,1)S(1)} %add_convert_fusion.7), channel_id=1, source_target_pairs={{0,2},{1,3},{2,0},{3,1},{4,6},{5,7},{6,4},{7,5},{8,9},{9,8},{10,11... | collective-permute-start | bytes 1216520 | tf_op jit(solution)/shard_map/ppermute | solution.py:453
  116.3 36.0 %collective-permute-start.30 = (bf16[1,16,6912]{2,1,0:T(8,128)(2,1)S(1)}, bf16[1,16,6912]{2,1,0:T(8,128)(2,1)S(1)}, u32[]{:S(2)}, u32[]{:S(2)}) collective-permute-start(bf16[1,16,6912]{2,1,0:T(8,128)(2,1)S(1)} %add_convert_fusion.11), channel_id=1, source_target_pairs={{0,2},{1,3},{2,0},{3,1},{4,6},{5,7},{6,4},{7,5},{8,9},{9,8},{10,11... | collective-permute-start | bytes 663560 | tf_op jit(solution)/shard_map/ppermute | solution.py:453
  129.4 20.8 %collective-permute-start.29 = (bf16[1,16,12672]{2,1,0:T(8,128)(2,1)S(1)}, bf16[1,16,12672]{2,1,0:T(8,128)(2,1)S(1)}, u32[]{:S(2)}, u32[]{:S(2)}) collective-permute-start(bf16[1,16,12672]{2,1,0:T(8,128)(2,1)S(1)} %add_convert_fusion.5), channel_id=1, source_target_pairs={{0,4},{1,5},{2,6},{3,7},{4,0},{5,1},{6,2},{7,3},{8,12},{9,13},{10,... | collective-permute-start | bytes 1216520 | tf_op jit(solution)/shard_map/ppermute | solution.py:453
  132.4 23.5 %collective-permute-start.31 = (bf16[4,144,768]{2,1,0:T(8,128)(2,1)S(1)}, bf16[4,144,768]{2,1,0:T(8,128)(2,1)S(1)}, u32[]{:S(2)}, u32[]{:S(2)}) collective-permute-start(bf16[4,144,768]{2,1,0:T(8,128)(2,1)S(1)} %constant_dynamic-update-slice_fusion.7.near_ref), channel_id=1, source_target_pairs={{0,1},{1,0},{2,3},{3,2},{4,5},{5,4},{6,7},{7,6},{8,10},{9,11},{10,... | collective-permute-start | bytes 2654216 | tf_op jit(solution)/shard_map/ppermute | solution.py:453
  150.2 11.3 %collective-permute-start.32 = (bf16[1,16,12672]{2,1,0:T(8,128)(2,1)S(1)}, bf16[1,16,12672]{2,1,0:T(8,128)(2,1)S(1)}, u32[]{:S(2)}, u32[]{:S(2)}) collective-permute-start(bf16[1,16,12672]{2,1,0:T(8,128)(2,1)S(1)} %add_convert_fusion.4), channel_id=1, source_target_pairs={{0,2},{1,3},{2,0},{3,1},{4,6},{5,7},{6,4},{7,5},{8,9},{9,8},{10,11... | collective-permute-start | bytes 1216520 | tf_op jit(solution)/shard_map/ppermute | solution.py:453
  152.4 13.0 %collective-permute-start.33 = (bf16[1,16,6912]{2,1,0:T(8,128)(2,1)S(1)}, bf16[1,16,6912]{2,1,0:T(8,128)(2,1)S(1)}, u32[]{:S(2)}, u32[]{:S(2)}) collective-permute-start(bf16[1,16,6912]{2,1,0:T(8,128)(2,1)S(1)} %add_convert_fusion.9), channel_id=1, source_target_pairs={{0,4},{1,5},{2,6},{3,7},{4,0},{5,1},{6,2},{7,3},{8,12},{9,13},{10,... | collective-permute-start | bytes 663560 | tf_op jit(solution)/shard_map/ppermute | solution.py:453
  161.6 23.5 %collective-permute-start.36 = (bf16[2,16,12672]{2,1,0:T(8,128)(2,1)S(1)}, bf16[2,16,12672]{2,1,0:T(8,128)(2,1)S(1)}, u32[]{:S(2)}, u32[]{:S(2)}) collective-permute-start(bf16[2,16,12672]{2,1,0:T(8,128)(2,1)S(1)} %constant_dynamic-update-slice_fusion.10.part_ref), channel_id=1, source_target_pairs={{0,1},{1,0},{2,3},{3,2},{4,5},{5,4},{6,7},{7,6},{8,10},{9,11},{10,... | collective-permute-start | bytes 2433032 | tf_op jit(solution)/shard_map/ppermute | solution.py:453
  165.4 9.6 %collective-permute-start.34 = (bf16[1,16,6912]{2,1,0:T(8,128)(2,1)S(1)}, bf16[1,16,6912]{2,1,0:T(8,128)(2,1)S(1)}, u32[]{:S(2)}, u32[]{:S(2)}) collective-permute-start(bf16[1,16,6912]{2,1,0:T(8,128)(2,1)S(1)} %add_convert_fusion.8), channel_id=1, source_target_pairs={{0,2},{1,3},{2,0},{3,1},{4,6},{5,7},{6,4},{7,5},{8,9},{9,8},{10,11... | collective-permute-start | bytes 663560 | tf_op jit(solution)/shard_map/ppermute | solution.py:453
  175.1 8.4 %collective-permute-start.35 = (bf16[2,16,6912]{2,1,0:T(8,128)(2,1)S(1)}, bf16[2,16,6912]{2,1,0:T(8,128)(2,1)S(1)}, u32[]{:S(2)}, u32[]{:S(2)}) collective-permute-start(bf16[2,16,6912]{2,1,0:T(8,128)(2,1)S(1)} %constant_dynamic-update-slice_fusion.12.part_ref), channel_id=1, source_target_pairs={{0,1},{1,0},{2,3},{3,2},{4,5},{5,4},{6,7},{7,6},{8,10},{9,11},{10,... | collective-permute-start | bytes 1327112 | tf_op jit(solution)/shard_map/ppermute | solution.py:453
